TPU v7x, 128 devices: a whole 4x4x4 slice. The times are simulated.
128 devices in a mesh: grp: 8 (over x_lo, z), vocab: 16 (over x_hi, y, core).
Axes of the slice: x: 4 (x_hi: 2, x_lo: 2; x = x_hi * 2 + x_lo), y: 4, z: 4, core: 2. Of those that a mesh axis runs over, the one named last changes fastest.
Arguments:
- teacher_hidden: bfloat16 [512, 4096], P('grp', 'vocab'), may hold values from -120 to 120
- student_hidden: bfloat16 [512, 5120], P('grp', 'vocab'), may hold values from -120 to 120
- teacher_head: bfloat16 [4096, 81920], P(None, ('grp', 'vocab')), may hold values from -0.09375 to 0.09375
- student_head: bfloat16 [5120, 81920], P(None, ('grp', 'vocab')), may hold values from -0.078125 to 0.078125
- lengths: int32 [8], replicated, may hold values from 1 to 128, 512 in all
- sampled: int32 [512], P('grp'), may hold values from 0 to 81919
Outputs:
- head_grad: bfloat16 [5120, 81920], P(None, ('grp', 'vocab'))
- hidden_grad: bfloat16 [512, 5120], P('grp', 'vocab')
- token_kl: float32 [512], P(('grp', 'vocab'))
- sample_ratio: float32 [512], P(('grp', 'vocab'))
Inputs may be any that keep to these rules, and one draw needn't show every extreme that they name: The lengths sum to 512; the longest is exactly 128.
All inputs are finite; a program needn't handle non-finite values.
Results may differ from a plain program's by a relative error of at most 0.0065.
Values may be sent and summed in bfloat16 or wider, within the bound.
No kernel may reach another device: no remote copies, remote signals or barrier semaphores. Data moves between devices by JAX's collectives and lax.ppermute only.
A program may use at most 128 MiB of HBM per device.

v0:
```python
import jax
import jax.numpy as jnp
from jax import lax
from jax.sharding import PartitionSpec as P

LOSS_SCALE = 16


def per_device(teacher_hidden, student_hidden, teacher_head, student_head, lengths, sampled):
    members = lax.axis_size("vocab")
    teacher_rows, student_rows = (
        lax.all_gather(teacher_hidden, "vocab", axis=1, tiled=True),
        lax.all_gather(student_hidden, "vocab", axis=1, tiled=True),
    )
    teacher_all, student_all, ids_all = (
        lax.all_gather(teacher_rows, "grp", axis=0, tiled=True),
        lax.all_gather(student_rows, "grp", axis=0, tiled=True),
        lax.all_gather(sampled, "grp", axis=0, tiled=True),
    )
    total_rows = teacher_all.shape[0]
    columns = teacher_head.shape[1]
    teacher_logits = jnp.dot(teacher_all, teacher_head, preferred_element_type=jnp.float32)
    student_logits = jnp.dot(student_all, student_head, preferred_element_type=jnp.float32)
    top_t = jnp.max(teacher_logits, axis=1)
    top_s = jnp.max(student_logits, axis=1)
    whole_top_t, whole_top_s = lax.pmax((top_t, top_s), ("grp", "vocab"))
    sum_t = jnp.sum(jnp.exp(teacher_logits - whole_top_t[:, None]), axis=1)
    sum_s = jnp.sum(jnp.exp(student_logits - whole_top_s[:, None]), axis=1)
    whole_sum_t, whole_sum_s = lax.psum((sum_t, sum_s), ("grp", "vocab"))
    teacher_logp = teacher_logits - (whole_top_t + jnp.log(whole_sum_t))[:, None]
    student_logp = student_logits - (whole_top_s + jnp.log(whole_sum_s))[:, None]
    teacher_prob = jnp.exp(teacher_logp)
    student_prob = jnp.exp(student_logp)
    log_ratio = teacher_logp - student_logp
    kl_part = jnp.sum(teacher_prob * log_ratio, axis=1)
    first_column = (lax.axis_index("grp") * members + lax.axis_index("vocab")) * columns
    offsets = (ids_all - first_column)[:, None]
    column_ids = jnp.arange(columns, dtype=jnp.int32)[None, :]
    pick_part = jnp.sum(jnp.where(column_ids == offsets, log_ratio, 0.0), axis=1)
    token_kl, sample_ratio = (
        lax.psum_scatter(kl_part, ("grp", "vocab"), scatter_dimension=0, tiled=True),
        lax.psum_scatter(pick_part, ("grp", "vocab"), scatter_dimension=0, tiled=True),
    )
    seq_count = lengths.shape[0]
    ends = jnp.cumsum(lengths)
    starts = ends - lengths
    position = jnp.arange(total_rows, dtype=jnp.int32)[:, None]
    inside = (position >= starts[None, :]) & (position < ends[None, :])
    seq_len = jnp.sum(jnp.where(inside, lengths[None, :], 0), axis=1)
    weight = LOSS_SCALE * total_rows / seq_count / seq_len.astype(jnp.float32)
    logit_grad = (weight[:, None] * (student_prob - teacher_prob)).astype(jnp.bfloat16)
    head_grad = lax.dot_general(
        student_all, logit_grad, (((0,), (0,)), ((), ())), preferred_element_type=jnp.float32
    ).astype(jnp.bfloat16)
    row_part = lax.psum_scatter(
        lax.dot_general(
            logit_grad, student_head, (((1,), (1,)), ((), ())), preferred_element_type=jnp.float32
        ),
        "grp",
        scatter_dimension=0,
        tiled=True,
    )
    hidden_grad = lax.psum_scatter(row_part, "vocab", scatter_dimension=1, tiled=True).astype(
        jnp.bfloat16
    )
    return (head_grad, hidden_grad, token_kl, sample_ratio)


def solution(mesh):
    return jax.shard_map(
        per_device,
        mesh=mesh,
        in_specs=(
            P("grp", "vocab"),
            P("grp", "vocab"),
            P(None, ("grp", "vocab")),
            P(None, ("grp", "vocab")),
            P(),
            P("grp"),
        ),
        out_specs=(
            P(None, ("grp", "vocab")),
            P("grp", "vocab"),
            P(("grp", "vocab")),
            P(("grp", "vocab")),
        ),
        check_vma=False,
    )
```

profile of v0, /device:TPU:1, one launch (start us, length us, event | category | flops | bytes accessed | tf_op | source)
XLA Modules:
  0.0 504.8 jit_solution(9693486708807867967)
XLA Ops:
  7.2 0.0 all-gather.6.cloned.1.call-start
  7.2 28.8 %all_gather.17 = bf16[64,4096]{1,0:T(8,128)(2,1)} all-gather(bf16[64,256]{1,0:T(8,128)(2,1)} %param.6), channel_id=1, replica_groups=mesh['grp'=8,'vocab'=16] {'vocab'}, dimensions={1}, use_global_device_ids=true | all-gather | bytes 557056 | tf_op jit(solution)/shard_map/all_gather | solution.py:12
  36.0 0.0 all-gather.6.cloned.1.call-update
  36.1 0.0 all-gather.4.cloned.1.call-start
  36.1 23.7 %all-gather = bf16[16,320,64]{1,2,0:T(8,128)(2,1)S(1)} all-gather(bf16[1,320,64]{1,2,0:T(8,128)(2,1)} %bitcast.25), channel_id=1, replica_groups=mesh['grp'=8,'vocab'=16] {'vocab'}, dimensions={0}, use_global_device_ids=true | all-gather | bytes 696320 | tf_op jit(solution)/shard_map/all_gather | solution.py:13
  59.8 0.5 copy.15
  60.3 1.5 reshape.48
  61.9 0.0 reduce-scatter.5.cloned.1.call-start
  61.9 0.6 dynamic-slice
  63.2 0.2 reduce-window.8
  63.4 0.2 dynamic-update-slice
  63.6 10.4 %all-reduce = s32[512]{0:T(512)S(1)} all-reduce(s32[512]{0:T(512)S(1)} %dynamic-update-slice), channel_id=1, replica_groups=mesh['grp'=8,'vocab'=16] {'grp'}, use_global_device_ids=true, to_apply=%add | all-reduce | flops 512 | bytes 4096
  73.9 0.1 select_reduce_fusion.1
  74.0 14.6 %all-gather.6.cloned.1.call-done = bf16[512,4096]{1,0:T(8,128)(2,1)} async-done(((bf16[64,4096]{1,0:T(8,128)(2,1)}), bf16[512,4096]{1,0:T(8,128)(2,1)}) %all-gather.6.cloned.1.call-update) | async-done | bytes 4194320 | tf_op jit(solution)/shard_map/all_gather | solution.py:16
  88.6 6.9 %fusion.2 = (f32[512]{0:T(512)S(1)}, f32[512,640]{1,0:T(8,128)S(1)}) fusion(bf16[512,4096]{1,0:T(8,128)(2,1)} %all-gather.6.cloned.1.call-done, bf16[4096,640]{1,0:T(8,128)(2,1)} %param.8), kind=kOutput, calls=%fused_computation.18 | convolution fusion | flops 2684681728 | bytes 10749952 | tf_op jit(solution)/shard_map/dot_general | solution.py:22
  95.5 56.3 %all-gather.4.cloned.1.call-done = bf16[512,5120]{1,0:T(8,128)(2,1)} async-done(((bf16[64,5120]{1,0:T(8,128)(2,1)}), bf16[512,5120]{1,0:T(8,128)(2,1)}) %all-gather.4.cloned.1.call-update) | async-done | bytes 5242896 | tf_op jit(solution)/shard_map/all_gather | solution.py:17
  151.8 8.2 %fusion.3 = (f32[512]{0:T(512)S(1)}, f32[512,640]{1,0:T(8,128)S(1)}) fusion(bf16[512,5120]{1,0:T(8,128)(2,1)} %all-gather.4.cloned.1.call-done, bf16[5120,640]{1,0:T(8,128)(2,1)} %param.9), kind=kOutput, calls=%fused_computation.19 | convolution fusion | flops 3355770368 | bytes 13109248 | tf_op jit(solution)/shard_map/dot_general | solution.py:23
  160.0 64.3 %all-reduce.5 = (f32[512]{0:T(512)S(1)}, f32[512]{0:T(512)S(1)}) all-reduce(f32[512]{0:T(512)S(1)} %get-tuple-element.29, f32[512]{0:T(512)S(1)} %get-tuple-element.31), channel_id=1, replica_groups=mesh['grp'=8,'vocab'=16] {'grp','vocab'}, use_global_device_ids=true, to_apply=%region_7.0 | all-reduce | flops 1024 | bytes 8192 | tf_op jit(solution)/shard_map/pmax | solution.py:26
  224.3 0.8 exponential_reduce_fusion
  225.1 63.8 %all-reduce.4 = (f32[512]{0:T(512)S(1)}, f32[512]{0:T(512)S(1)}) all-reduce(f32[512]{0:T(512)S(1)} %get-tuple-element.33, f32[512]{0:T(512)S(1)} %get-tuple-element.34), channel_id=1, replica_groups=mesh['grp'=8,'vocab'=16] {'grp','vocab'}, use_global_device_ids=true, to_apply=%region_9.10 | all-reduce | flops 1024 | bytes 8192 | tf_op jit(solution)/shard_map/psum | solution.py:29
  289.0 1.0 select_reduce_fusion
  290.0 9.7 %fusion.4 = f32[512,5120]{1,0:T(8,128)} fusion(bf16[512,640]{1,0:T(8,128)(2,1)S(1)} %get-tuple-element.28, bf16[5120,640]{1,0:T(8,128)(2,1)} %param.9), kind=kOutput, calls=%fused_computation.20 | convolution fusion | flops 3355443200 | bytes 17694720 | tf_op jit(solution)/shard_map/dot_general | solution.py:56
  299.7 0.2 reduce-scatter.7.cloned.1.call-start
  299.9 108.9 %reduce-scatter.5.cloned.1.call-done = f32[64,5120]{1,0:T(8,128)} async-done(((f32[512,5120]{1,0:T(8,128)}), f32[64,5120]{1,0:T(8,128)}) %reduce-scatter.5.cloned.1.call-update) | async-done | bytes 1310736 | tf_op jit(solution)/shard_map/reduce_scatter | solution.py:55
  408.9 3.1 copy.17
  411.9 0.0 reduce-scatter.7.cloned.1.call-update
  412.0 65.2 %all-reduce.3 = (f32[512]{0:T(512)S(1)}, f32[512]{0:T(512)S(1)}) all-reduce(f32[512]{0:T(512)S(1)} %get-tuple-element.21, f32[512]{0:T(512)S(1)} %get-tuple-element.20), channel_id=4, replica_groups=mesh['grp'=8,'vocab'=16] {'grp','vocab'}, use_global_device_ids=true, to_apply=%region_13.14.clone | all-reduce | flops 1024 | bytes 8192
  477.1 0.6 dynamic-slice.1
  477.7 0.6 dynamic-slice.2
  478.3 8.9 %fusion = bf16[5120,640]{0,1:T(8,128)(2,1)} fusion(bf16[512,640]{1,0:T(8,128)(2,1)S(1)} %get-tuple-element.28, bf16[512,5120]{1,0:T(8,128)(2,1)} %all-gather.4.cloned.1.call-done), kind=kOutput, calls=%fused_computation.1 | convolution fusion | flops 3358720000 | bytes 12451840 | tf_op jit(solution)/shard_map/dot_general | solution.py:52
  487.2 9.5 %copy.16 = bf16[5120,640]{1,0:T(8,128)(2,1)} copy(bf16[5120,640]{0,1:T(8,128)(2,1)} %fusion) | data formatting | bytes 13107200
  496.6 1.6 copy.18
  (15 shorter events, 0.1 us)
Async XLA Ops:
  7.2 81.4 %all-gather.6.cloned.1.call-start = ((), (), s32[]{:S(2)}) async-start(), calls=%async_computation.3 | async-start | bytes 4718592 | tf_op jit(solution)/shard_map/all_gather | solution.py:16
  36.1 115.7 %all-gather.4.cloned.1.call-start = ((), (), s32[]{:S(2)}) async-start(), calls=%async_computation.2 | async-start | bytes 5898240 | tf_op jit(solution)/shard_map/all_gather | solution.py:17
  60.3 1.6 copy-start.2
  60.3 2.9 copy-start
  60.3 3.0 copy-start.1
  61.9 347.0 %reduce-scatter.5.cloned.1.call-start = ((), (), s32[]{:S(2)}) async-start(), calls=%async_computation.4 | async-start | bytes 11796480 | tf_op jit(solution)/shard_map/reduce_scatter | solution.py:55
  299.7 196.9 %reduce-scatter.7.cloned.1.call-start = ((), (), s32[]{:S(2)}) async-start(), calls=%async_computation.5 | async-start | bytes 2785280
Sparse Core Ops, SparseCore 0:
  36.2 52.3 all-gather.5
  90.8 60.8 all-gather.3
  299.8 108.9 reduce-scatter.4
  412.7 70.8 reduce-scatter.6
where the time goes:
time: 505 us
  blocking collectives  256 us (51%)
  waiting for transfers between devices  180 us (36%)
  matrix products  33.7 us (7%)
  local copies, waits for them, and re-layouts  18.1 us (4%)
  between operations  14.5 us (3%)
    reduce_scatter x1, waiting for transfers between devices, per_device(): lax.psum_scatter(lax.dot_general(logit_grad, student_head, (((1,), (1,)),...  109 us
    unnamed x2, blocking collectives  75.5 us
    pmax x1, blocking collectives, per_device(): whole_top_t, whole_top_s = lax.pmax((top_t, top_s), ('grp', 'vocab'))  64.3 us
    psum x1, blocking collectives, per_device(): whole_sum_t, whole_sum_s = lax.psum((sum_t, sum_s), ('grp', 'vocab'))  63.8 us
    all_gather x1, waiting for transfers between devices, per_device(): lax.all_gather(student_rows, 'grp', axis=0, tiled=True)  56.3 us
    all_gather x1, blocking collectives, per_device(): lax.all_gather(teacher_hidden, 'vocab', axis=1, tiled=True)  28.8 us
    all_gather x1, blocking collectives, per_device(): lax.all_gather(student_hidden, 'vocab', axis=1, tiled=True)  23.7 us
    unnamed x15, local copies, waits for them, and re-layouts  17.6 us
  transfers between devices with their start and end apart: 4, of which 3 were waited for; matrix products, arithmetic and copies ran while one was open for 6% of the time, Pallas kernels for 0%

commit v1 on v0

v1 whole, which is shorter than its diff:
```python
import functools
import itertools

import jax
import jax.numpy as jnp
import numpy as np
from jax import lax
from jax.experimental import pallas as pl
from jax.experimental.pallas import tpu as pltpu
from jax.sharding import PartitionSpec as P

LOSS_SCALE = 16
BOTH = ("grp", "vocab")
F32, BF16 = jnp.float32, jnp.bfloat16
HALF = 32
LANES = 128
ID_ROWS = 16
PIECES = 2
LIMIT = 56
DEPTH = 4
CORNER_OF = (0, 4, 2, 1, 3, 5, 6, 7)


def device(x, y, z, core):
    return ((x % 2) * 4 + z) * 16 + ((x // 2) * 4 + y) * 2 + core


def cubes(core, step, rank):
    seen, groups = set(), []
    for where in itertools.product(range(4), repeat=3):
        if where in seen:
            continue
        pairs = [sorted((p, p ^ step), key=rank) for p in where]
        members = list(itertools.product(*pairs))
        seen.update(members)
        groups.append([device(*m, core) for m in members])
    return groups


def low(p):
    return p & 1


def high(p):
    return p >> 1


def parity(p):
    return (p & 1) ^ (p >> 1)


FIRST = cubes(0, 1, low) + cubes(1, 3, high)
SAME_CORE = [[2 * chip + core for chip in range(64)] for core in (0, 1)]
SWAP = [(i, i ^ 1) for i in range(128)]


def chips():
    return itertools.product(range(4), repeat=3)


def number(rank, place):
    return rank(place[0]) * 4 + rank(place[1]) * 2 + rank(place[2])


def positions():
    table = np.zeros((2, 64), np.int32)
    for place in chips():
        chip = device(*place, 0) // 2
        table[0, chip] = number(high, place) * 8 + number(low, place)
        table[1, chip] = number(parity, place) * 8 + number(high, place)
    return table


def corners():
    table = np.zeros(128, np.int32)
    for place in chips():
        table[device(*place, 0)] = number(high, place)
        table[device(*place, 1)] = number(parity, place)
    return table


def links(axes):
    pairs = []
    for place in chips():
        for core in (0, 1):
            other = list(place)
            for axis in axes:
                other[axis] ^= (3, 1)[core]
            pairs.append((device(*place, core), device(*other, core)))
    return pairs


POSITIONS = positions()
CORNERS = corners()


def swap(value):
    return lax.ppermute(value, BOTH, SWAP)


def to_all(block, groups):
    size = len(groups[0])
    return lax.all_to_all(
        jnp.broadcast_to(block, (size,) + block.shape), BOTH, 0, 0, axis_index_groups=groups
    )


def second_gather(near):
    def along(value, *axes):
        return lax.ppermute(value, BOTH, links(axes))

    one = [along(near, axis) for axis in range(3)]
    far = along(near, 0, 1, 2)
    two = [along(one[(axis + 2) % 3], (axis + 1) % 3) for axis in range(3)]
    return [near, *one, *two, far]


def rows_of(table_ref, blocks_ref, chunk, at, strips):
    parts = [blocks_ref[table_ref[group * 8 + chunk], at : at + strips * HALF] for group in range(8)]
    return jnp.concatenate(
        [
            jnp.concatenate([p[s * HALF : (s + 1) * HALF] for p in parts], axis=0)
            for s in range(strips)
        ],
        axis=1,
    )


class Stream:
    def __init__(self, sems):
        self.sems = sems
        self.copies = []
        self.started = 0

    def add(self, source, target):
        self.copies.append(pltpu.make_async_copy(source, target, self.sems.at[len(self.copies)]))
        return len(self.copies) - 1

    def start(self, count):
        for copy in self.copies[self.started : count]:
            copy.start()
        self.started = max(self.started, min(count, len(self.copies)))

    def wait(self, i):
        self.copies[i].wait()
        self.start(i + 1 + DEPTH)


def put_beside(pairs_and_buffers, sems):
    copies = []
    for pair, buffer in pairs_and_buffers:
        rows, columns = pair[0].shape
        size = rows // 4
        for i in range(4):
            for j, ref in enumerate(pair):
                at = pl.ds(i * size, size)
                copies.append(
                    pltpu.make_async_copy(
                        ref.at[at], buffer.at[at, pl.ds(j * columns, columns)], sems.at[len(copies)]
                    )
                )
                copies[-1].start()
    for copy in copies:
        copy.wait()


def prefetch_kernel(own_t, other_t, own_s, other_s, first, second, third, heads_t, heads_s, sems):
    put_beside([((own_t, other_t), heads_t), ((own_s, other_s), heads_s)], sems)


def logits_kernel(
    table_ref, place_ref, *refs
):
    units, (heads_t, heads_s, teacher, student, stats_out, lhs_out) = refs[:8], refs[8:14]
    blocks_ref, lhs_t, lhs_s, powers, stats, work, sems, out_sems = refs[14:]
    arriving = []
    for n, unit in enumerate(units):
        start = (place_ref[2] ^ CORNER_OF[n]) * 8
        arriving.append(pltpu.make_async_copy(unit, blocks_ref.at[pl.ds(start, 8)], sems.at[n]))
        arriving[-1].start()
    columns = heads_t.shape[1] // 2
    lane = lax.broadcasted_iota(jnp.int32, (HALF, LANES), 1)
    column = lax.broadcasted_iota(jnp.int32, (HALF, columns), 1)
    column = jnp.concatenate([column + place_ref[0], column + place_ref[1]], axis=1)
    at_s = 4 * HALF + ID_ROWS

    def columns_of(values, first):
        row = jnp.zeros((HALF, LANES), F32)
        for j, value in enumerate(values):
            row = jnp.where(lane == first + j, value, row)
        return row

    for copy in arriving:
        copy.wait()
    for chunk in range(8):
        lhs_t[:, chunk * 4 * LANES : (chunk + 1) * 4 * LANES] = rows_of(table_ref, blocks_ref, chunk, 0, 4)
    teacher[...] = jnp.dot(lhs_t[...], heads_t[...], preferred_element_type=F32)
    for chunk in range(8):
        lhs_s[:, chunk * 5 * LANES : (chunk + 1) * 5 * LANES] = rows_of(table_ref, blocks_ref, chunk, at_s, 5)
    leaving = [pltpu.make_async_copy(lhs_s, lhs_out, out_sems.at[0])]
    leaving[0].start()
    digits = [blocks_ref[table_ref[group * 8], 4 * HALF : at_s].astype(F32) for group in range(8)]
    ids = jnp.concatenate([d[0:1] * 4096.0 + d[1:2] * 64.0 + d[2:3] for d in digits], axis=0)
    ids = jnp.concatenate([ids, jnp.zeros((LANES - 8, LANES), F32)], axis=0).T.astype(jnp.int32)
    for group in range(8):
        rows = pl.ds(group * HALF, HALF)
        t = teacher[rows, :]
        top = jnp.max(t, axis=1, keepdims=True)
        t = t - top
        e = jnp.exp(t)
        powers[rows, :] = e
        work[rows, :] = columns_of(
            (top, jnp.sum(e, axis=1, keepdims=True), jnp.sum(e * t, axis=1, keepdims=True)), 0
        )
    student[...] = jnp.dot(lhs_s[...], heads_s[...], preferred_element_type=F32)
    for group in range(8):
        rows = pl.ds(group * HALF, HALF)
        s = student[rows, :]
        hit = column == ids[:HALF, group : group + 1]
        picked = jnp.sum(jnp.where(hit, teacher[rows, :] - s, 0.0), axis=1, keepdims=True)
        top = jnp.max(s, axis=1, keepdims=True)
        s = s - top
        total = jnp.sum(jnp.exp(s), axis=1, keepdims=True)
        term = jnp.sum(powers[rows, :] * s, axis=1, keepdims=True)
        work[rows, :] += columns_of((top, total, term, picked), 3)
    stats[...] = jnp.broadcast_to(work[...].T[:8, :], stats.shape)
    leaving.append(pltpu.make_async_copy(stats, stats_out, out_sems.at[1]))
    leaving[1].start()
    for copy in leaving:
        copy.wait()


def gradient_kernel(
    stats_ref, weight_ref, teacher, student, own_s, other_s, part_out, grads_out, kl_ref,
    heads, part, grads, work, sems, out_sems,
):
    stream = Stream(sems)
    size, columns = own_s.shape[0] // 4, own_s.shape[1]
    for i in range(4):
        at = pl.ds(i * size, size)
        for j, ref in enumerate((own_s, other_s)):
            stream.add(ref.at[at], heads.at[at, pl.ds(j * columns, columns)])
    stream.start(DEPTH)
    top_t, sum_t, term_t, top_s, sum_s, term_s, picked = (stats_ref[:, j, :] for j in range(7))
    whole_t = jnp.max(top_t, axis=0, keepdims=True)
    whole_s = jnp.max(top_s, axis=0, keepdims=True)
    scale_t = jnp.exp(top_t - whole_t)
    total_t = jnp.sum(scale_t * sum_t, axis=0, keepdims=True)
    total_s = jnp.sum(jnp.exp(top_s - whole_s) * sum_s, axis=0, keepdims=True)
    log_t, log_s = jnp.log(total_t), jnp.log(total_s)
    shift = (top_t - whole_t) - (top_s - whole_s)
    kl = jnp.sum(scale_t * (term_t - term_s + sum_t * shift), axis=0, keepdims=True) / total_t - (log_t - log_s)
    lse_t, lse_s = whole_t + log_t, whole_s + log_s
    ratio = jnp.sum(picked, axis=0, keepdims=True) - (lse_t - lse_s)
    tokens = kl.shape[1]
    kl_ref[...] = jnp.concatenate([kl, ratio, jnp.zeros((6, tokens), F32)], axis=0)
    rows = jnp.concatenate([lse_t, lse_s, weight_ref[...], jnp.zeros((LANES - 3, tokens), F32)], axis=0)
    work[...] = rows.T

    for i in range(tokens // HALF):
        at = pl.ds(i * HALF, HALF)
        at_t, at_s, weight = (work[at, j : j + 1] for j in range(3))
        grad = weight * (jnp.exp(student[at, :] - at_s) - jnp.exp(teacher[at, :] - at_t))
        grads[at, :] = grad.astype(BF16)
    leaving = [pltpu.make_async_copy(grads, grads_out, out_sems.at[4])]
    leaving[0].start()
    width = part.shape[3]
    chunks = size // width
    for i in range(4):
        stream.wait(2 * i)
        stream.wait(2 * i + 1)
        product = lax.dot_general(
            grads[...], heads[i * size : (i + 1) * size, :], (((1,), (1,)), ((), ())), preferred_element_type=F32
        ).astype(BF16)
        for group in range(8):
            for j in range(chunks):
                part[group, chunks * i + j] = product[
                    group * HALF : (group + 1) * HALF, j * width : (j + 1) * width
                ]
        at = pl.ds(chunks * i, chunks)
        leaving.append(pltpu.make_async_copy(part.at[:, at], part_out.at[:, at], out_sems.at[i]))
        leaving[-1].start()
    for copy in leaving:
        copy.wait()


def head_kernel(own_ref, other_ref, mine_ref, got_ref, out_ref):
    rows = jnp.concatenate([own_ref[...], other_ref[...]], axis=0)
    grad = jnp.concatenate([mine_ref[...], got_ref[...]], axis=0)
    out_ref[...] = lax.dot_general(
        rows, grad, (((0,), (0,)), ((), ())), preferred_element_type=F32
    ).astype(BF16)


SMEM = pl.BlockSpec(memory_space=pltpu.SMEM)
VMEM = pl.BlockSpec(memory_space=pltpu.VMEM)
HBM = pl.BlockSpec(memory_space=pltpu.HBM)


def in_hbm(value):
    return pltpu.with_memory_space_constraint(value, pltpu.HBM)


def params(limit):
    return pltpu.CompilerParams(vmem_limit_bytes=limit << 20)


def cost(flops, size):
    return pl.CostEstimate(flops=flops, bytes_accessed=size, transcendentals=0)


def in_vmem(value):
    return pltpu.with_memory_space_constraint(value, pltpu.VMEM)


def prefetch(own_t, other_t, own_s, other_s, after):
    (wide_t, columns), wide_s = own_t.shape, own_s.shape[0]
    return pl.pallas_call(
        prefetch_kernel,
        name="prefetch_heads",
        in_specs=[HBM] * (4 + len(after)),
        out_specs=[VMEM] * 2,
        out_shape=[pltpu.VMEM((wide_t, 2 * columns), BF16), pltpu.VMEM((wide_s, 2 * columns), BF16)],
        scratch_shapes=[pltpu.SemaphoreType.DMA((16,))],
        compiler_params=params(2),
        cost_estimate=cost(0, 8 * (wide_t + wide_s) * columns),
    )(*map(in_hbm, (own_t, other_t, own_s, other_s, *after)))


def logits_of(table, place, units, heads_t, heads_s):
    tokens = 8 * HALF
    (wide_t, columns), wide_s = heads_t.shape, heads_s.shape[0]
    logits = pltpu.VMEM((tokens, columns), F32)
    return pl.pallas_call(
        logits_kernel,
        name="logits",
        in_specs=[SMEM, SMEM] + [HBM] * 8 + [VMEM] * 2,
        out_specs=[VMEM, VMEM, HBM, HBM],
        out_shape=[
            logits,
            logits,
            pltpu.HBM((64, 8, tokens), F32),
            pltpu.HBM((tokens, wide_s), BF16),
        ],
        scratch_shapes=[
            pltpu.VMEM((64, *units[0].shape[1:]), BF16),
            pltpu.VMEM((tokens, wide_t), BF16),
            pltpu.VMEM((tokens, wide_s), BF16),
            pltpu.VMEM((tokens, columns), F32),
            pltpu.VMEM((64, 8, tokens), F32),
            pltpu.VMEM((tokens, LANES), F32),
            pltpu.SemaphoreType.DMA((8,)),
            pltpu.SemaphoreType.DMA((2,)),
        ],
        compiler_params=params(24),
        cost_estimate=cost(2 * tokens * (wide_t + wide_s) * columns, 8 << 20),
    )(table, place, *map(in_hbm, units), *map(in_vmem, (heads_t, heads_s)))


def gradient_of(stats, weight, teacher, student, own_s, other_s):
    tokens, columns = teacher.shape
    wide = own_s.shape[0]
    return pl.pallas_call(
        gradient_kernel,
        name="hidden_gradient",
        in_specs=[VMEM] * 4 + [HBM] * 2,
        out_specs=[HBM, HBM, VMEM],
        out_shape=[
            pltpu.HBM((8, 8, HALF, wide // 8), BF16),
            pltpu.HBM((tokens, columns), BF16),
            jax.ShapeDtypeStruct((8, tokens), F32),
        ],
        scratch_shapes=[
            pltpu.VMEM((wide, columns), BF16),
            pltpu.VMEM((8, 8, HALF, wide // 8), BF16),
            pltpu.VMEM((tokens, columns), BF16),
            pltpu.VMEM((tokens, LANES), F32),
            pltpu.SemaphoreType.DMA((8,)),
            pltpu.SemaphoreType.DMA((5,)),
        ],
        compiler_params=params(LIMIT),
        cost_estimate=cost(2 * tokens * wide * columns, 2 * wide * columns),
    )(stats, weight, *map(in_vmem, (teacher, student)), *map(in_hbm, (own_s, other_s)))


def head_gradient_of(own, other, mine, got):
    (tokens, wide), columns = own.shape, got.shape[1]
    width = wide // 8
    strip = pl.BlockSpec((tokens, width), lambda k: (0, k))
    whole = pl.BlockSpec((tokens, columns), lambda k: (0, 0))
    return pl.pallas_call(
        head_kernel,
        name="head_gradient",
        grid=(8,),
        in_specs=[strip, strip, whole, whole],
        out_specs=pl.BlockSpec((width, columns), lambda k: (k, 0)),
        out_shape=jax.ShapeDtypeStruct((wide, columns), BF16),
        compiler_params=params(LIMIT),
        cost_estimate=cost(4 * tokens * wide * columns, 16 << 20),
    )(own, other, mine, got)


def weights(lengths, total_rows):
    seq_count = lengths.shape[0]
    ends = jnp.cumsum(lengths)
    starts = ends - lengths
    position = jnp.arange(total_rows, dtype=jnp.int32)[:, None]
    inside = (position >= starts[None, :]) & (position < ends[None, :])
    seq_len = jnp.sum(jnp.where(inside, lengths[None, :], 0), axis=1)
    return LOSS_SCALE * total_rows / seq_count / seq_len.astype(F32)


def per_device(teacher_hidden, student_hidden, teacher_head, student_head, lengths, sampled):
    group, member = lax.axis_index("grp"), lax.axis_index("vocab")
    core = member % 2
    is_first = core == 0
    wide_t, columns = teacher_head.shape
    wide_s = student_head.shape[0]
    tokens = 8 * HALF
    part_t, part_s = wide_t // 8, wide_s // 8
    strips_t, strips_s = part_t // LANES, part_s // LANES

    got_t, got_s = swap(teacher_hidden), swap(student_hidden)
    teacher_late, student_late, got_t, got_s = lax.optimization_barrier(
        (teacher_head, student_head, got_t, got_s)
    )
    other_teacher_head = swap(teacher_late)
    other_student_head = swap(student_late)

    def half(value):
        value = value.reshape(2, HALF, -1)
        return jnp.where(is_first, value[0], value[1])

    def sides(own, got):
        own, got = half(own), half(got)
        return jnp.where(is_first, own, got), jnp.where(is_first, got, own)

    def strips(a, b, count):
        rows = jnp.concatenate([a, b], axis=1).reshape(HALF, count, LANES)
        return rows.transpose(1, 0, 2).reshape(count * HALF, LANES)

    ids = sampled.reshape(2, HALF)
    ids = jnp.where(is_first, ids[0], ids[1])
    digits = jnp.stack([ids // 4096, (ids // 64) % 64, ids % 64]).astype(BF16)
    digits = jnp.pad(digits, ((0, ID_ROWS - 3), (0, LANES - HALF)))
    block = jnp.concatenate(
        [
            strips(*sides(teacher_hidden, got_t), strips_t),
            digits,
            strips(*sides(student_hidden, got_s), strips_s),
        ]
    )
    near = to_all(block, FIRST)
    units = second_gather(near)
    heads_t, heads_s = prefetch(
        teacher_head, other_teacher_head, student_head, other_student_head, units[1:4]
    )

    tables = jnp.asarray(POSITIONS)
    table = jnp.where(is_first, tables[0], tables[1])
    number_of = group * lax.axis_size("vocab") + member
    place = jnp.stack(
        [number_of * columns, (number_of + 1 - 2 * core) * columns, jnp.asarray(CORNERS)[number_of]]
    ).astype(jnp.int32)
    teacher_logits, student_logits, stats, own_rows = logits_of(table, place, units, heads_t, heads_s)
    other_rows = swap(own_rows)
    all_stats = lax.all_to_all(stats, BOTH, 0, 0, axis_index_groups=SAME_CORE)

    weight = weights(lengths, 2 * tokens).reshape(8, 2, HALF)
    weight = jnp.where(is_first, weight[:, 0], weight[:, 1]).reshape(1, tokens)
    part, grads, kl = gradient_of(
        all_stats, weight, teacher_logits, student_logits, student_head, other_student_head
    )
    got_grad = swap(grads[:, columns:])
    parts = lax.all_to_all(part.reshape(64, HALF, part_s), BOTH, 0, 0, axis_index_groups=SAME_CORE)
    head_grad = head_gradient_of(own_rows, other_rows, grads, got_grad)
    parts, head_grad = lax.optimization_barrier((parts, head_grad))
    hidden = jnp.sum(parts.astype(F32), axis=0).astype(BF16)
    one, two = hidden[:, : part_s // 2], hidden[:, part_s // 2 :]
    kept = jnp.where(is_first, one, two)
    got = swap(jnp.where(is_first, two, one))
    hidden_grad = jnp.concatenate(
        [jnp.where(is_first, kept, got), jnp.where(is_first, got, kept)], axis=0
    )

    def own_tokens(who):
        return lax.dynamic_slice(kl, (0, group * HALF + (4 * who) % HALF), (2, 4))

    got = swap(own_tokens(member + 1 - 2 * core))
    out = jnp.where(member // 8 == core, own_tokens(member), got)
    return head_grad, hidden_grad, out[0], out[1]


def solution(mesh):
    return jax.shard_map(
        per_device,
        mesh=mesh,
        in_specs=(
            P("grp", "vocab"),
            P("grp", "vocab"),
            P(None, BOTH),
            P(None, BOTH),
            P(),
            P("grp"),
        ),
        out_specs=(P(None, BOTH), P("grp", "vocab"), P(BOTH), P(BOTH)),
        check_vma=False,
    )
```

time: 505 us -> 135 us (0.27)
  blocking collectives: 256 us -> 20.8 us
  waiting for transfers between devices: 180 us -> 32.9 us
  Pallas kernels: 0 us -> 39.5 us
  matrix products: 33.7 us -> 0 us
  starting transfers between devices: 0.35 us -> 28.5 us
  between operations: 14.5 us -> 0.9 us
  local copies, waits for them, and re-layouts: 18.1 us -> 5.01 us
    reduce_scatter x1 -> x0, waiting for transfers between devices: 109 us -> none  [per_device(): lax.psum_scatter(lax.dot_general(logit_grad, student_head, (((1,), (1,)),...]
    unnamed x2 -> x0, blocking collectives: 75.5 us -> none
    all_gather x2 -> x0, waiting for transfers between devices: 70.8 us -> none  [the longest x1 56.3 us: per_device(): lax.all_gather(student_rows, 'grp', axis=0, tiled=True)]
    pmax x1 -> x0, blocking collectives: 64.3 us -> none  [per_device(): whole_top_t, whole_top_s = lax.pmax((top_t, top_s), ('grp', 'vocab'))]
    psum x1 -> x0, blocking collectives: 63.8 us -> none  [per_device(): whole_sum_t, whole_sum_s = lax.psum((sum_t, sum_s), ('grp', 'vocab'))]
    all_gather x2 -> x0, blocking collectives: 52.5 us -> none  [the longest x1 28.8 us: per_device(): lax.all_gather(teacher_hidden, 'vocab', axis=1, tiled=True)]
    pallas_call x0 -> x4, Pallas kernels: none -> 39.5 us  [the longest x1 11.8 us: logits_of(): pl.pallas_call(logits_kernel, name='logits', in_specs=[SMEM, SMEM] + [HBM...]
    dot_general x4 -> x0, matrix products: 33.7 us -> none  [the longest x1 9.7 us: per_device(): lax.dot_general(logit_grad, student_head, (((1,), (1,)), ((), ())), prefe...]
  transfers between devices with their start and end apart: 4 -> 17, of which waited for: 3 -> 8; matrix products, arithmetic and copies ran while one was open for 6% -> 7% of each run, Pallas kernels for 0% -> 21%
where the time goes in v1:
time: 135 us; the launch traced here: 134 us
  Pallas kernels  39.5 us (29%)
  waiting for transfers between devices  32.9 us (24%)
  starting transfers between devices  28.5 us (21%)
  blocking collectives  20.8 us (15%)
  other arithmetic  6.72 us (5%)
  local copies, waits for them, and re-layouts  5.01 us (4%)
    all_to_all x1, blocking collectives, to_all(): lax.all_to_all(jnp.broadcast_to(block, (size,) + block.shape), BOTH, 0, 0...  20.8 us
    ppermute x8, starting transfers between devices, swap(): return lax.ppermute(value, BOTH, SWAP)  14.9 us
    all_to_all x1, waiting for transfers between devices, per_device(): lax.all_to_all(part.reshape(64, HALF, part_s), BOTH, 0, 0, axis_index_gro...  12.1 us
    pallas_call x1, Pallas kernels, logits_of(): pl.pallas_call(logits_kernel, name='logits', in_specs=[SMEM, SMEM] + [HBM...  11.8 us
    ppermute x7, waiting for transfers between devices, along(): return lax.ppermute(value, BOTH, links(axes))  11.8 us
    pallas_call x1, Pallas kernels, head_gradient_of(): pl.pallas_call(head_kernel, name='head_gradient', grid=(8,), in_specs=[st...  10.1 us
    pallas_call x1, Pallas kernels, gradient_of(): pl.pallas_call(gradient_kernel, name='hidden_gradient', in_specs=[VMEM] *...  9.67 us
    pallas_call x1, Pallas kernels, prefetch(): pl.pallas_call(prefetch_kernel, name='prefetch_heads', in_specs=[HBM] * (...  7.92 us
  transfers between devices with their start and end apart: 17, of which 8 were waited for; matrix products, arithmetic and copies ran while one was open for 7% of the time, Pallas kernels for 21%

profile of v1, /device:TPU:1, one launch (start us, length us, event | category | flops | bytes accessed | tf_op | source)
XLA Modules:
  0.0 134.3 jit_solution(9241742064144787160)
XLA Ops:
  0.6 1.5 %collective-permute-start.1 = (bf16[64,320]{1,0:T(8,128)(2,1)}, bf16[64,320]{1,0:T(8,128)(2,1)S(1)}, u32[]{:S(2)}, u32[]{:S(2)}) collective-permute-start(bf16[64,320]{1,0:T(8,128)(2,1)} %param.9), channel_id=1, source_target_pairs={{0,1},{1,0},{2,3},{3,2},{4,5},{5,4},{6,7},{7,6},{8,9},{9,8},{10,11... | collective-permute-start | bytes 122888 | tf_op jit(solution)/shard_map/ppermute | solution.py:98
  2.2 1.3 collective-permute-done
  4.1 0.8 convert_bitcast_fusion
  4.9 0.8 broadcast_select_fusion.5
  5.9 0.7 select_bitcast_fusion.1
  6.7 20.8 %all_to_all.15.refs_0_ = bf16[8,304,128]{2,1,0:T(8,128)(2,1)S(1)} all-to-all(bf16[8,304,128]{2,1,0:T(8,128)(2,1)S(1)} %broadcast_in_dim.19), channel_id=1, replica_groups={{0,16,2,18,64,80,66,82},{32,48,34,50,96,112,98,114},{4,20,6,22,68,84,70..., dimensions={0} | all-to-all | bytes 1245184 | tf_op jit(solution)/shard_map/all_to_all | solution.py:103
  27.7 9.0 %collective-permute-done.4.third.refs_3_ = bf16[8,304,128]{2,1,0:T(8,128)(2,1)S(1)} collective-permute-done((bf16[8,304,128]{2,1,0:T(8,128)(2,1)S(1)}, bf16[8,304,128]{2,1,0:T(8,128)(2,1)S(1)}, u32[]{:S(2)}, u32[]{:S(2)}) %collective-permute-start.4) | collective-permute-done | bytes 622624 | tf_op jit(solution)/shard_map/ppermute | solution.py:110
  36.9 2.5 %collective-permute-start.7 = (bf16[8,304,128]{2,1,0:T(8,128)(2,1)S(1)}, bf16[8,304,128]{2,1,0:T(8,128)(2,1)}, u32[]{:S(2)}, u32[]{:S(2)}) collective-permute-start(bf16[8,304,128]{2,1,0:T(8,128)(2,1)S(1)} %collective-permute-done.3.second.refs_2_), channel_id=1, source_target_pairs={{0,72},{1,65},{16,88},{17,81},{32,104},{33,97},{48,120},{49,113},{... | collective-permute-start | bytes 1867784 | tf_op jit(solution)/shard_map/ppermute | solution.py:110
  39.3 1.2 collective-permute-start.6
  40.5 0.8 reduce-window.8
  41.3 1.2 dynamic_slice.9
  42.6 0.7 pad_add_fusion.place_ref
  43.3 0.7 fusion.11.table_ref
  44.0 7.9 %prefetch_heads.1 = (bf16[4096,1280]{1,0:T(8,128)(2,1)S(1)}, bf16[5120,1280]{1,0:T(8,128)(2,1)S(1)}) custom-call(bf16[4096,640]{1,0:T(8,128)(2,1)} %own_t.1, bf16[4096,640]{1,0:T(8,128)(2,1)} %collective-permute-done.9.other_t, bf16[5120,640]{1,0:T(8,128)(2,1)} %own_s.3, bf16[5120,640]{1,0:T(8,128)(2,1)} %collective-permute-done.10.other_s, ...), custom_call_target="tpu_custom_call" | custom-call | bytes 47185920 | tf_op jit(solution)/shard_map/prefetch_heads/pallas_call | solution.py:318
  51.9 1.0 collective-permute-done.5.refs_4_
  52.9 1.8 %collective-permute-done.6.refs_5_ = bf16[8,304,128]{2,1,0:T(8,128)(2,1)} collective-permute-done((bf16[8,304,128]{2,1,0:T(8,128)(2,1)S(1)}, bf16[8,304,128]{2,1,0:T(8,128)(2,1)}, u32[]{:S(2)}, u32[]{:S(2)}) %collective-permute-start.6) | collective-permute-done | bytes 622624 | tf_op jit(solution)/shard_map/ppermute | solution.py:110
  54.7 11.8 %logits.1 = (f32[256,1280]{1,0:T(8,128)S(1)}, f32[256,1280]{1,0:T(8,128)S(1)}, f32[64,8,256]{2,1,0:T(8,128)}, bf16[256,5120]{1,0:T(8,128)(2,1)}) custom-call(s32[64]{0:T(128)S(1)} %fusion.11.table_ref, s32[3]{0:T(128)S(1)} %pad_add_fusion.place_ref, bf16[8,304,128]{2,1,0:T(8,128)(2,1)} %copy-done.3, bf16[8,304,128]{2,1,0:T(8,128)(2,1)} %copy-done.2, ...), custom_call_target="tpu_custom_call" | custom-call | flops 6039797760 | bytes 8388608 | tf_op jit(solution)/shard_map/logits/pallas_call | solution.py:334
  66.6 4.6 %all-to-all-start.1 = ((f32[64,8,256]{2,1,0:T(8,128)}), f32[64,8,256]{2,1,0:T(8,128)S(1)}, u32[]{:S(2)}, u32[]{:S(2)}) async-start(f32[64,8,256]{2,1,0:T(8,128)} %get-tuple-element.25), calls=%async_computation.1 | async-start | bytes 1048576 | tf_op jit(solution)/shard_map/all_to_all | solution.py:467
  71.4 3.3 %collective-permute-start.11 = (bf16[256,5120]{1,0:T(8,128)(2,1)}, bf16[256,5120]{1,0:T(8,128)(2,1)}, u32[]{:S(2)}, u32[]{:S(2)}) collective-permute-start(bf16[256,5120]{1,0:T(8,128)(2,1)} %get-tuple-element.29.own_ref), channel_id=1, source_target_pairs={{0,1},{1,0},{2,3},{3,2},{4,5},{5,4},{6,7},{7,6},{8,9},{9,8},{10,11... | collective-permute-start | bytes 7864328 | tf_op jit(solution)/shard_map/ppermute | solution.py:98
  74.8 0.7 select_n.211.weight_ref
  75.4 6.2 %all-to-all-done.1.stats_ref = f32[64,8,256]{2,1,0:T(8,128)S(1)} async-done(((f32[64,8,256]{2,1,0:T(8,128)}), f32[64,8,256]{2,1,0:T(8,128)S(1)}, u32[]{:S(2)}, u32[]{:S(2)}) %all-to-all-start.1) | async-done | bytes 524320 | tf_op jit(solution)/shard_map/all_to_all | solution.py:467
  81.6 0.8 copy-done.4
  82.4 9.7 %hidden_gradient.1 = (bf16[8,8,32,640]{3,2,1,0:T(8,128)(2,1)}, bf16[256,1280]{1,0:T(8,128)(2,1)}, f32[8,256]{1,0:T(8,128)}) custom-call(f32[64,8,256]{2,1,0:T(8,128)} %copy-done.4, f32[1,256]{1,0:T(1,128)} %select_n.211.weight_ref, f32[256,1280]{1,0:T(8,128)S(1)} %get-tuple-element.26.teacher, f32[256,1280]{1,0:T(8,128)S(1)} %get-tuple-element.27.student, ...), custom_call_target="tpu_custom_call" | custom-call | flops 3355443200 | bytes 13107200 | tf_op jit(solution)/shard_map/hidden_gradient/pallas_call | solution.py:363
  92.1 5.0 %all-to-all-start.2 = ((bf16[64,32,640]{2,1,0:T(8,128)(2,1)}), bf16[64,32,640]{2,1,0:T(8,128)(2,1)S(1)}, u32[]{:S(2)}, u32[]{:S(2)}) async-start(bf16[64,32,640]{2,1,0:T(8,128)(2,1)} %bitcast.31), calls=%async_computation.2 | async-start | bytes 5242880 | tf_op jit(solution)/shard_map/all_to_all | solution.py:475
  97.3 4.6 %collective-permute-start.12 = (bf16[256,640]{1,0:T(8,128)(2,1)S(1)}, bf16[256,640]{1,0:T(8,128)(2,1)S(1)}, u32[]{:S(2)}, u32[]{:S(2)}) collective-permute-start(bf16[256,640]{1,0:T(8,128)(2,1)S(1)} %slice.81), channel_id=1, source_target_pairs={{0,1},{1,0},{2,3},{3,2},{4,5},{5,4},{6,7},{7,6},{8,9},{9,8},{10,11... | collective-permute-start | bytes 983048 | tf_op jit(solution)/shard_map/ppermute | solution.py:98
  101.9 0.8 constant_dynamic-slice_fusion
  102.7 1.1 collective-permute-done.14
  103.8 0.8 dynamic-slice_select_fusion
  104.6 0.7 copy-done.7
  105.3 10.1 %head_gradient.1 = bf16[5120,640]{1,0:T(8,128)(2,1)} custom-call(bf16[256,5120]{1,0:T(8,128)(2,1)} %get-tuple-element.29.own_ref, bf16[256,5120]{1,0:T(8,128)(2,1)} %collective-permute-done.11.other_ref, bf16[256,1280]{1,0:T(8,128)(2,1)} %get-tuple-element.30.mine_ref, bf16[256,640]{1,0:T(8,128)(2,1)} %copy-done.7), custom_call_target="tpu_custom_call" | custom-call | flops 3355443200 | bytes 16777216 | tf_op jit(solution)/shard_map/head_gradient/pallas_call | solution.py:391
  115.4 12.1 %all-to-all-done.2 = bf16[64,32,640]{2,1,0:T(8,128)(2,1)S(1)} async-done(((bf16[64,32,640]{2,1,0:T(8,128)(2,1)}), bf16[64,32,640]{2,1,0:T(8,128)(2,1)S(1)}, u32[]{:S(2)}, u32[]{:S(2)}) %all-to-all-start.2) | async-done | bytes 2621472 | tf_op jit(solution)/shard_map/all_to_all | solution.py:475
  127.9 4.8 %collective-permute-start.13 = (bf16[32,320]{1,0:T(8,128)(2,1)S(1)}, bf16[32,320]{1,0:T(8,128)(2,1)S(1)}, u32[]{:S(2)}, u32[]{:S(2)}) collective-permute-start(bf16[32,320]{1,0:T(8,128)(2,1)S(1)} %broadcast_select_fusion.2), channel_id=1, source_target_pairs={{0,1},{1,0},{2,3},{3,2},{4,5},{5,4},{6,7},{7,6},{8,9},{9,8},{10,11... | collective-permute-start | bytes 61448 | tf_op jit(solution)/shard_map/ppermute | solution.py:98
  (55 shorter events, 3.5 us)
Async XLA Ops:
  0.6 2.9 %collective-permute-start.1 = (bf16[64,320]{1,0:T(8,128)(2,1)}, bf16[64,320]{1,0:T(8,128)(2,1)S(1)}, u32[]{:S(2)}, u32[]{:S(2)}) collective-permute-start(bf16[64,320]{1,0:T(8,128)(2,1)} %param.9), channel_id=1, source_target_pairs={{0,1},{1,0},{2,3},{3,2},{4,5},{5,4},{6,7},{7,6},{8,9},{9,8},{10,11... | collective-permute-start | bytes 122888 | tf_op jit(solution)/shard_map/ppermute | solution.py:98
  2.1 1.4 %collective-permute-start = (bf16[64,256]{1,0:T(8,128)(2,1)}, bf16[64,256]{1,0:T(8,128)(2,1)S(1)}, u32[]{:S(2)}, u32[]{:S(2)}) collective-permute-start(bf16[64,256]{1,0:T(8,128)(2,1)} %param.8), channel_id=1, source_target_pairs={{0,1},{1,0},{2,3},{3,2},{4,5},{5,4},{6,7},{7,6},{8,9},{9,8},{10,11... | collective-permute-start | bytes 98312 | tf_op jit(solution)/shard_map/ppermute | solution.py:98
  3.6 40.4 %collective-permute-start.10 = (bf16[5120,640]{1,0:T(8,128)(2,1)}, bf16[5120,640]{1,0:T(8,128)(2,1)}, u32[]{:S(2)}, u32[]{:S(2)}) collective-permute-start(bf16[5120,640]{1,0:T(8,128)(2,1)} %own_s.3), channel_id=1, source_target_pairs={{0,1},{1,0},{2,3},{3,2},{4,5},{5,4},{6,7},{7,6},{8,9},{9,8},{10,11... | collective-permute-start | bytes 19660808 | tf_op jit(solution)/shard_map/ppermute | solution.py:98
  3.7 35.6 %collective-permute-start.9 = (bf16[4096,640]{1,0:T(8,128)(2,1)}, bf16[4096,640]{1,0:T(8,128)(2,1)}, u32[]{:S(2)}, u32[]{:S(2)}) collective-permute-start(bf16[4096,640]{1,0:T(8,128)(2,1)} %own_t.1), channel_id=1, source_target_pairs={{0,1},{1,0},{2,3},{3,2},{4,5},{5,4},{6,7},{7,6},{8,9},{9,8},{10,11... | collective-permute-start | bytes 15728648 | tf_op jit(solution)/shard_map/ppermute | solution.py:98
  27.6 27.1 %copy-start.3 = (bf16[8,304,128]{2,1,0:T(8,128)(2,1)}, bf16[8,304,128]{2,1,0:T(8,128)(2,1)S(1)}, u32[]{:S(2)}) copy-start(bf16[8,304,128]{2,1,0:T(8,128)(2,1)S(1)} %all_to_all.15.refs_0_) | copy-start | bytes 1867780
  27.6 9.1 %collective-permute-start.4 = (bf16[8,304,128]{2,1,0:T(8,128)(2,1)S(1)}, bf16[8,304,128]{2,1,0:T(8,128)(2,1)S(1)}, u32[]{:S(2)}, u32[]{:S(2)}) collective-permute-start(bf16[8,304,128]{2,1,0:T(8,128)(2,1)S(1)} %all_to_all.15.refs_0_), channel_id=1, source_target_pairs={{0,48},{1,17},{16,32},{17,1},{32,16},{33,49},{48,0},{49,33},{2,50}... | collective-permute-start | bytes 1867784 | tf_op jit(solution)/shard_map/ppermute | solution.py:110
  27.6 9.1 %collective-permute-start.3 = (bf16[8,304,128]{2,1,0:T(8,128)(2,1)S(1)}, bf16[8,304,128]{2,1,0:T(8,128)(2,1)S(1)}, u32[]{:S(2)}, u32[]{:S(2)}) collective-permute-start(bf16[8,304,128]{2,1,0:T(8,128)(2,1)S(1)} %all_to_all.15.refs_0_), channel_id=1, source_target_pairs={{0,6},{1,3},{16,22},{17,19},{32,38},{33,35},{48,54},{49,51},{2,4},... | collective-permute-start | bytes 1867784 | tf_op jit(solution)/shard_map/ppermute | solution.py:110
  27.6 9.3 %collective-permute-start.2 = (bf16[8,304,128]{2,1,0:T(8,128)(2,1)S(1)}, bf16[8,304,128]{2,1,0:T(8,128)(2,1)S(1)}, u32[]{:S(2)}, u32[]{:S(2)}) collective-permute-start(bf16[8,304,128]{2,1,0:T(8,128)(2,1)S(1)} %all_to_all.15.refs_0_), channel_id=1, source_target_pairs={{0,72},{1,65},{16,88},{17,81},{32,104},{33,97},{48,120},{49,113},{... | collective-permute-start | bytes 1867784 | tf_op jit(solution)/shard_map/ppermute | solution.py:110
  36.6 7.3 %copy-start = (bf16[8,304,128]{2,1,0:T(8,128)(2,1)}, bf16[8,304,128]{2,1,0:T(8,128)(2,1)S(1)}, u32[]{:S(2)}) copy-start(bf16[8,304,128]{2,1,0:T(8,128)(2,1)S(1)} %collective-permute-done.4.third.refs_3_) | copy-start | bytes 1867780
  36.6 15.2 %collective-permute-start.8 = (bf16[8,304,128]{2,1,0:T(8,128)(2,1)S(1)}, bf16[8,304,128]{2,1,0:T(8,128)(2,1)S(1)}, u32[]{:S(2)}, u32[]{:S(2)}) collective-permute-start(bf16[8,304,128]{2,1,0:T(8,128)(2,1)S(1)} %all_to_all.15.refs_0_), channel_id=1, source_target_pairs={{0,126},{1,83},{16,110},{17,67},{32,94},{33,115},{48,78},{49,99},{... | collective-permute-start | bytes 1867784 | tf_op jit(solution)/shard_map/ppermute | solution.py:110
  36.7 7.3 %copy-start.1 = (bf16[8,304,128]{2,1,0:T(8,128)(2,1)}, bf16[8,304,128]{2,1,0:T(8,128)(2,1)S(1)}, u32[]{:S(2)}) copy-start(bf16[8,304,128]{2,1,0:T(8,128)(2,1)S(1)} %collective-permute-done.3.second.refs_2_) | copy-start | bytes 1867780
  36.7 16.2 %collective-permute-start.5 = (bf16[8,304,128]{2,1,0:T(8,128)(2,1)S(1)}, bf16[8,304,128]{2,1,0:T(8,128)(2,1)}, u32[]{:S(2)}, u32[]{:S(2)}) collective-permute-start(bf16[8,304,128]{2,1,0:T(8,128)(2,1)S(1)} %collective-permute-done.4.third.refs_3_), channel_id=1, source_target_pairs={{0,6},{1,3},{16,22},{17,19},{32,38},{33,35},{48,54},{49,51},{2,4},... | collective-permute-start | bytes 1867784 | tf_op jit(solution)/shard_map/ppermute | solution.py:110
  36.9 7.1 %copy-start.2 = (bf16[8,304,128]{2,1,0:T(8,128)(2,1)}, bf16[8,304,128]{2,1,0:T(8,128)(2,1)S(1)}, u32[]{:S(2)}) copy-start(bf16[8,304,128]{2,1,0:T(8,128)(2,1)S(1)} %collective-permute-done.2.first.refs_1_) | copy-start | bytes 1867780
  36.9 16.0 %collective-permute-start.7 = (bf16[8,304,128]{2,1,0:T(8,128)(2,1)S(1)}, bf16[8,304,128]{2,1,0:T(8,128)(2,1)}, u32[]{:S(2)}, u32[]{:S(2)}) collective-permute-start(bf16[8,304,128]{2,1,0:T(8,128)(2,1)S(1)} %collective-permute-done.3.second.refs_2_), channel_id=1, source_target_pairs={{0,72},{1,65},{16,88},{17,81},{32,104},{33,97},{48,120},{49,113},{... | collective-permute-start | bytes 1867784 | tf_op jit(solution)/shard_map/ppermute | solution.py:110
  39.3 15.4 %collective-permute-start.6 = (bf16[8,304,128]{2,1,0:T(8,128)(2,1)S(1)}, bf16[8,304,128]{2,1,0:T(8,128)(2,1)}, u32[]{:S(2)}, u32[]{:S(2)}) collective-permute-start(bf16[8,304,128]{2,1,0:T(8,128)(2,1)S(1)} %collective-permute-done.2.first.refs_1_), channel_id=1, source_target_pairs={{0,48},{1,17},{16,32},{17,1},{32,16},{33,49},{48,0},{49,33},{2,50}... | collective-permute-start | bytes 1867784 | tf_op jit(solution)/shard_map/ppermute | solution.py:110
  51.9 2.8 %copy-start.6 = (bf16[8,304,128]{2,1,0:T(8,128)(2,1)}, bf16[8,304,128]{2,1,0:T(8,128)(2,1)S(1)}, u32[]{:S(2)}) copy-start(bf16[8,304,128]{2,1,0:T(8,128)(2,1)S(1)} %collective-permute-done.8.refs_7_) | copy-start | bytes 1867780
  54.7 16.5 %copy-start.8 = (s32[8]{0:T(128)S(1)}, s32[8]{0:T(128)}, u32[]{:S(2)}) copy-start(s32[8]{0:T(128)} %param.12) | copy-start | bytes 100
  66.6 15.1 %all-to-all-start.1 = ((f32[64,8,256]{2,1,0:T(8,128)}), f32[64,8,256]{2,1,0:T(8,128)S(1)}, u32[]{:S(2)}, u32[]{:S(2)}) async-start(f32[64,8,256]{2,1,0:T(8,128)} %get-tuple-element.25), calls=%async_computation.1 | async-start | bytes 1048576 | tf_op jit(solution)/shard_map/all_to_all | solution.py:467
  71.4 33.2 %collective-permute-start.11 = (bf16[256,5120]{1,0:T(8,128)(2,1)}, bf16[256,5120]{1,0:T(8,128)(2,1)}, u32[]{:S(2)}, u32[]{:S(2)}) collective-permute-start(bf16[256,5120]{1,0:T(8,128)(2,1)} %get-tuple-element.29.own_ref), channel_id=1, source_target_pairs={{0,1},{1,0},{2,3},{3,2},{4,5},{5,4},{6,7},{7,6},{8,9},{9,8},{10,11... | collective-permute-start | bytes 7864328 | tf_op jit(solution)/shard_map/ppermute | solution.py:98
  81.6 0.8 copy-start.4
  92.1 5.1 %copy-start.5 = (bf16[256,1280]{1,0:T(8,128)(2,1)S(1)}, bf16[256,1280]{1,0:T(8,128)(2,1)}, u32[]{:S(2)}) copy-start(bf16[256,1280]{1,0:T(8,128)(2,1)} %get-tuple-element.30.mine_ref) | copy-start | bytes 1966084
  92.1 35.3 %all-to-all-start.2 = ((bf16[64,32,640]{2,1,0:T(8,128)(2,1)}), bf16[64,32,640]{2,1,0:T(8,128)(2,1)S(1)}, u32[]{:S(2)}, u32[]{:S(2)}) async-start(bf16[64,32,640]{2,1,0:T(8,128)(2,1)} %bitcast.31), calls=%async_computation.2 | async-start | bytes 5242880 | tf_op jit(solution)/shard_map/all_to_all | solution.py:475
  97.3 7.3 %collective-permute-start.12 = (bf16[256,640]{1,0:T(8,128)(2,1)S(1)}, bf16[256,640]{1,0:T(8,128)(2,1)S(1)}, u32[]{:S(2)}, u32[]{:S(2)}) collective-permute-start(bf16[256,640]{1,0:T(8,128)(2,1)S(1)} %slice.81), channel_id=1, source_target_pairs={{0,1},{1,0},{2,3},{3,2},{4,5},{5,4},{6,7},{7,6},{8,9},{9,8},{10,11... | collective-permute-start | bytes 983048 | tf_op jit(solution)/shard_map/ppermute | solution.py:98
  102.7 1.1 collective-permute-start.14
  104.6 0.7 copy-start.7
  127.9 5.6 %collective-permute-start.13 = (bf16[32,320]{1,0:T(8,128)(2,1)S(1)}, bf16[32,320]{1,0:T(8,128)(2,1)S(1)}, u32[]{:S(2)}, u32[]{:S(2)}) collective-permute-start(bf16[32,320]{1,0:T(8,128)(2,1)S(1)} %broadcast_select_fusion.2), channel_id=1, source_target_pairs={{0,1},{1,0},{2,3},{3,2},{4,5},{5,4},{6,7},{7,6},{8,9},{9,8},{10,11... | collective-permute-start | bytes 61448 | tf_op jit(solution)/shard_map/ppermute | solution.py:98

commit v2 on v1

--- a/solution.py
+++ b/solution.py
@@ -17,7 +17,9 @@
 ID_ROWS = 16
 PIECES = 2
 LIMIT = 56
-DEPTH = 4
+DEPTH = 8
+TILE = 256
+SHARES = ((0, 1), (2, 3), (4, 5), (6,), (7,))
 CORNER_OF = (0, 4, 2, 1, 3, 5, 6, 7)
 
 
@@ -71,14 +73,6 @@
     return table
 
 
-def corners():
-    table = np.zeros(128, np.int32)
-    for place in chips():
-        table[device(*place, 0)] = number(high, place)
-        table[device(*place, 1)] = number(parity, place)
-    return table
-
-
 def links(axes):
     pairs = []
     for place in chips():
@@ -91,7 +85,6 @@
 
 
 POSITIONS = positions()
-CORNERS = corners()
 
 
 def swap(value):
@@ -115,8 +108,8 @@
     return [near, *one, *two, far]
 
 
-def rows_of(table_ref, blocks_ref, chunk, at, strips):
-    parts = [blocks_ref[table_ref[group * 8 + chunk], at : at + strips * HALF] for group in range(8)]
+def rows_of(core, blocks_ref, chunk, at, strips):
+    parts = [blocks_ref[position(core, group, chunk), at : at + strips * HALF] for group in range(8)]
     return jnp.concatenate(
         [
             jnp.concatenate([p[s * HALF : (s + 1) * HALF] for p in parts], axis=0)
@@ -124,6 +117,11 @@
         ],
         axis=1,
     )
+
+
+def position(core, group, chunk):
+    zero, one = (int(table[group * 8 + chunk]) for table in POSITIONS)
+    return zero + core * (one - zero)
 
 
 class Stream:
@@ -169,20 +167,27 @@
 
 
 def logits_kernel(
-    table_ref, place_ref, *refs
+    place_ref, *refs
 ):
     units, (heads_t, heads_s, teacher, student, stats_out, lhs_out) = refs[:8], refs[8:14]
     blocks_ref, lhs_t, lhs_s, powers, stats, work, sems, out_sems = refs[14:]
+    core = place_ref[3]
+    at_s = 4 * HALF + ID_ROWS
     arriving = []
-    for n, unit in enumerate(units):
-        start = (place_ref[2] ^ CORNER_OF[n]) * 8
-        arriving.append(pltpu.make_async_copy(unit, blocks_ref.at[pl.ds(start, 8)], sems.at[n]))
-        arriving[-1].start()
+    for part, (at, size) in enumerate(((0, at_s), (at_s, 5 * HALF))):
+        for n, unit in enumerate(units):
+            start = (place_ref[2] ^ CORNER_OF[n]) * 8
+            rows = pl.ds(at, size)
+            arriving.append(
+                pltpu.make_async_copy(
+                    unit.at[:, rows], blocks_ref.at[pl.ds(start, 8), rows], sems.at[part, n]
+                )
+            )
+            arriving[-1].start()
     columns = heads_t.shape[1] // 2
     lane = lax.broadcasted_iota(jnp.int32, (HALF, LANES), 1)
     column = lax.broadcasted_iota(jnp.int32, (HALF, columns), 1)
     column = jnp.concatenate([column + place_ref[0], column + place_ref[1]], axis=1)
-    at_s = 4 * HALF + ID_ROWS
 
     def columns_of(values, first):
         row = jnp.zeros((HALF, LANES), F32)
@@ -190,19 +195,7 @@
             row = jnp.where(lane == first + j, value, row)
         return row
 
-    for copy in arriving:
-        copy.wait()
-    for chunk in range(8):
-        lhs_t[:, chunk * 4 * LANES : (chunk + 1) * 4 * LANES] = rows_of(table_ref, blocks_ref, chunk, 0, 4)
-    teacher[...] = jnp.dot(lhs_t[...], heads_t[...], preferred_element_type=F32)
-    for chunk in range(8):
-        lhs_s[:, chunk * 5 * LANES : (chunk + 1) * 5 * LANES] = rows_of(table_ref, blocks_ref, chunk, at_s, 5)
-    leaving = [pltpu.make_async_copy(lhs_s, lhs_out, out_sems.at[0])]
-    leaving[0].start()
-    digits = [blocks_ref[table_ref[group * 8], 4 * HALF : at_s].astype(F32) for group in range(8)]
-    ids = jnp.concatenate([d[0:1] * 4096.0 + d[1:2] * 64.0 + d[2:3] for d in digits], axis=0)
-    ids = jnp.concatenate([ids, jnp.zeros((LANES - 8, LANES), F32)], axis=0).T.astype(jnp.int32)
-    for group in range(8):
+    def teacher_values(group):
         rows = pl.ds(group * HALF, HALF)
         t = teacher[rows, :]
         top = jnp.max(t, axis=1, keepdims=True)
@@ -212,7 +205,30 @@
         work[rows, :] = columns_of(
             (top, jnp.sum(e, axis=1, keepdims=True), jnp.sum(e * t, axis=1, keepdims=True)), 0
         )
-    student[...] = jnp.dot(lhs_s[...], heads_s[...], preferred_element_type=F32)
+
+    for copy in arriving[:8]:
+        copy.wait()
+    for chunk in range(8):
+        lhs_t[:, chunk * 4 * LANES : (chunk + 1) * 4 * LANES] = rows_of(core, blocks_ref, chunk, 0, 4)
+    for copy in arriving[8:]:
+        copy.wait()
+    for j, chunks in enumerate(SHARES):
+        at = slice(j * TILE, (j + 1) * TILE)
+        teacher[:, at] = jnp.dot(lhs_t[...], heads_t[:, at], preferred_element_type=F32)
+        for chunk in chunks:
+            lhs_s[:, chunk * 5 * LANES : (chunk + 1) * 5 * LANES] = rows_of(
+                core, blocks_ref, chunk, at_s, 5
+            )
+    leaving = [pltpu.make_async_copy(lhs_s, lhs_out, out_sems.at[0])]
+    leaving[0].start()
+    for j, groups in enumerate(SHARES):
+        at = slice(j * TILE, (j + 1) * TILE)
+        student[:, at] = jnp.dot(lhs_s[...], heads_s[:, at], preferred_element_type=F32)
+        for group in groups:
+            teacher_values(group)
+    digits = [blocks_ref[position(core, group, 0), 4 * HALF : at_s].astype(F32) for group in range(8)]
+    ids = jnp.concatenate([d[0:1] * 4096.0 + d[1:2] * 64.0 + d[2:3] for d in digits], axis=0)
+    ids = jnp.concatenate([ids, jnp.zeros((LANES - 8, LANES), F32)], axis=0).T.astype(jnp.int32)
     for group in range(8):
         rows = pl.ds(group * HALF, HALF)
         s = student[rows, :]
@@ -220,10 +236,15 @@
         picked = jnp.sum(jnp.where(hit, teacher[rows, :] - s, 0.0), axis=1, keepdims=True)
         top = jnp.max(s, axis=1, keepdims=True)
         s = s - top
-        total = jnp.sum(jnp.exp(s), axis=1, keepdims=True)
+        log_s = jnp.log(jnp.sum(jnp.exp(s), axis=1, keepdims=True))
         term = jnp.sum(powers[rows, :] * s, axis=1, keepdims=True)
-        work[rows, :] += columns_of((top, total, term, picked), 3)
-    stats[...] = jnp.broadcast_to(work[...].T[:8, :], stats.shape)
+        top_t, sum_t, term_t = (work[rows, j : j + 1] for j in range(3))
+        log_t = jnp.log(sum_t)
+        ratio = (term_t - term) / sum_t - (log_t - log_s)
+        work[rows, :] = columns_of((top_t + log_t, top + log_s, ratio, picked), 0)
+    values = work[...].T
+    values = [values[j : j + 1, h * LANES : (h + 1) * LANES] for j in range(4) for h in range(2)]
+    stats[...] = jnp.broadcast_to(jnp.concatenate(values, axis=0), stats.shape)
     leaving.append(pltpu.make_async_copy(stats, stats_out, out_sems.at[1]))
     leaving[1].start()
     for copy in leaving:
@@ -231,7 +252,7 @@
 
 
 def gradient_kernel(
-    stats_ref, weight_ref, teacher, student, own_s, other_s, part_out, grads_out, kl_ref,
+    place_ref, lengths_ref, stats_ref, teacher, student, own_s, other_s, part_out, grads_out, kl_ref,
     heads, part, grads, work, sems, out_sems,
 ):
     stream = Stream(sems)
@@ -241,20 +262,32 @@
         for j, ref in enumerate((own_s, other_s)):
             stream.add(ref.at[at], heads.at[at, pl.ds(j * columns, columns)])
     stream.start(DEPTH)
-    top_t, sum_t, term_t, top_s, sum_s, term_s, picked = (stats_ref[:, j, :] for j in range(7))
-    whole_t = jnp.max(top_t, axis=0, keepdims=True)
-    whole_s = jnp.max(top_s, axis=0, keepdims=True)
-    scale_t = jnp.exp(top_t - whole_t)
-    total_t = jnp.sum(scale_t * sum_t, axis=0, keepdims=True)
-    total_s = jnp.sum(jnp.exp(top_s - whole_s) * sum_s, axis=0, keepdims=True)
-    log_t, log_s = jnp.log(total_t), jnp.log(total_s)
-    shift = (top_t - whole_t) - (top_s - whole_s)
-    kl = jnp.sum(scale_t * (term_t - term_s + sum_t * shift), axis=0, keepdims=True) / total_t - (log_t - log_s)
-    lse_t, lse_s = whole_t + log_t, whole_s + log_s
-    ratio = jnp.sum(picked, axis=0, keepdims=True) - (lse_t - lse_s)
-    tokens = kl.shape[1]
-    kl_ref[...] = jnp.concatenate([kl, ratio, jnp.zeros((6, tokens), F32)], axis=0)
-    rows = jnp.concatenate([lse_t, lse_s, weight_ref[...], jnp.zeros((LANES - 3, tokens), F32)], axis=0)
+    part_t, part_s, ratios, picked = (stats_ref[:, 2 * j : 2 * j + 2, :] for j in range(4))
+
+    def log_sum(parts):
+        top = jnp.max(parts, axis=0, keepdims=True)
+        return top + jnp.log(jnp.sum(jnp.exp(parts - top), axis=0, keepdims=True))
+
+    lse_t, lse_s = log_sum(part_t), log_sum(part_s)
+    from_t = part_t - lse_t
+    kl = jnp.sum(jnp.exp(from_t) * (ratios + (from_t - (part_s - lse_s))), axis=0)
+    lse_t, lse_s = lse_t[0], lse_s[0]
+    ratio = jnp.sum(picked, axis=0) - (lse_t - lse_s)
+
+    def row(value):
+        return jnp.concatenate([value[0:1], value[1:2]], axis=1)
+
+    tokens = 2 * LANES
+    kl_ref[...] = jnp.concatenate([row(kl), row(ratio), jnp.zeros((6, tokens), F32)], axis=0)
+    token = lax.broadcasted_iota(jnp.int32, (1, tokens), 1)
+    token = token + (token // HALF + place_ref[3]) * HALF
+    length, end = jnp.zeros((1, tokens), jnp.int32), jnp.int32(0)
+    for i in range(lengths_ref.shape[0]):
+        inside = token >= end
+        end = end + lengths_ref[i]
+        length = jnp.where(inside & (token < end), lengths_ref[i], length)
+    weight = (LOSS_SCALE * 2 * tokens / lengths_ref.shape[0]) / length.astype(F32)
+    rows = jnp.concatenate([row(lse_t), row(lse_s), weight, jnp.zeros((LANES - 3, tokens), F32)], axis=0)
     work[...] = rows.T
 
     for i in range(tokens // HALF):
@@ -318,28 +351,28 @@
     return pl.pallas_call(
         prefetch_kernel,
         name="prefetch_heads",
-        in_specs=[HBM] * (4 + len(after)),
+        in_specs=[HBM] * 4 + [pl.BlockSpec(memory_space=pl.ANY)] * len(after),
         out_specs=[VMEM] * 2,
         out_shape=[pltpu.VMEM((wide_t, 2 * columns), BF16), pltpu.VMEM((wide_s, 2 * columns), BF16)],
         scratch_shapes=[pltpu.SemaphoreType.DMA((16,))],
         compiler_params=params(2),
         cost_estimate=cost(0, 8 * (wide_t + wide_s) * columns),
-    )(*map(in_hbm, (own_t, other_t, own_s, other_s, *after)))
-
-
-def logits_of(table, place, units, heads_t, heads_s):
+    )(*map(in_hbm, (own_t, other_t, own_s, other_s)), *after)
+
+
+def logits_of(place, units, heads_t, heads_s):
     tokens = 8 * HALF
     (wide_t, columns), wide_s = heads_t.shape, heads_s.shape[0]
     logits = pltpu.VMEM((tokens, columns), F32)
     return pl.pallas_call(
         logits_kernel,
         name="logits",
-        in_specs=[SMEM, SMEM] + [HBM] * 8 + [VMEM] * 2,
+        in_specs=[SMEM] + [HBM] * 8 + [VMEM] * 2,
         out_specs=[VMEM, VMEM, HBM, HBM],
         out_shape=[
             logits,
             logits,
-            pltpu.HBM((64, 8, tokens), F32),
+            pltpu.HBM((64, 8, LANES), F32),
             pltpu.HBM((tokens, wide_s), BF16),
         ],
         scratch_shapes=[
@@ -347,23 +380,23 @@
             pltpu.VMEM((tokens, wide_t), BF16),
             pltpu.VMEM((tokens, wide_s), BF16),
             pltpu.VMEM((tokens, columns), F32),
-            pltpu.VMEM((64, 8, tokens), F32),
+            pltpu.VMEM((64, 8, LANES), F32),
             pltpu.VMEM((tokens, LANES), F32),
-            pltpu.SemaphoreType.DMA((8,)),
+            pltpu.SemaphoreType.DMA((2, 8)),
             pltpu.SemaphoreType.DMA((2,)),
         ],
         compiler_params=params(24),
         cost_estimate=cost(2 * tokens * (wide_t + wide_s) * columns, 8 << 20),
-    )(table, place, *map(in_hbm, units), *map(in_vmem, (heads_t, heads_s)))
-
-
-def gradient_of(stats, weight, teacher, student, own_s, other_s):
+    )(place, *map(in_hbm, units), *map(in_vmem, (heads_t, heads_s)))
+
+
+def gradient_of(place, lengths, stats, teacher, student, own_s, other_s):
     tokens, columns = teacher.shape
     wide = own_s.shape[0]
     return pl.pallas_call(
         gradient_kernel,
         name="hidden_gradient",
-        in_specs=[VMEM] * 4 + [HBM] * 2,
+        in_specs=[SMEM] * 2 + [VMEM] * 3 + [HBM] * 2,
         out_specs=[HBM, HBM, VMEM],
         out_shape=[
             pltpu.HBM((8, 8, HALF, wide // 8), BF16),
@@ -380,7 +413,7 @@
         ],
         compiler_params=params(LIMIT),
         cost_estimate=cost(2 * tokens * wide * columns, 2 * wide * columns),
-    )(stats, weight, *map(in_vmem, (teacher, student)), *map(in_hbm, (own_s, other_s)))
+    )(place, lengths, *map(in_vmem, (stats, teacher, student)), *map(in_hbm, (own_s, other_s)))
 
 
 def head_gradient_of(own, other, mine, got):
@@ -400,16 +433,6 @@
     )(own, other, mine, got)
 
 
-def weights(lengths, total_rows):
-    seq_count = lengths.shape[0]
-    ends = jnp.cumsum(lengths)
-    starts = ends - lengths
-    position = jnp.arange(total_rows, dtype=jnp.int32)[:, None]
-    inside = (position >= starts[None, :]) & (position < ends[None, :])
-    seq_len = jnp.sum(jnp.where(inside, lengths[None, :], 0), axis=1)
-    return LOSS_SCALE * total_rows / seq_count / seq_len.astype(F32)
-
-
 def per_device(teacher_hidden, student_hidden, teacher_head, student_head, lengths, sampled):
     group, member = lax.axis_index("grp"), lax.axis_index("vocab")
     core = member % 2
@@ -456,20 +479,18 @@
         teacher_head, other_teacher_head, student_head, other_student_head, units[1:4]
     )
 
-    tables = jnp.asarray(POSITIONS)
-    table = jnp.where(is_first, tables[0], tables[1])
     number_of = group * lax.axis_size("vocab") + member
-    place = jnp.stack(
-        [number_of * columns, (number_of + 1 - 2 * core) * columns, jnp.asarray(CORNERS)[number_of]]
-    ).astype(jnp.int32)
-    teacher_logits, student_logits, stats, own_rows = logits_of(table, place, units, heads_t, heads_s)
+    x_high, y, x_low, z = member // 8, member // 2 % 4, group // 4, group % 4
+    corner = x_high * 4 + y // 2 * 2 + z // 2
+    corner = corner ^ (core * (x_low * 4 + y % 2 * 2 + z % 2))
+    place = [number_of * columns, (number_of + 1 - 2 * core) * columns, corner, core]
+    place = jnp.stack(place).astype(jnp.int32)
+    teacher_logits, student_logits, stats, own_rows = logits_of(place, units, heads_t, heads_s)
     other_rows = swap(own_rows)
     all_stats = lax.all_to_all(stats, BOTH, 0, 0, axis_index_groups=SAME_CORE)
 
-    weight = weights(lengths, 2 * tokens).reshape(8, 2, HALF)
-    weight = jnp.where(is_first, weight[:, 0], weight[:, 1]).reshape(1, tokens)
     part, grads, kl = gradient_of(
-        all_stats, weight, teacher_logits, student_logits, student_head, other_student_head
+        place, lengths, all_stats, teacher_logits, student_logits, student_head, other_student_head
     )
     got_grad = swap(grads[:, columns:])
     parts = lax.all_to_all(part.reshape(64, HALF, part_s), BOTH, 0, 0, axis_index_groups=SAME_CORE)

time: 135 us -> 133 us (0.985)
  waiting for transfers between devices: 32.9 us -> 36 us
  local copies, waits for them, and re-layouts: 5.01 us -> 2.24 us
  other arithmetic: 6.72 us -> 4.47 us
    ppermute x7, waiting for transfers between devices: 11.8 us -> 15.1 us  [along(): return lax.ppermute(value, BOTH, links(axes))]
    another operation x2 -> x1, other arithmetic: 1.55 us -> 0.08 us  [per_device(): place = jnp.stack(place).astype(jnp.int32)]
  transfers between devices with their start and end apart: 17 -> 17, of which waited for: 8 -> 8; matrix products, arithmetic and copies ran while one was open for 7% -> 4% of each run, Pallas kernels for 21% -> 21%
where the time goes in v2:
time: 133 us; the launch traced here: 132 us
  Pallas kernels  39.2 us (29%)
  waiting for transfers between devices  36 us (27%)
  starting transfers between devices  28.4 us (21%)
  blocking collectives  20.8 us (16%)
  other arithmetic  4.47 us (3%)
  local copies, waits for them, and re-layouts  2.24 us (2%)
    all_to_all x1, blocking collectives, to_all(): lax.all_to_all(jnp.broadcast_to(block, (size,) + block.shape), BOTH, 0, 0...  20.8 us
    ppermute x7, waiting for transfers between devices, along(): return lax.ppermute(value, BOTH, links(axes))  15.1 us
    ppermute x8, starting transfers between devices, swap(): return lax.ppermute(value, BOTH, SWAP)  15 us
    all_to_all x1, waiting for transfers between devices, per_device(): lax.all_to_all(part.reshape(64, HALF, part_s), BOTH, 0, 0, axis_index_gro...  12.2 us
    pallas_call x1, Pallas kernels, logits_of(): pl.pallas_call(logits_kernel, name='logits', in_specs=[SMEM] + [HBM] * 8...  11.8 us
    pallas_call x1, Pallas kernels, head_gradient_of(): pl.pallas_call(head_kernel, name='head_gradient', grid=(8,), in_specs=[st...  10 us
    pallas_call x1, Pallas kernels, gradient_of(): pl.pallas_call(gradient_kernel, name='hidden_gradient', in_specs=[SMEM] *...  9.47 us
    pallas_call x1, Pallas kernels, prefetch(): pl.pallas_call(prefetch_kernel, name='prefetch_heads', in_specs=[HBM] * 4...  7.91 us
  transfers between devices with their start and end apart: 17, of which 8 were waited for; matrix products, arithmetic and copies ran while one was open for 4% of the time, Pallas kernels for 21%

profile of v2, /device:TPU:1, one launch (start us, length us, event | category | flops | bytes accessed | tf_op | source)
XLA Modules:
  0.0 132.0 jit_solution(2483424139190904682)
XLA Ops:
  0.6 1.5 %collective-permute-start.1 = (bf16[64,320]{1,0:T(8,128)(2,1)}, bf16[64,320]{1,0:T(8,128)(2,1)S(1)}, u32[]{:S(2)}, u32[]{:S(2)}) collective-permute-start(bf16[64,320]{1,0:T(8,128)(2,1)} %param.7), channel_id=1, source_target_pairs={{0,1},{1,0},{2,3},{3,2},{4,5},{5,4},{6,7},{7,6},{8,9},{9,8},{10,11... | collective-permute-start | bytes 122888 | tf_op jit(solution)/shard_map/ppermute | solution.py:91
  2.2 1.3 %collective-permute-done = bf16[64,256]{1,0:T(8,128)(2,1)S(1)} collective-permute-done((bf16[64,256]{1,0:T(8,128)(2,1)}, bf16[64,256]{1,0:T(8,128)(2,1)S(1)}, u32[]{:S(2)}, u32[]{:S(2)}) %collective-permute-start) | collective-permute-done | bytes 32800 | tf_op jit(solution)/shard_map/ppermute | solution.py:91
  3.7 0.3 collective-permute-start.9
  4.1 0.8 convert_bitcast_fusion
  4.9 0.8 broadcast_select_fusion.5
  5.9 0.7 select_bitcast_fusion.1
  6.7 20.8 %all_to_all.15.refs_0_ = bf16[8,304,128]{2,1,0:T(8,128)(2,1)S(1)} all-to-all(bf16[8,304,128]{2,1,0:T(8,128)(2,1)S(1)} %broadcast_in_dim.3), channel_id=1, replica_groups={{0,16,2,18,64,80,66,82},{32,48,34,50,96,112,98,114},{4,20,6,22,68,84,70..., dimensions={0} | all-to-all | bytes 1245184 | tf_op jit(solution)/shard_map/all_to_all | solution.py:96
  27.7 9.0 %collective-permute-done.4.third.refs_3_ = bf16[8,304,128]{2,1,0:T(8,128)(2,1)S(1)} collective-permute-done((bf16[8,304,128]{2,1,0:T(8,128)(2,1)S(1)}, bf16[8,304,128]{2,1,0:T(8,128)(2,1)S(1)}, u32[]{:S(2)}, u32[]{:S(2)}) %collective-permute-start.4) | collective-permute-done | bytes 622624 | tf_op jit(solution)/shard_map/ppermute | solution.py:103
  36.7 0.2 collective-permute-start.5
  36.9 2.5 %collective-permute-start.7 = (bf16[8,304,128]{2,1,0:T(8,128)(2,1)S(1)}, bf16[8,304,128]{2,1,0:T(8,128)(2,1)}, u32[]{:S(2)}, u32[]{:S(2)}) collective-permute-start(bf16[8,304,128]{2,1,0:T(8,128)(2,1)S(1)} %collective-permute-done.3.second.refs_2_), channel_id=1, source_target_pairs={{0,72},{1,65},{16,88},{17,81},{32,104},{33,97},{48,120},{49,113},{... | collective-permute-start | bytes 1867784 | tf_op jit(solution)/shard_map/ppermute | solution.py:103
  39.3 1.2 collective-permute-start.6
  40.6 7.9 %prefetch_heads.1 = (bf16[4096,1280]{1,0:T(8,128)(2,1)S(1)}, bf16[5120,1280]{1,0:T(8,128)(2,1)S(1)}) custom-call(bf16[4096,640]{1,0:T(8,128)(2,1)} %own_t.1, bf16[4096,640]{1,0:T(8,128)(2,1)} %collective-permute-done.9.other_t, bf16[5120,640]{1,0:T(8,128)(2,1)} %own_s.3, bf16[5120,640]{1,0:T(8,128)(2,1)} %collective-permute-done.10.other_s, ...), custom_call_target="tpu_custom_call" | custom-call | bytes 47185920 | tf_op jit(solution)/shard_map/prefetch_heads/pallas_call | solution.py:351
  48.6 4.3 %collective-permute-done.5.refs_4_ = bf16[8,304,128]{2,1,0:T(8,128)(2,1)} collective-permute-done((bf16[8,304,128]{2,1,0:T(8,128)(2,1)S(1)}, bf16[8,304,128]{2,1,0:T(8,128)(2,1)}, u32[]{:S(2)}, u32[]{:S(2)}) %collective-permute-start.5) | collective-permute-done | bytes 622624 | tf_op jit(solution)/shard_map/ppermute | solution.py:103
  52.9 1.8 %collective-permute-done.6.refs_5_ = bf16[8,304,128]{2,1,0:T(8,128)(2,1)} collective-permute-done((bf16[8,304,128]{2,1,0:T(8,128)(2,1)S(1)}, bf16[8,304,128]{2,1,0:T(8,128)(2,1)}, u32[]{:S(2)}, u32[]{:S(2)}) %collective-permute-start.6) | collective-permute-done | bytes 622624 | tf_op jit(solution)/shard_map/ppermute | solution.py:103
  54.7 11.8 %logits.1 = (f32[256,1280]{1,0:T(8,128)S(1)}, f32[256,1280]{1,0:T(8,128)S(1)}, f32[64,8,128]{2,1,0:T(8,128)}, bf16[256,5120]{1,0:T(8,128)(2,1)}) custom-call(s32[4]{0:T(128)S(1)} %pad_add_fusion.place_ref, bf16[8,304,128]{2,1,0:T(8,128)(2,1)} %copy-done.4, bf16[8,304,128]{2,1,0:T(8,128)(2,1)} %copy-done.2, bf16[8,304,128]{2,1,0:T(8,128)(2,1)} %copy-done.1, ...), custom_call_target="tpu_custom_call" | custom-call | flops 6039797760 | bytes 8388608 | tf_op jit(solution)/shard_map/logits/pallas_call | solution.py:367
  66.5 4.6 %all-to-all-start.1 = ((f32[64,8,128]{2,1,0:T(8,128)}), f32[64,8,128]{2,1,0:T(8,128)S(1)}, u32[]{:S(2)}, u32[]{:S(2)}) async-start(f32[64,8,128]{2,1,0:T(8,128)} %get-tuple-element.25), calls=%async_computation.1 | async-start | bytes 524288 | tf_op jit(solution)/shard_map/all_to_all | solution.py:490
  71.1 3.4 %collective-permute-start.11 = (bf16[256,5120]{1,0:T(8,128)(2,1)}, bf16[256,5120]{1,0:T(8,128)(2,1)}, u32[]{:S(2)}, u32[]{:S(2)}) collective-permute-start(bf16[256,5120]{1,0:T(8,128)(2,1)} %get-tuple-element.29.own_ref), channel_id=1, source_target_pairs={{0,1},{1,0},{2,3},{3,2},{4,5},{5,4},{6,7},{7,6},{8,9},{9,8},{10,11... | collective-permute-start | bytes 7864328 | tf_op jit(solution)/shard_map/ppermute | solution.py:91
  74.5 5.9 %all-to-all-done.1.stats_ref = f32[64,8,128]{2,1,0:T(8,128)S(1)} async-done(((f32[64,8,128]{2,1,0:T(8,128)}), f32[64,8,128]{2,1,0:T(8,128)S(1)}, u32[]{:S(2)}, u32[]{:S(2)}) %all-to-all-start.1) | async-done | bytes 262176 | tf_op jit(solution)/shard_map/all_to_all | solution.py:490
  80.4 9.5 %hidden_gradient.1 = (bf16[8,8,32,640]{3,2,1,0:T(8,128)(2,1)}, bf16[256,1280]{1,0:T(8,128)(2,1)}, f32[8,256]{1,0:T(8,128)}) custom-call(s32[4]{0:T(128)} %copy-done.3, s32[8]{0:T(128)} %lengths_ref.1, f32[64,8,128]{2,1,0:T(8,128)S(1)} %all-to-all-done.1.stats_ref, f32[256,1280]{1,0:T(8,128)S(1)} %get-tuple-element.26.teacher, ...), custom_call_target="tpu_custom_call" | custom-call | flops 3355443200 | bytes 13107200 | tf_op jit(solution)/shard_map/hidden_gradient/pallas_call | solution.py:396
  89.9 4.9 %all-to-all-start.2 = ((bf16[64,32,640]{2,1,0:T(8,128)(2,1)}), bf16[64,32,640]{2,1,0:T(8,128)(2,1)S(1)}, u32[]{:S(2)}, u32[]{:S(2)}) async-start(bf16[64,32,640]{2,1,0:T(8,128)(2,1)} %bitcast.28), calls=%async_computation.2 | async-start | bytes 5242880 | tf_op jit(solution)/shard_map/all_to_all | solution.py:496
  94.9 4.6 %collective-permute-start.12 = (bf16[256,640]{1,0:T(8,128)(2,1)S(1)}, bf16[256,640]{1,0:T(8,128)(2,1)S(1)}, u32[]{:S(2)}, u32[]{:S(2)}) collective-permute-start(bf16[256,640]{1,0:T(8,128)(2,1)S(1)} %slice.65), channel_id=1, source_target_pairs={{0,1},{1,0},{2,3},{3,2},{4,5},{5,4},{6,7},{7,6},{8,9},{9,8},{10,11... | collective-permute-start | bytes 983048 | tf_op jit(solution)/shard_map/ppermute | solution.py:91
  99.5 0.8 constant_dynamic-slice_fusion
  100.3 1.1 collective-permute-done.14
  101.4 0.8 dynamic-slice_select_fusion
  102.2 0.7 copy-done.7
  102.9 10.0 %head_gradient.1 = bf16[5120,640]{1,0:T(8,128)(2,1)} custom-call(bf16[256,5120]{1,0:T(8,128)(2,1)} %get-tuple-element.29.own_ref, bf16[256,5120]{1,0:T(8,128)(2,1)} %collective-permute-done.11.other_ref, bf16[256,1280]{1,0:T(8,128)(2,1)} %get-tuple-element.30.mine_ref, bf16[256,640]{1,0:T(8,128)(2,1)} %copy-done.7), custom_call_target="tpu_custom_call" | custom-call | flops 3355443200 | bytes 16777216 | tf_op jit(solution)/shard_map/head_gradient/pallas_call | solution.py:424
  113.0 12.2 %all-to-all-done.2 = bf16[64,32,640]{2,1,0:T(8,128)(2,1)S(1)} async-done(((bf16[64,32,640]{2,1,0:T(8,128)(2,1)}), bf16[64,32,640]{2,1,0:T(8,128)(2,1)S(1)}, u32[]{:S(2)}, u32[]{:S(2)}) %all-to-all-start.2) | async-done | bytes 2621472 | tf_op jit(solution)/shard_map/all_to_all | solution.py:496
  125.1 0.4 reduce_sum.12
  125.6 4.9 %collective-permute-start.13 = (bf16[32,320]{1,0:T(8,128)(2,1)S(1)}, bf16[32,320]{1,0:T(8,128)(2,1)S(1)}, u32[]{:S(2)}, u32[]{:S(2)}) collective-permute-start(bf16[32,320]{1,0:T(8,128)(2,1)S(1)} %broadcast_select_fusion.2), channel_id=1, source_target_pairs={{0,1},{1,0},{2,3},{3,2},{4,5},{5,4},{6,7},{7,6},{8,9},{9,8},{10,11... | collective-permute-start | bytes 61448 | tf_op jit(solution)/shard_map/ppermute | solution.py:91
  130.4 0.5 slice_bitcast_fusion
  131.0 0.3 collective-permute-done.13
  131.4 0.6 pad_maximum_fusion.1
  (44 shorter events, 1.0 us)
Async XLA Ops:
  0.6 2.9 %collective-permute-start.1 = (bf16[64,320]{1,0:T(8,128)(2,1)}, bf16[64,320]{1,0:T(8,128)(2,1)S(1)}, u32[]{:S(2)}, u32[]{:S(2)}) collective-permute-start(bf16[64,320]{1,0:T(8,128)(2,1)} %param.7), channel_id=1, source_target_pairs={{0,1},{1,0},{2,3},{3,2},{4,5},{5,4},{6,7},{7,6},{8,9},{9,8},{10,11... | collective-permute-start | bytes 122888 | tf_op jit(solution)/shard_map/ppermute | solution.py:91
  2.1 1.4 %collective-permute-start = (bf16[64,256]{1,0:T(8,128)(2,1)}, bf16[64,256]{1,0:T(8,128)(2,1)S(1)}, u32[]{:S(2)}, u32[]{:S(2)}) collective-permute-start(bf16[64,256]{1,0:T(8,128)(2,1)} %param.6), channel_id=1, source_target_pairs={{0,1},{1,0},{2,3},{3,2},{4,5},{5,4},{6,7},{7,6},{8,9},{9,8},{10,11... | collective-permute-start | bytes 98312 | tf_op jit(solution)/shard_map/ppermute | solution.py:91
  3.6 37.0 %collective-permute-start.10 = (bf16[5120,640]{1,0:T(8,128)(2,1)}, bf16[5120,640]{1,0:T(8,128)(2,1)}, u32[]{:S(2)}, u32[]{:S(2)}) collective-permute-start(bf16[5120,640]{1,0:T(8,128)(2,1)} %own_s.3), channel_id=1, source_target_pairs={{0,1},{1,0},{2,3},{3,2},{4,5},{5,4},{6,7},{7,6},{8,9},{9,8},{10,11... | collective-permute-start | bytes 19660808 | tf_op jit(solution)/shard_map/ppermute | solution.py:91
  3.7 35.6 %collective-permute-start.9 = (bf16[4096,640]{1,0:T(8,128)(2,1)}, bf16[4096,640]{1,0:T(8,128)(2,1)}, u32[]{:S(2)}, u32[]{:S(2)}) collective-permute-start(bf16[4096,640]{1,0:T(8,128)(2,1)} %own_t.1), channel_id=1, source_target_pairs={{0,1},{1,0},{2,3},{3,2},{4,5},{5,4},{6,7},{7,6},{8,9},{9,8},{10,11... | collective-permute-start | bytes 15728648 | tf_op jit(solution)/shard_map/ppermute | solution.py:91
  27.6 20.9 %copy-start.4 = (bf16[8,304,128]{2,1,0:T(8,128)(2,1)}, bf16[8,304,128]{2,1,0:T(8,128)(2,1)S(1)}, u32[]{:S(2)}) copy-start(bf16[8,304,128]{2,1,0:T(8,128)(2,1)S(1)} %all_to_all.15.refs_0_) | copy-start | bytes 1867780
  27.6 9.1 %collective-permute-start.4 = (bf16[8,304,128]{2,1,0:T(8,128)(2,1)S(1)}, bf16[8,304,128]{2,1,0:T(8,128)(2,1)S(1)}, u32[]{:S(2)}, u32[]{:S(2)}) collective-permute-start(bf16[8,304,128]{2,1,0:T(8,128)(2,1)S(1)} %all_to_all.15.refs_0_), channel_id=1, source_target_pairs={{0,48},{1,17},{16,32},{17,1},{32,16},{33,49},{48,0},{49,33},{2,50}... | collective-permute-start | bytes 1867784 | tf_op jit(solution)/shard_map/ppermute | solution.py:103
  27.6 9.1 %collective-permute-start.3 = (bf16[8,304,128]{2,1,0:T(8,128)(2,1)S(1)}, bf16[8,304,128]{2,1,0:T(8,128)(2,1)S(1)}, u32[]{:S(2)}, u32[]{:S(2)}) collective-permute-start(bf16[8,304,128]{2,1,0:T(8,128)(2,1)S(1)} %all_to_all.15.refs_0_), channel_id=1, source_target_pairs={{0,6},{1,3},{16,22},{17,19},{32,38},{33,35},{48,54},{49,51},{2,4},... | collective-permute-start | bytes 1867784 | tf_op jit(solution)/shard_map/ppermute | solution.py:103
  27.6 9.3 %collective-permute-start.2 = (bf16[8,304,128]{2,1,0:T(8,128)(2,1)S(1)}, bf16[8,304,128]{2,1,0:T(8,128)(2,1)S(1)}, u32[]{:S(2)}, u32[]{:S(2)}) collective-permute-start(bf16[8,304,128]{2,1,0:T(8,128)(2,1)S(1)} %all_to_all.15.refs_0_), channel_id=1, source_target_pairs={{0,72},{1,65},{16,88},{17,81},{32,104},{33,97},{48,120},{49,113},{... | collective-permute-start | bytes 1867784 | tf_op jit(solution)/shard_map/ppermute | solution.py:103
  36.6 11.9 %copy-start = (bf16[8,304,128]{2,1,0:T(8,128)(2,1)}, bf16[8,304,128]{2,1,0:T(8,128)(2,1)S(1)}, u32[]{:S(2)}) copy-start(bf16[8,304,128]{2,1,0:T(8,128)(2,1)S(1)} %collective-permute-done.4.third.refs_3_) | copy-start | bytes 1867780
  36.6 11.9 %collective-permute-start.8 = (bf16[8,304,128]{2,1,0:T(8,128)(2,1)S(1)}, bf16[8,304,128]{2,1,0:T(8,128)(2,1)S(1)}, u32[]{:S(2)}, u32[]{:S(2)}) collective-permute-start(bf16[8,304,128]{2,1,0:T(8,128)(2,1)S(1)} %all_to_all.15.refs_0_), channel_id=1, source_target_pairs={{0,126},{1,83},{16,110},{17,67},{32,94},{33,115},{48,78},{49,99},{... | collective-permute-start | bytes 1867784 | tf_op jit(solution)/shard_map/ppermute | solution.py:103
  36.7 11.9 %copy-start.1 = (bf16[8,304,128]{2,1,0:T(8,128)(2,1)}, bf16[8,304,128]{2,1,0:T(8,128)(2,1)S(1)}, u32[]{:S(2)}) copy-start(bf16[8,304,128]{2,1,0:T(8,128)(2,1)S(1)} %collective-permute-done.3.second.refs_2_) | copy-start | bytes 1867780
  36.7 16.2 %collective-permute-start.5 = (bf16[8,304,128]{2,1,0:T(8,128)(2,1)S(1)}, bf16[8,304,128]{2,1,0:T(8,128)(2,1)}, u32[]{:S(2)}, u32[]{:S(2)}) collective-permute-start(bf16[8,304,128]{2,1,0:T(8,128)(2,1)S(1)} %collective-permute-done.4.third.refs_3_), channel_id=1, source_target_pairs={{0,6},{1,3},{16,22},{17,19},{32,38},{33,35},{48,54},{49,51},{2,4},... | collective-permute-start | bytes 1867784 | tf_op jit(solution)/shard_map/ppermute | solution.py:103
  36.9 11.7 %copy-start.2 = (bf16[8,304,128]{2,1,0:T(8,128)(2,1)}, bf16[8,304,128]{2,1,0:T(8,128)(2,1)S(1)}, u32[]{:S(2)}) copy-start(bf16[8,304,128]{2,1,0:T(8,128)(2,1)S(1)} %collective-permute-done.2.first.refs_1_) | copy-start | bytes 1867780
  36.9 16.0 %collective-permute-start.7 = (bf16[8,304,128]{2,1,0:T(8,128)(2,1)S(1)}, bf16[8,304,128]{2,1,0:T(8,128)(2,1)}, u32[]{:S(2)}, u32[]{:S(2)}) collective-permute-start(bf16[8,304,128]{2,1,0:T(8,128)(2,1)S(1)} %collective-permute-done.3.second.refs_2_), channel_id=1, source_target_pairs={{0,72},{1,65},{16,88},{17,81},{32,104},{33,97},{48,120},{49,113},{... | collective-permute-start | bytes 1867784 | tf_op jit(solution)/shard_map/ppermute | solution.py:103
  39.3 15.4 %collective-permute-start.6 = (bf16[8,304,128]{2,1,0:T(8,128)(2,1)S(1)}, bf16[8,304,128]{2,1,0:T(8,128)(2,1)}, u32[]{:S(2)}, u32[]{:S(2)}) collective-permute-start(bf16[8,304,128]{2,1,0:T(8,128)(2,1)S(1)} %collective-permute-done.2.first.refs_1_), channel_id=1, source_target_pairs={{0,48},{1,17},{16,32},{17,1},{32,16},{33,49},{48,0},{49,33},{2,50}... | collective-permute-start | bytes 1867784 | tf_op jit(solution)/shard_map/ppermute | solution.py:103
  40.6 14.1 %copy-start.3 = (s32[4]{0:T(128)}, s32[4]{0:T(128)S(1)}, u32[]{:S(2)}) copy-start(s32[4]{0:T(128)S(1)} %pad_add_fusion.place_ref) | copy-start | bytes 52
  48.5 6.2 %copy-start.6 = (bf16[8,304,128]{2,1,0:T(8,128)(2,1)}, bf16[8,304,128]{2,1,0:T(8,128)(2,1)S(1)}, u32[]{:S(2)}) copy-start(bf16[8,304,128]{2,1,0:T(8,128)(2,1)S(1)} %collective-permute-done.8.refs_7_) | copy-start | bytes 1867780
  66.5 13.9 %all-to-all-start.1 = ((f32[64,8,128]{2,1,0:T(8,128)}), f32[64,8,128]{2,1,0:T(8,128)S(1)}, u32[]{:S(2)}, u32[]{:S(2)}) async-start(f32[64,8,128]{2,1,0:T(8,128)} %get-tuple-element.25), calls=%async_computation.1 | async-start | bytes 524288 | tf_op jit(solution)/shard_map/all_to_all | solution.py:490
  71.1 31.0 %collective-permute-start.11 = (bf16[256,5120]{1,0:T(8,128)(2,1)}, bf16[256,5120]{1,0:T(8,128)(2,1)}, u32[]{:S(2)}, u32[]{:S(2)}) collective-permute-start(bf16[256,5120]{1,0:T(8,128)(2,1)} %get-tuple-element.29.own_ref), channel_id=1, source_target_pairs={{0,1},{1,0},{2,3},{3,2},{4,5},{5,4},{6,7},{7,6},{8,9},{9,8},{10,11... | collective-permute-start | bytes 7864328 | tf_op jit(solution)/shard_map/ppermute | solution.py:91
  89.9 4.9 %copy-start.5 = (bf16[256,1280]{1,0:T(8,128)(2,1)S(1)}, bf16[256,1280]{1,0:T(8,128)(2,1)}, u32[]{:S(2)}) copy-start(bf16[256,1280]{1,0:T(8,128)(2,1)} %get-tuple-element.30.mine_ref) | copy-start | bytes 1966084
  89.9 35.2 %all-to-all-start.2 = ((bf16[64,32,640]{2,1,0:T(8,128)(2,1)}), bf16[64,32,640]{2,1,0:T(8,128)(2,1)S(1)}, u32[]{:S(2)}, u32[]{:S(2)}) async-start(bf16[64,32,640]{2,1,0:T(8,128)(2,1)} %bitcast.28), calls=%async_computation.2 | async-start | bytes 5242880 | tf_op jit(solution)/shard_map/all_to_all | solution.py:496
  94.9 7.3 %collective-permute-start.12 = (bf16[256,640]{1,0:T(8,128)(2,1)S(1)}, bf16[256,640]{1,0:T(8,128)(2,1)S(1)}, u32[]{:S(2)}, u32[]{:S(2)}) collective-permute-start(bf16[256,640]{1,0:T(8,128)(2,1)S(1)} %slice.65), channel_id=1, source_target_pairs={{0,1},{1,0},{2,3},{3,2},{4,5},{5,4},{6,7},{7,6},{8,9},{9,8},{10,11... | collective-permute-start | bytes 983048 | tf_op jit(solution)/shard_map/ppermute | solution.py:91
  100.3 1.1 collective-permute-start.14
  102.2 0.7 copy-start.7
  125.6 5.7 %collective-permute-start.13 = (bf16[32,320]{1,0:T(8,128)(2,1)S(1)}, bf16[32,320]{1,0:T(8,128)(2,1)S(1)}, u32[]{:S(2)}, u32[]{:S(2)}) collective-permute-start(bf16[32,320]{1,0:T(8,128)(2,1)S(1)} %broadcast_select_fusion.2), channel_id=1, source_target_pairs={{0,1},{1,0},{2,3},{3,2},{4,5},{5,4},{6,7},{7,6},{8,9},{9,8},{10,11... | collective-permute-start | bytes 61448 | tf_op jit(solution)/shard_map/ppermute | solution.py:91

commit v3 on v2

--- a/solution.py
+++ b/solution.py
@@ -444,11 +444,8 @@
     strips_t, strips_s = part_t // LANES, part_s // LANES
 
     got_t, got_s = swap(teacher_hidden), swap(student_hidden)
-    teacher_late, student_late, got_t, got_s = lax.optimization_barrier(
-        (teacher_head, student_head, got_t, got_s)
-    )
+    teacher_late, got_t, got_s = lax.optimization_barrier((teacher_head, got_t, got_s))
     other_teacher_head = swap(teacher_late)
-    other_student_head = swap(student_late)
 
     def half(value):
         value = value.reshape(2, HALF, -1)
@@ -474,6 +471,8 @@
         ]
     )
     near = to_all(block, FIRST)
+    near, other_teacher_head, student_late = lax.optimization_barrier((near, other_teacher_head, student_head))
+    other_student_head = swap(student_late)
     units = second_gather(near)
     heads_t, heads_s = prefetch(
         teacher_head, other_teacher_head, student_head, other_student_head, units[1:4]

time: 133 us -> 133 us (level)
  waiting for transfers between devices: 36 us -> 28 us
  starting transfers between devices: 28.4 us -> 36.3 us
    ppermute x8, starting transfers between devices: 15 us -> 19.8 us  [swap(): return lax.ppermute(value, BOTH, SWAP)]
    ppermute x7, waiting for transfers between devices: 15.1 us -> 11.9 us  [along(): return lax.ppermute(value, BOTH, links(axes))]
    all_to_all x1, waiting for transfers between devices: 5.9 us -> 3.52 us  [per_device(): all_stats = lax.all_to_all(stats, BOTH, 0, 0, axis_index_groups=SAME_CORE)]
    all_to_all x1, waiting for transfers between devices: 12.2 us -> 9.79 us  [per_device(): lax.all_to_all(part.reshape(64, HALF, part_s), BOTH, 0, 0, axis_index_gro...]
    all_to_all x1, starting transfers between devices: 4.88 us -> 6.55 us  [per_device(): lax.all_to_all(part.reshape(64, HALF, part_s), BOTH, 0, 0, axis_index_gro...]
    ppermute x7, starting transfers between devices: 3.91 us -> 5.28 us  [along(): return lax.ppermute(value, BOTH, links(axes))]
  transfers between devices with their start and end apart: 17 -> 17, of which waited for: 8 -> 10; matrix products, arithmetic and copies ran while one was open for 4% -> 4% of each run, Pallas kernels for 21% -> 21%
where the time goes in v3:
time: 133 us; the launch traced here: 132 us
  Pallas kernels  39.2 us (29%)
  starting transfers between devices  36.3 us (27%)
  waiting for transfers between devices  28 us (21%)
  blocking collectives  20.8 us (16%)
  other arithmetic  4.47 us (3%)
  local copies, waits for them, and re-layouts  2.24 us (2%)
    all_to_all x1, blocking collectives, to_all(): lax.all_to_all(jnp.broadcast_to(block, (size,) + block.shape), BOTH, 0, 0...  20.8 us
    ppermute x8, starting transfers between devices, swap(): return lax.ppermute(value, BOTH, SWAP)  19.8 us
    ppermute x7, waiting for transfers between devices, along(): return lax.ppermute(value, BOTH, links(axes))  11.9 us
    pallas_call x1, Pallas kernels, logits_of(): pl.pallas_call(logits_kernel, name='logits', in_specs=[SMEM] + [HBM] * 8...  11.8 us
    pallas_call x1, Pallas kernels, head_gradient_of(): pl.pallas_call(head_kernel, name='head_gradient', grid=(8,), in_specs=[st...  10 us
    all_to_all x1, waiting for transfers between devices, per_device(): lax.all_to_all(part.reshape(64, HALF, part_s), BOTH, 0, 0, axis_index_gro...  9.79 us
    pallas_call x1, Pallas kernels, gradient_of(): pl.pallas_call(gradient_kernel, name='hidden_gradient', in_specs=[SMEM] *...  9.48 us
    pallas_call x1, Pallas kernels, prefetch(): pl.pallas_call(prefetch_kernel, name='prefetch_heads', in_specs=[HBM] * 4...  7.91 us
  transfers between devices with their start and end apart: 17, of which 10 were waited for; matrix products, arithmetic and copies ran while one was open for 4% of the time, Pallas kernels for 21%

profile of v3, /device:TPU:1, one launch (start us, length us, event | category | flops | bytes accessed | tf_op | source)
XLA Modules:
  0.0 131.9 jit_solution(6623629911101292566)
XLA Ops:
  0.6 1.5 %collective-permute-start.1 = (bf16[64,320]{1,0:T(8,128)(2,1)}, bf16[64,320]{1,0:T(8,128)(2,1)S(1)}, u32[]{:S(2)}, u32[]{:S(2)}) collective-permute-start(bf16[64,320]{1,0:T(8,128)(2,1)} %param.7), channel_id=1, source_target_pairs={{0,1},{1,0},{2,3},{3,2},{4,5},{5,4},{6,7},{7,6},{8,9},{9,8},{10,11... | collective-permute-start | bytes 122888 | tf_op jit(solution)/shard_map/ppermute | solution.py:91
  2.1 0.1 collective-permute-start
  2.2 1.3 %collective-permute-done = bf16[64,256]{1,0:T(8,128)(2,1)S(1)} collective-permute-done((bf16[64,256]{1,0:T(8,128)(2,1)}, bf16[64,256]{1,0:T(8,128)(2,1)S(1)}, u32[]{:S(2)}, u32[]{:S(2)}) %collective-permute-start) | collective-permute-done | bytes 32800 | tf_op jit(solution)/shard_map/ppermute | solution.py:91
  3.6 0.2 collective-permute-start.2
  3.7 0.8 convert_bitcast_fusion
  4.6 0.8 broadcast_select_fusion.5
  5.5 0.7 select_bitcast_fusion.1
  6.4 20.8 %all_to_all.15.refs_0_ = bf16[8,304,128]{2,1,0:T(8,128)(2,1)S(1)} all-to-all(bf16[8,304,128]{2,1,0:T(8,128)(2,1)S(1)} %broadcast_in_dim.3), channel_id=1, replica_groups={{0,16,2,18,64,80,66,82},{32,48,34,50,96,112,98,114},{4,20,6,22,68,84,70..., dimensions={0} | all-to-all | bytes 1245184 | tf_op jit(solution)/shard_map/all_to_all | solution.py:96
  27.5 3.6 %collective-permute-start.9 = (bf16[8,304,128]{2,1,0:T(8,128)(2,1)S(1)}, bf16[8,304,128]{2,1,0:T(8,128)(2,1)S(1)}, u32[]{:S(2)}, u32[]{:S(2)}) collective-permute-start(bf16[8,304,128]{2,1,0:T(8,128)(2,1)S(1)} %all_to_all.15.refs_0_), channel_id=1, source_target_pairs={{0,126},{1,83},{16,110},{17,67},{32,94},{33,115},{48,78},{49,99},{... | collective-permute-start | bytes 1867784 | tf_op jit(solution)/shard_map/ppermute | solution.py:103
  31.1 5.5 %collective-permute-done.5.third.refs_3_ = bf16[8,304,128]{2,1,0:T(8,128)(2,1)S(1)} collective-permute-done((bf16[8,304,128]{2,1,0:T(8,128)(2,1)S(1)}, bf16[8,304,128]{2,1,0:T(8,128)(2,1)S(1)}, u32[]{:S(2)}, u32[]{:S(2)}) %collective-permute-start.5) | collective-permute-done | bytes 622624 | tf_op jit(solution)/shard_map/ppermute | solution.py:103
  36.9 1.4 %collective-permute-start.7 = (bf16[8,304,128]{2,1,0:T(8,128)(2,1)S(1)}, bf16[8,304,128]{2,1,0:T(8,128)(2,1)}, u32[]{:S(2)}, u32[]{:S(2)}) collective-permute-start(bf16[8,304,128]{2,1,0:T(8,128)(2,1)S(1)} %collective-permute-done.3.first.refs_1_), channel_id=1, source_target_pairs={{0,48},{1,17},{16,32},{17,1},{32,16},{33,49},{48,0},{49,33},{2,50}... | collective-permute-start | bytes 1867784 | tf_op jit(solution)/shard_map/ppermute | solution.py:103
  38.3 7.9 %prefetch_heads.1 = (bf16[4096,1280]{1,0:T(8,128)(2,1)S(1)}, bf16[5120,1280]{1,0:T(8,128)(2,1)S(1)}) custom-call(bf16[4096,640]{1,0:T(8,128)(2,1)} %own_t.1, bf16[4096,640]{1,0:T(8,128)(2,1)} %collective-permute-done.2.other_t, bf16[5120,640]{1,0:T(8,128)(2,1)} %own_s.3, bf16[5120,640]{1,0:T(8,128)(2,1)} %collective-permute-done.10.other_s, ...), custom_call_target="tpu_custom_call" | custom-call | bytes 47185920 | tf_op jit(solution)/shard_map/prefetch_heads/pallas_call | solution.py:351
  46.3 5.1 %collective-permute-done.6.refs_4_ = bf16[8,304,128]{2,1,0:T(8,128)(2,1)} collective-permute-done((bf16[8,304,128]{2,1,0:T(8,128)(2,1)S(1)}, bf16[8,304,128]{2,1,0:T(8,128)(2,1)}, u32[]{:S(2)}, u32[]{:S(2)}) %collective-permute-start.6) | collective-permute-done | bytes 622624 | tf_op jit(solution)/shard_map/ppermute | solution.py:103
  51.4 1.1 collective-permute-done.7.refs_5_
  52.5 11.8 %logits.1 = (f32[256,1280]{1,0:T(8,128)S(1)}, f32[256,1280]{1,0:T(8,128)S(1)}, f32[64,8,128]{2,1,0:T(8,128)}, bf16[256,5120]{1,0:T(8,128)(2,1)}) custom-call(s32[4]{0:T(128)S(1)} %pad_add_fusion.place_ref, bf16[8,304,128]{2,1,0:T(8,128)(2,1)} %copy-done.4, bf16[8,304,128]{2,1,0:T(8,128)(2,1)} %copy-done.2, bf16[8,304,128]{2,1,0:T(8,128)(2,1)} %copy-done.1, ...), custom_call_target="tpu_custom_call" | custom-call | flops 6039797760 | bytes 8388608 | tf_op jit(solution)/shard_map/logits/pallas_call | solution.py:367
  64.3 4.6 %all-to-all-start.1 = ((f32[64,8,128]{2,1,0:T(8,128)}), f32[64,8,128]{2,1,0:T(8,128)S(1)}, u32[]{:S(2)}, u32[]{:S(2)}) async-start(f32[64,8,128]{2,1,0:T(8,128)} %get-tuple-element.29), calls=%async_computation.1 | async-start | bytes 524288 | tf_op jit(solution)/shard_map/all_to_all | solution.py:489
  68.9 5.8 %collective-permute-start.11 = (bf16[256,5120]{1,0:T(8,128)(2,1)}, bf16[256,5120]{1,0:T(8,128)(2,1)}, u32[]{:S(2)}, u32[]{:S(2)}) collective-permute-start(bf16[256,5120]{1,0:T(8,128)(2,1)} %get-tuple-element.33.own_ref), channel_id=1, source_target_pairs={{0,1},{1,0},{2,3},{3,2},{4,5},{5,4},{6,7},{7,6},{8,9},{9,8},{10,11... | collective-permute-start | bytes 7864328 | tf_op jit(solution)/shard_map/ppermute | solution.py:91
  74.7 3.5 %all-to-all-done.1.stats_ref = f32[64,8,128]{2,1,0:T(8,128)S(1)} async-done(((f32[64,8,128]{2,1,0:T(8,128)}), f32[64,8,128]{2,1,0:T(8,128)S(1)}, u32[]{:S(2)}, u32[]{:S(2)}) %all-to-all-start.1) | async-done | bytes 262176 | tf_op jit(solution)/shard_map/all_to_all | solution.py:489
  78.2 9.5 %hidden_gradient.1 = (bf16[8,8,32,640]{3,2,1,0:T(8,128)(2,1)}, bf16[256,1280]{1,0:T(8,128)(2,1)}, f32[8,256]{1,0:T(8,128)}) custom-call(s32[4]{0:T(128)} %copy-done.3, s32[8]{0:T(128)} %lengths_ref.1, f32[64,8,128]{2,1,0:T(8,128)S(1)} %all-to-all-done.1.stats_ref, f32[256,1280]{1,0:T(8,128)S(1)} %get-tuple-element.30.teacher, ...), custom_call_target="tpu_custom_call" | custom-call | flops 3355443200 | bytes 13107200 | tf_op jit(solution)/shard_map/hidden_gradient/pallas_call | solution.py:396
  87.7 6.5 %all-to-all-start.2 = ((bf16[64,32,640]{2,1,0:T(8,128)(2,1)}), bf16[64,32,640]{2,1,0:T(8,128)(2,1)S(1)}, u32[]{:S(2)}, u32[]{:S(2)}) async-start(bf16[64,32,640]{2,1,0:T(8,128)(2,1)} %bitcast.28), calls=%async_computation.2 | async-start | bytes 5242880 | tf_op jit(solution)/shard_map/all_to_all | solution.py:495
  94.4 5.3 %collective-permute-start.12 = (bf16[256,640]{1,0:T(8,128)(2,1)S(1)}, bf16[256,640]{1,0:T(8,128)(2,1)S(1)}, u32[]{:S(2)}, u32[]{:S(2)}) collective-permute-start(bf16[256,640]{1,0:T(8,128)(2,1)S(1)} %slice.65), channel_id=1, source_target_pairs={{0,1},{1,0},{2,3},{3,2},{4,5},{5,4},{6,7},{7,6},{8,9},{9,8},{10,11... | collective-permute-start | bytes 983048 | tf_op jit(solution)/shard_map/ppermute | solution.py:91
  99.7 0.8 constant_dynamic-slice_fusion
  100.5 1.1 collective-permute-done.14
  101.6 0.8 dynamic-slice_select_fusion
  102.4 0.7 copy-done.7
  103.1 10.0 %head_gradient.1 = bf16[5120,640]{1,0:T(8,128)(2,1)} custom-call(bf16[256,5120]{1,0:T(8,128)(2,1)} %get-tuple-element.33.own_ref, bf16[256,5120]{1,0:T(8,128)(2,1)} %collective-permute-done.11.other_ref, bf16[256,1280]{1,0:T(8,128)(2,1)} %get-tuple-element.34.mine_ref, bf16[256,640]{1,0:T(8,128)(2,1)} %copy-done.7), custom_call_target="tpu_custom_call" | custom-call | flops 3355443200 | bytes 16777216 | tf_op jit(solution)/shard_map/head_gradient/pallas_call | solution.py:424
  113.2 9.8 %all-to-all-done.2 = bf16[64,32,640]{2,1,0:T(8,128)(2,1)S(1)} async-done(((bf16[64,32,640]{2,1,0:T(8,128)(2,1)}), bf16[64,32,640]{2,1,0:T(8,128)(2,1)S(1)}, u32[]{:S(2)}, u32[]{:S(2)}) %all-to-all-start.2) | async-done | bytes 2621472 | tf_op jit(solution)/shard_map/all_to_all | solution.py:495
  122.9 0.4 reduce_sum.12
  123.4 7.0 %collective-permute-start.13 = (bf16[32,320]{1,0:T(8,128)(2,1)S(1)}, bf16[32,320]{1,0:T(8,128)(2,1)S(1)}, u32[]{:S(2)}, u32[]{:S(2)}) collective-permute-start(bf16[32,320]{1,0:T(8,128)(2,1)S(1)} %broadcast_select_fusion.2), channel_id=1, source_target_pairs={{0,1},{1,0},{2,3},{3,2},{4,5},{5,4},{6,7},{7,6},{8,9},{9,8},{10,11... | collective-permute-start | bytes 61448 | tf_op jit(solution)/shard_map/ppermute | solution.py:91
  130.4 0.5 slice_bitcast_fusion
  130.9 0.3 collective-permute-done.13
  131.3 0.6 pad_maximum_fusion.1
  (44 shorter events, 1.1 us)
Async XLA Ops:
  0.6 2.9 %collective-permute-start.1 = (bf16[64,320]{1,0:T(8,128)(2,1)}, bf16[64,320]{1,0:T(8,128)(2,1)S(1)}, u32[]{:S(2)}, u32[]{:S(2)}) collective-permute-start(bf16[64,320]{1,0:T(8,128)(2,1)} %param.7), channel_id=1, source_target_pairs={{0,1},{1,0},{2,3},{3,2},{4,5},{5,4},{6,7},{7,6},{8,9},{9,8},{10,11... | collective-permute-start | bytes 122888 | tf_op jit(solution)/shard_map/ppermute | solution.py:91
  2.1 1.4 %collective-permute-start = (bf16[64,256]{1,0:T(8,128)(2,1)}, bf16[64,256]{1,0:T(8,128)(2,1)S(1)}, u32[]{:S(2)}, u32[]{:S(2)}) collective-permute-start(bf16[64,256]{1,0:T(8,128)(2,1)} %param.6), channel_id=1, source_target_pairs={{0,1},{1,0},{2,3},{3,2},{4,5},{5,4},{6,7},{7,6},{8,9},{9,8},{10,11... | collective-permute-start | bytes 98312 | tf_op jit(solution)/shard_map/ppermute | solution.py:91
  3.6 23.6 %collective-permute-start.2 = (bf16[4096,640]{1,0:T(8,128)(2,1)}, bf16[4096,640]{1,0:T(8,128)(2,1)}, u32[]{:S(2)}, u32[]{:S(2)}) collective-permute-start(bf16[4096,640]{1,0:T(8,128)(2,1)} %own_t.1), channel_id=1, source_target_pairs={{0,1},{1,0},{2,3},{3,2},{4,5},{5,4},{6,7},{7,6},{8,9},{9,8},{10,11... | collective-permute-start | bytes 15728648 | tf_op jit(solution)/shard_map/ppermute | solution.py:91
  27.2 19.0 %copy-start.4 = (bf16[8,304,128]{2,1,0:T(8,128)(2,1)}, bf16[8,304,128]{2,1,0:T(8,128)(2,1)S(1)}, u32[]{:S(2)}) copy-start(bf16[8,304,128]{2,1,0:T(8,128)(2,1)S(1)} %all_to_all.15.refs_0_) | copy-start | bytes 1867780
  27.2 11.1 %collective-permute-start.10 = (bf16[5120,640]{1,0:T(8,128)(2,1)}, bf16[5120,640]{1,0:T(8,128)(2,1)}, u32[]{:S(2)}, u32[]{:S(2)}) collective-permute-start(bf16[5120,640]{1,0:T(8,128)(2,1)} %own_s.3), channel_id=1, source_target_pairs={{0,1},{1,0},{2,3},{3,2},{4,5},{5,4},{6,7},{7,6},{8,9},{9,8},{10,11... | collective-permute-start | bytes 19660808 | tf_op jit(solution)/shard_map/ppermute | solution.py:91
  27.2 9.5 %collective-permute-start.5 = (bf16[8,304,128]{2,1,0:T(8,128)(2,1)S(1)}, bf16[8,304,128]{2,1,0:T(8,128)(2,1)S(1)}, u32[]{:S(2)}, u32[]{:S(2)}) collective-permute-start(bf16[8,304,128]{2,1,0:T(8,128)(2,1)S(1)} %all_to_all.15.refs_0_), channel_id=1, source_target_pairs={{0,48},{1,17},{16,32},{17,1},{32,16},{33,49},{48,0},{49,33},{2,50}... | collective-permute-start | bytes 1867784 | tf_op jit(solution)/shard_map/ppermute | solution.py:103
  27.3 9.5 %collective-permute-start.4 = (bf16[8,304,128]{2,1,0:T(8,128)(2,1)S(1)}, bf16[8,304,128]{2,1,0:T(8,128)(2,1)S(1)}, u32[]{:S(2)}, u32[]{:S(2)}) collective-permute-start(bf16[8,304,128]{2,1,0:T(8,128)(2,1)S(1)} %all_to_all.15.refs_0_), channel_id=1, source_target_pairs={{0,6},{1,3},{16,22},{17,19},{32,38},{33,35},{48,54},{49,51},{2,4},... | collective-permute-start | bytes 1867784 | tf_op jit(solution)/shard_map/ppermute | solution.py:103
  27.4 9.5 %collective-permute-start.3 = (bf16[8,304,128]{2,1,0:T(8,128)(2,1)S(1)}, bf16[8,304,128]{2,1,0:T(8,128)(2,1)S(1)}, u32[]{:S(2)}, u32[]{:S(2)}) collective-permute-start(bf16[8,304,128]{2,1,0:T(8,128)(2,1)S(1)} %all_to_all.15.refs_0_), channel_id=1, source_target_pairs={{0,72},{1,65},{16,88},{17,81},{32,104},{33,97},{48,120},{49,113},{... | collective-permute-start | bytes 1867784 | tf_op jit(solution)/shard_map/ppermute | solution.py:103
  27.5 18.8 %collective-permute-start.9 = (bf16[8,304,128]{2,1,0:T(8,128)(2,1)S(1)}, bf16[8,304,128]{2,1,0:T(8,128)(2,1)S(1)}, u32[]{:S(2)}, u32[]{:S(2)}) collective-permute-start(bf16[8,304,128]{2,1,0:T(8,128)(2,1)S(1)} %all_to_all.15.refs_0_), channel_id=1, source_target_pairs={{0,126},{1,83},{16,110},{17,67},{32,94},{33,115},{48,78},{49,99},{... | collective-permute-start | bytes 1867784 | tf_op jit(solution)/shard_map/ppermute | solution.py:103
  36.7 9.6 %copy-start = (bf16[8,304,128]{2,1,0:T(8,128)(2,1)}, bf16[8,304,128]{2,1,0:T(8,128)(2,1)S(1)}, u32[]{:S(2)}) copy-start(bf16[8,304,128]{2,1,0:T(8,128)(2,1)S(1)} %collective-permute-done.5.third.refs_3_) | copy-start | bytes 1867780
  36.7 14.7 %collective-permute-start.6 = (bf16[8,304,128]{2,1,0:T(8,128)(2,1)S(1)}, bf16[8,304,128]{2,1,0:T(8,128)(2,1)}, u32[]{:S(2)}, u32[]{:S(2)}) collective-permute-start(bf16[8,304,128]{2,1,0:T(8,128)(2,1)S(1)} %collective-permute-done.5.third.refs_3_), channel_id=1, source_target_pairs={{0,6},{1,3},{16,22},{17,19},{32,38},{33,35},{48,54},{49,51},{2,4},... | collective-permute-start | bytes 1867784 | tf_op jit(solution)/shard_map/ppermute | solution.py:103
  36.8 9.5 %copy-start.1 = (bf16[8,304,128]{2,1,0:T(8,128)(2,1)}, bf16[8,304,128]{2,1,0:T(8,128)(2,1)S(1)}, u32[]{:S(2)}) copy-start(bf16[8,304,128]{2,1,0:T(8,128)(2,1)S(1)} %collective-permute-done.4.second.refs_2_) | copy-start | bytes 1867780
  36.8 14.6 %collective-permute-start.8 = (bf16[8,304,128]{2,1,0:T(8,128)(2,1)S(1)}, bf16[8,304,128]{2,1,0:T(8,128)(2,1)}, u32[]{:S(2)}, u32[]{:S(2)}) collective-permute-start(bf16[8,304,128]{2,1,0:T(8,128)(2,1)S(1)} %collective-permute-done.4.second.refs_2_), channel_id=1, source_target_pairs={{0,72},{1,65},{16,88},{17,81},{32,104},{33,97},{48,120},{49,113},{... | collective-permute-start | bytes 1867784 | tf_op jit(solution)/shard_map/ppermute | solution.py:103
  36.9 9.4 %copy-start.2 = (bf16[8,304,128]{2,1,0:T(8,128)(2,1)}, bf16[8,304,128]{2,1,0:T(8,128)(2,1)S(1)}, u32[]{:S(2)}) copy-start(bf16[8,304,128]{2,1,0:T(8,128)(2,1)S(1)} %collective-permute-done.3.first.refs_1_) | copy-start | bytes 1867780
  36.9 15.7 %collective-permute-start.7 = (bf16[8,304,128]{2,1,0:T(8,128)(2,1)S(1)}, bf16[8,304,128]{2,1,0:T(8,128)(2,1)}, u32[]{:S(2)}, u32[]{:S(2)}) collective-permute-start(bf16[8,304,128]{2,1,0:T(8,128)(2,1)S(1)} %collective-permute-done.3.first.refs_1_), channel_id=1, source_target_pairs={{0,48},{1,17},{16,32},{17,1},{32,16},{33,49},{48,0},{49,33},{2,50}... | collective-permute-start | bytes 1867784 | tf_op jit(solution)/shard_map/ppermute | solution.py:103
  38.3 14.2 %copy-start.3 = (s32[4]{0:T(128)}, s32[4]{0:T(128)S(1)}, u32[]{:S(2)}) copy-start(s32[4]{0:T(128)S(1)} %pad_add_fusion.place_ref) | copy-start | bytes 52
  46.3 6.2 %copy-start.6 = (bf16[8,304,128]{2,1,0:T(8,128)(2,1)}, bf16[8,304,128]{2,1,0:T(8,128)(2,1)S(1)}, u32[]{:S(2)}) copy-start(bf16[8,304,128]{2,1,0:T(8,128)(2,1)S(1)} %collective-permute-done.9.refs_7_) | copy-start | bytes 1867780
  64.3 13.9 %all-to-all-start.1 = ((f32[64,8,128]{2,1,0:T(8,128)}), f32[64,8,128]{2,1,0:T(8,128)S(1)}, u32[]{:S(2)}, u32[]{:S(2)}) async-start(f32[64,8,128]{2,1,0:T(8,128)} %get-tuple-element.29), calls=%async_computation.1 | async-start | bytes 524288 | tf_op jit(solution)/shard_map/all_to_all | solution.py:489
  68.9 33.4 %collective-permute-start.11 = (bf16[256,5120]{1,0:T(8,128)(2,1)}, bf16[256,5120]{1,0:T(8,128)(2,1)}, u32[]{:S(2)}, u32[]{:S(2)}) collective-permute-start(bf16[256,5120]{1,0:T(8,128)(2,1)} %get-tuple-element.33.own_ref), channel_id=1, source_target_pairs={{0,1},{1,0},{2,3},{3,2},{4,5},{5,4},{6,7},{7,6},{8,9},{9,8},{10,11... | collective-permute-start | bytes 7864328 | tf_op jit(solution)/shard_map/ppermute | solution.py:91
  87.7 6.6 %copy-start.5 = (bf16[256,1280]{1,0:T(8,128)(2,1)S(1)}, bf16[256,1280]{1,0:T(8,128)(2,1)}, u32[]{:S(2)}) copy-start(bf16[256,1280]{1,0:T(8,128)(2,1)} %get-tuple-element.34.mine_ref) | copy-start | bytes 1966084
  87.7 35.2 %all-to-all-start.2 = ((bf16[64,32,640]{2,1,0:T(8,128)(2,1)}), bf16[64,32,640]{2,1,0:T(8,128)(2,1)S(1)}, u32[]{:S(2)}, u32[]{:S(2)}) async-start(bf16[64,32,640]{2,1,0:T(8,128)(2,1)} %bitcast.28), calls=%async_computation.2 | async-start | bytes 5242880 | tf_op jit(solution)/shard_map/all_to_all | solution.py:495
  94.4 8.0 %collective-permute-start.12 = (bf16[256,640]{1,0:T(8,128)(2,1)S(1)}, bf16[256,640]{1,0:T(8,128)(2,1)S(1)}, u32[]{:S(2)}, u32[]{:S(2)}) collective-permute-start(bf16[256,640]{1,0:T(8,128)(2,1)S(1)} %slice.65), channel_id=1, source_target_pairs={{0,1},{1,0},{2,3},{3,2},{4,5},{5,4},{6,7},{7,6},{8,9},{9,8},{10,11... | collective-permute-start | bytes 983048 | tf_op jit(solution)/shard_map/ppermute | solution.py:91
  100.5 1.1 collective-permute-start.14
  102.4 0.7 copy-start.7
  123.4 7.8 %collective-permute-start.13 = (bf16[32,320]{1,0:T(8,128)(2,1)S(1)}, bf16[32,320]{1,0:T(8,128)(2,1)S(1)}, u32[]{:S(2)}, u32[]{:S(2)}) collective-permute-start(bf16[32,320]{1,0:T(8,128)(2,1)S(1)} %broadcast_select_fusion.2), channel_id=1, source_target_pairs={{0,1},{1,0},{2,3},{3,2},{4,5},{5,4},{6,7},{7,6},{8,9},{9,8},{10,11... | collective-permute-start | bytes 61448 | tf_op jit(solution)/shard_map/ppermute | solution.py:91

commit v4 on v2

--- a/solution.py
+++ b/solution.py
@@ -19,7 +19,7 @@
 LIMIT = 56
 DEPTH = 8
 TILE = 256
-SHARES = ((0, 1), (2, 3), (4, 5), (6,), (7,))
+SHARES = ((), (0, 1), (2, 3), (4, 5), (6, 7))
 CORNER_OF = (0, 4, 2, 1, 3, 5, 6, 7)
 
 
@@ -183,7 +183,8 @@
                     unit.at[:, rows], blocks_ref.at[pl.ds(start, 8), rows], sems.at[part, n]
                 )
             )
-            arriving[-1].start()
+    for copy in arriving[:8]:
+        copy.start()
     columns = heads_t.shape[1] // 2
     lane = lax.broadcasted_iota(jnp.int32, (HALF, LANES), 1)
     column = lax.broadcasted_iota(jnp.int32, (HALF, columns), 1)
@@ -208,13 +209,16 @@
 
     for copy in arriving[:8]:
         copy.wait()
+    for copy in arriving[8:]:
+        copy.start()
     for chunk in range(8):
         lhs_t[:, chunk * 4 * LANES : (chunk + 1) * 4 * LANES] = rows_of(core, blocks_ref, chunk, 0, 4)
-    for copy in arriving[8:]:
-        copy.wait()
     for j, chunks in enumerate(SHARES):
         at = slice(j * TILE, (j + 1) * TILE)
         teacher[:, at] = jnp.dot(lhs_t[...], heads_t[:, at], preferred_element_type=F32)
+        if j == 1:
+            for copy in arriving[8:]:
+                copy.wait()
         for chunk in chunks:
             lhs_s[:, chunk * 5 * LANES : (chunk + 1) * 5 * LANES] = rows_of(
                 core, blocks_ref, chunk, at_s, 5
@@ -433,6 +437,52 @@
     )(own, other, mine, got)
 
 
+def pack_kernel(core_ref, own_t_in, got_t, own_s_in, got_s, ids_ref, out_ref, own_t, own_s, sems):
+    copies = [
+        pltpu.make_async_copy(own_t_in, own_t, sems.at[0]),
+        pltpu.make_async_copy(own_s_in, own_s, sems.at[1]),
+    ]
+    for copy in copies:
+        copy.start()
+    first = core_ref[0] == 0
+
+    def sides(own_ref, got_ref):
+        own, got = (ref[...].astype(F32) for ref in (own_ref, got_ref))
+        own, got = (jnp.where(first, v[:HALF], v[HALF:]) for v in (own, got))
+        return jnp.where(first, own, got), jnp.where(first, got, own)
+
+    ids = jnp.where(first, ids_ref[:, :HALF], ids_ref[:, HALF:])
+    ids = jnp.concatenate([ids, jnp.zeros((1, LANES - HALF), jnp.int32)], axis=1)
+    ids = jnp.concatenate([ids // 4096, ids // 64 % 64, ids % 64, jnp.zeros((ID_ROWS - 3, LANES), jnp.int32)], axis=0)
+    for copy in copies:
+        copy.wait()
+    teacher = jnp.concatenate(sides(own_t, got_t), axis=1)
+    student = jnp.concatenate(sides(own_s, got_s), axis=1)
+    rows = [teacher[:, i : i + LANES] for i in range(0, teacher.shape[1], LANES)]
+    rows.append(ids.astype(F32))
+    rows += [student[:, i : i + LANES] for i in range(0, student.shape[1], LANES)]
+    block = jnp.concatenate(rows, axis=0).astype(BF16)
+    out_ref[...] = jnp.broadcast_to(block, out_ref.shape)
+
+
+def pack(core, own_t, got_t, own_s, got_s, sampled):
+    rows = (own_t.shape[1] + own_s.shape[1]) * 2 * HALF // LANES + ID_ROWS
+    return pl.pallas_call(
+        pack_kernel,
+        name="pack",
+        in_specs=[SMEM, HBM, VMEM, HBM, VMEM, VMEM],
+        out_specs=VMEM,
+        out_shape=jax.ShapeDtypeStruct((8, rows, LANES), BF16),
+        scratch_shapes=[
+            pltpu.VMEM(own_t.shape, BF16),
+            pltpu.VMEM(own_s.shape, BF16),
+            pltpu.SemaphoreType.DMA((2,)),
+        ],
+        compiler_params=params(6),
+        cost_estimate=cost(0, 1 << 20),
+    )(core.reshape(1).astype(jnp.int32), in_hbm(own_t), in_vmem(got_t), in_hbm(own_s), in_vmem(got_s), sampled.reshape(1, 2 * HALF))
+
+
 def per_device(teacher_hidden, student_hidden, teacher_head, student_head, lengths, sampled):
     group, member = lax.axis_index("grp"), lax.axis_index("vocab")
     core = member % 2
@@ -444,36 +494,13 @@
     strips_t, strips_s = part_t // LANES, part_s // LANES
 
     got_t, got_s = swap(teacher_hidden), swap(student_hidden)
-    teacher_late, student_late, got_t, got_s = lax.optimization_barrier(
-        (teacher_head, student_head, got_t, got_s)
-    )
+    teacher_late, student_late, got_t, got_s = lax.optimization_barrier((teacher_head, student_head, got_t, got_s))
     other_teacher_head = swap(teacher_late)
     other_student_head = swap(student_late)
 
-    def half(value):
-        value = value.reshape(2, HALF, -1)
-        return jnp.where(is_first, value[0], value[1])
-
-    def sides(own, got):
-        own, got = half(own), half(got)
-        return jnp.where(is_first, own, got), jnp.where(is_first, got, own)
-
-    def strips(a, b, count):
-        rows = jnp.concatenate([a, b], axis=1).reshape(HALF, count, LANES)
-        return rows.transpose(1, 0, 2).reshape(count * HALF, LANES)
-
-    ids = sampled.reshape(2, HALF)
-    ids = jnp.where(is_first, ids[0], ids[1])
-    digits = jnp.stack([ids // 4096, (ids // 64) % 64, ids % 64]).astype(BF16)
-    digits = jnp.pad(digits, ((0, ID_ROWS - 3), (0, LANES - HALF)))
-    block = jnp.concatenate(
-        [
-            strips(*sides(teacher_hidden, got_t), strips_t),
-            digits,
-            strips(*sides(student_hidden, got_s), strips_s),
-        ]
-    )
-    near = to_all(block, FIRST)
+    blocks = pack(core, teacher_hidden, got_t, student_hidden, got_s, sampled)
+    near = lax.all_to_all(blocks, BOTH, 0, 0, axis_index_groups=FIRST)
+    near, other_student_head = lax.optimization_barrier((near, other_student_head))
     units = second_gather(near)
     heads_t, heads_s = prefetch(
         teacher_head, other_teacher_head, student_head, other_student_head, units[1:4]

time: 133 us -> 130 us (0.977)
  starting transfers between devices: 28.4 us -> 25.5 us
  other arithmetic: 4.47 us -> 2.01 us
  waiting for transfers between devices: 36 us -> 37.4 us
    ppermute x8, starting transfers between devices: 15 us -> 10.4 us  [swap(): return lax.ppermute(value, BOTH, SWAP)]
    ppermute x7, waiting for transfers between devices: 15.1 us -> 11.5 us  [along(): return lax.ppermute(value, BOTH, links(axes))]
    all_to_all x1, waiting for transfers between devices: 12.2 us -> 15.8 us  [per_device(): lax.all_to_all(part.reshape(64, HALF, part_s), BOTH, 0, 0, axis_index_gro...]
    select_n x3 -> x0, other arithmetic: 1.6 us -> none  [the longest x2 0.83 us: per_device(): digits = jnp.stack([ids // 4096, ids // 64 % 64, ids % 64]).astype(BF16)]
    all_to_all x1, waiting for transfers between devices: 5.9 us -> 7.38 us  [per_device(): all_stats = lax.all_to_all(stats, BOTH, 0, 0, axis_index_groups=SAME_CORE)]
    ppermute x7, starting transfers between devices: 3.91 us -> 5.33 us  [along(): return lax.ppermute(value, BOTH, links(axes))]
  transfers between devices with their start and end apart: 17 -> 17, of which waited for: 8 -> 10; matrix products, arithmetic and copies ran while one was open for 4% -> 2% of each run, Pallas kernels for 21% -> 22%
where the time goes in v4:
time: 130 us; the launch traced here: 129 us
  Pallas kernels  39.9 us (31%)
  waiting for transfers between devices  37.4 us (29%)
  starting transfers between devices  25.5 us (20%)
  blocking collectives  20.8 us (16%)
  local copies, waits for them, and re-layouts  2.72 us (2%)
  other arithmetic  2.01 us (2%)
    all_to_all x1, blocking collectives, per_device(): near = lax.all_to_all(blocks, BOTH, 0, 0, axis_index_groups=FIRST)  20.8 us
    all_to_all x1, waiting for transfers between devices, per_device(): lax.all_to_all(part.reshape(64, HALF, part_s), BOTH, 0, 0, axis_index_gro...  15.8 us
    pallas_call x1, Pallas kernels, logits_of(): pl.pallas_call(logits_kernel, name='logits', in_specs=[SMEM] + [HBM] * 8...  11.6 us
    ppermute x7, waiting for transfers between devices, along(): return lax.ppermute(value, BOTH, links(axes))  11.5 us
    ppermute x8, starting transfers between devices, swap(): return lax.ppermute(value, BOTH, SWAP)  10.4 us
    pallas_call x1, Pallas kernels, head_gradient_of(): pl.pallas_call(head_kernel, name='head_gradient', grid=(8,), in_specs=[st...  10 us
    pallas_call x1, Pallas kernels, gradient_of(): pl.pallas_call(gradient_kernel, name='hidden_gradient', in_specs=[SMEM] *...  9.44 us
    pallas_call x1, Pallas kernels, prefetch(): pl.pallas_call(prefetch_kernel, name='prefetch_heads', in_specs=[HBM] * 4...  7.91 us
  transfers between devices with their start and end apart: 17, of which 10 were waited for; matrix products, arithmetic and copies ran while one was open for 2% of the time, Pallas kernels for 22%

profile of v4, /device:TPU:1, one launch (start us, length us, event | category | flops | bytes accessed | tf_op | source)
XLA Modules:
  0.0 129.2 jit_solution(4767565548671647065)
XLA Ops:
  0.6 1.5 %collective-permute-start.1 = (bf16[64,320]{1,0:T(8,128)(2,1)}, bf16[64,320]{1,0:T(8,128)(2,1)S(1)}, u32[]{:S(2)}, u32[]{:S(2)}) collective-permute-start(bf16[64,320]{1,0:T(8,128)(2,1)} %own_s_in.1), channel_id=1, source_target_pairs={{0,1},{1,0},{2,3},{3,2},{4,5},{5,4},{6,7},{7,6},{8,9},{9,8},{10,11... | collective-permute-start | bytes 122888 | tf_op jit(solution)/shard_map/ppermute | solution.py:91
  2.2 1.3 %collective-permute-done.got_t = bf16[64,256]{1,0:T(8,128)(2,1)S(1)} collective-permute-done((bf16[64,256]{1,0:T(8,128)(2,1)}, bf16[64,256]{1,0:T(8,128)(2,1)S(1)}, u32[]{:S(2)}, u32[]{:S(2)}) %collective-permute-start) | collective-permute-done | bytes 32800 | tf_op jit(solution)/shard_map/ppermute | solution.py:91
  3.6 0.2 collective-permute-start.2
  3.7 0.3 collective-permute-start.10
  4.1 0.7 copy-done.4
  4.7 0.9 pack.1
  5.7 20.8 %all_to_all.15.refs_0_ = bf16[8,304,128]{2,1,0:T(8,128)(2,1)S(1)} all-to-all(bf16[8,304,128]{2,1,0:T(8,128)(2,1)S(1)} %pack.1), channel_id=1, replica_groups={{0,16,2,18,64,80,66,82},{32,48,34,50,96,112,98,114},{4,20,6,22,68,84,70..., dimensions={0} | all-to-all | bytes 1245184 | tf_op jit(solution)/shard_map/all_to_all | solution.py:502
  26.7 3.6 %collective-permute-start.9 = (bf16[8,304,128]{2,1,0:T(8,128)(2,1)S(1)}, bf16[8,304,128]{2,1,0:T(8,128)(2,1)S(1)}, u32[]{:S(2)}, u32[]{:S(2)}) collective-permute-start(bf16[8,304,128]{2,1,0:T(8,128)(2,1)S(1)} %all_to_all.15.refs_0_), channel_id=1, source_target_pairs={{0,126},{1,83},{16,110},{17,67},{32,94},{33,115},{48,78},{49,99},{... | collective-permute-start | bytes 1867784 | tf_op jit(solution)/shard_map/ppermute | solution.py:103
  30.3 5.3 %collective-permute-done.5.third.refs_3_ = bf16[8,304,128]{2,1,0:T(8,128)(2,1)S(1)} collective-permute-done((bf16[8,304,128]{2,1,0:T(8,128)(2,1)S(1)}, bf16[8,304,128]{2,1,0:T(8,128)(2,1)S(1)}, u32[]{:S(2)}, u32[]{:S(2)}) %collective-permute-start.5) | collective-permute-done | bytes 622624 | tf_op jit(solution)/shard_map/ppermute | solution.py:103
  35.7 0.4 collective-permute-done.3.first.refs_1_
  36.1 1.5 %collective-permute-start.7 = (bf16[8,304,128]{2,1,0:T(8,128)(2,1)S(1)}, bf16[8,304,128]{2,1,0:T(8,128)(2,1)}, u32[]{:S(2)}, u32[]{:S(2)}) collective-permute-start(bf16[8,304,128]{2,1,0:T(8,128)(2,1)S(1)} %collective-permute-done.3.first.refs_1_), channel_id=1, source_target_pairs={{0,48},{1,17},{16,32},{17,1},{32,16},{33,49},{48,0},{49,33},{2,50}... | collective-permute-start | bytes 1867784 | tf_op jit(solution)/shard_map/ppermute | solution.py:103
  37.6 7.9 %prefetch_heads.1 = (bf16[4096,1280]{1,0:T(8,128)(2,1)S(1)}, bf16[5120,1280]{1,0:T(8,128)(2,1)S(1)}) custom-call(bf16[4096,640]{1,0:T(8,128)(2,1)} %own_t.1, bf16[4096,640]{1,0:T(8,128)(2,1)} %collective-permute-done.10.other_t, bf16[5120,640]{1,0:T(8,128)(2,1)} %own_s.3, bf16[5120,640]{1,0:T(8,128)(2,1)} %collective-permute-done.2.other_s, ...), custom_call_target="tpu_custom_call" | custom-call | bytes 47185920 | tf_op jit(solution)/shard_map/prefetch_heads/pallas_call | solution.py:355
  45.6 4.7 %collective-permute-done.6.refs_4_ = bf16[8,304,128]{2,1,0:T(8,128)(2,1)} collective-permute-done((bf16[8,304,128]{2,1,0:T(8,128)(2,1)S(1)}, bf16[8,304,128]{2,1,0:T(8,128)(2,1)}, u32[]{:S(2)}, u32[]{:S(2)}) %collective-permute-start.6) | collective-permute-done | bytes 622624 | tf_op jit(solution)/shard_map/ppermute | solution.py:103
  50.3 1.1 collective-permute-done.7.refs_5_
  51.4 11.6 %logits.1 = (f32[256,1280]{1,0:T(8,128)S(1)}, f32[256,1280]{1,0:T(8,128)S(1)}, f32[64,8,128]{2,1,0:T(8,128)}, bf16[256,5120]{1,0:T(8,128)(2,1)}) custom-call(s32[4]{0:T(128)S(1)} %pad_add_fusion.place_ref, bf16[8,304,128]{2,1,0:T(8,128)(2,1)} %copy-done.5, bf16[8,304,128]{2,1,0:T(8,128)(2,1)} %copy-done.2, bf16[8,304,128]{2,1,0:T(8,128)(2,1)} %copy-done.1, ...), custom_call_target="tpu_custom_call" | custom-call | flops 6039797760 | bytes 8388608 | tf_op jit(solution)/shard_map/logits/pallas_call | solution.py:371
  63.0 4.6 %all-to-all-start.1 = ((f32[64,8,128]{2,1,0:T(8,128)}), f32[64,8,128]{2,1,0:T(8,128)S(1)}, u32[]{:S(2)}, u32[]{:S(2)}) async-start(f32[64,8,128]{2,1,0:T(8,128)} %get-tuple-element.29), calls=%async_computation.1 | async-start | bytes 524288 | tf_op jit(solution)/shard_map/all_to_all | solution.py:517
  67.7 1.9 %collective-permute-start.11 = (bf16[256,5120]{1,0:T(8,128)(2,1)}, bf16[256,5120]{1,0:T(8,128)(2,1)}, u32[]{:S(2)}, u32[]{:S(2)}) collective-permute-start(bf16[256,5120]{1,0:T(8,128)(2,1)} %get-tuple-element.33.own_ref), channel_id=1, source_target_pairs={{0,1},{1,0},{2,3},{3,2},{4,5},{5,4},{6,7},{7,6},{8,9},{9,8},{10,11... | collective-permute-start | bytes 7864328 | tf_op jit(solution)/shard_map/ppermute | solution.py:91
  69.6 7.4 %all-to-all-done.1.stats_ref = f32[64,8,128]{2,1,0:T(8,128)S(1)} async-done(((f32[64,8,128]{2,1,0:T(8,128)}), f32[64,8,128]{2,1,0:T(8,128)S(1)}, u32[]{:S(2)}, u32[]{:S(2)}) %all-to-all-start.1) | async-done | bytes 262176 | tf_op jit(solution)/shard_map/all_to_all | solution.py:517
  77.0 9.4 %hidden_gradient.1 = (bf16[8,8,32,640]{3,2,1,0:T(8,128)(2,1)}, bf16[256,1280]{1,0:T(8,128)(2,1)}, f32[8,256]{1,0:T(8,128)}) custom-call(s32[4]{0:T(128)} %copy-done.3, s32[8]{0:T(128)} %lengths_ref.1, f32[64,8,128]{2,1,0:T(8,128)S(1)} %all-to-all-done.1.stats_ref, f32[256,1280]{1,0:T(8,128)S(1)} %get-tuple-element.30.teacher, ...), custom_call_target="tpu_custom_call" | custom-call | flops 3355443200 | bytes 13107200 | tf_op jit(solution)/shard_map/hidden_gradient/pallas_call | solution.py:400
  86.4 5.1 %all-to-all-start.2 = ((bf16[64,32,640]{2,1,0:T(8,128)(2,1)}), bf16[64,32,640]{2,1,0:T(8,128)(2,1)S(1)}, u32[]{:S(2)}, u32[]{:S(2)}) async-start(bf16[64,32,640]{2,1,0:T(8,128)(2,1)} %bitcast.11), calls=%async_computation.2 | async-start | bytes 5242880 | tf_op jit(solution)/shard_map/all_to_all | solution.py:523
  91.7 2.9 %collective-permute-start.12 = (bf16[256,640]{1,0:T(8,128)(2,1)S(1)}, bf16[256,640]{1,0:T(8,128)(2,1)S(1)}, u32[]{:S(2)}, u32[]{:S(2)}) collective-permute-start(bf16[256,640]{1,0:T(8,128)(2,1)S(1)} %slice.15), channel_id=1, source_target_pairs={{0,1},{1,0},{2,3},{3,2},{4,5},{5,4},{6,7},{7,6},{8,9},{9,8},{10,11... | collective-permute-start | bytes 983048 | tf_op jit(solution)/shard_map/ppermute | solution.py:91
  94.5 0.8 constant_dynamic-slice_fusion
  95.3 1.1 collective-permute-done.14
  96.4 0.8 dynamic-slice_select_fusion
  97.2 0.7 copy-done.8
  97.9 10.0 %head_gradient.1 = bf16[5120,640]{1,0:T(8,128)(2,1)} custom-call(bf16[256,5120]{1,0:T(8,128)(2,1)} %get-tuple-element.33.own_ref, bf16[256,5120]{1,0:T(8,128)(2,1)} %collective-permute-done.11.other_ref, bf16[256,1280]{1,0:T(8,128)(2,1)} %get-tuple-element.34.mine_ref, bf16[256,640]{1,0:T(8,128)(2,1)} %copy-done.8), custom_call_target="tpu_custom_call" | custom-call | flops 3355443200 | bytes 16777216 | tf_op jit(solution)/shard_map/head_gradient/pallas_call | solution.py:428
  108.0 15.8 %all-to-all-done.2 = bf16[64,32,640]{2,1,0:T(8,128)(2,1)S(1)} async-done(((bf16[64,32,640]{2,1,0:T(8,128)(2,1)}), bf16[64,32,640]{2,1,0:T(8,128)(2,1)S(1)}, u32[]{:S(2)}, u32[]{:S(2)}) %all-to-all-start.2) | async-done | bytes 2621472 | tf_op jit(solution)/shard_map/all_to_all | solution.py:523
  123.7 0.4 reduce_sum.12
  124.2 3.5 %collective-permute-start.13 = (bf16[32,320]{1,0:T(8,128)(2,1)S(1)}, bf16[32,320]{1,0:T(8,128)(2,1)S(1)}, u32[]{:S(2)}, u32[]{:S(2)}) collective-permute-start(bf16[32,320]{1,0:T(8,128)(2,1)S(1)} %broadcast_select_fusion.2), channel_id=1, source_target_pairs={{0,1},{1,0},{2,3},{3,2},{4,5},{5,4},{6,7},{7,6},{8,9},{9,8},{10,11... | collective-permute-start | bytes 61448 | tf_op jit(solution)/shard_map/ppermute | solution.py:91
  127.7 0.5 slice_bitcast_fusion
  128.2 0.3 collective-permute-done.13
  128.6 0.6 pad_maximum_fusion
  (35 shorter events, 0.7 us)
Async XLA Ops:
  0.6 2.9 %collective-permute-start.1 = (bf16[64,320]{1,0:T(8,128)(2,1)}, bf16[64,320]{1,0:T(8,128)(2,1)S(1)}, u32[]{:S(2)}, u32[]{:S(2)}) collective-permute-start(bf16[64,320]{1,0:T(8,128)(2,1)} %own_s_in.1), channel_id=1, source_target_pairs={{0,1},{1,0},{2,3},{3,2},{4,5},{5,4},{6,7},{7,6},{8,9},{9,8},{10,11... | collective-permute-start | bytes 122888 | tf_op jit(solution)/shard_map/ppermute | solution.py:91
  2.1 1.4 %collective-permute-start = (bf16[64,256]{1,0:T(8,128)(2,1)}, bf16[64,256]{1,0:T(8,128)(2,1)S(1)}, u32[]{:S(2)}, u32[]{:S(2)}) collective-permute-start(bf16[64,256]{1,0:T(8,128)(2,1)} %own_t_in.1), channel_id=1, source_target_pairs={{0,1},{1,0},{2,3},{3,2},{4,5},{5,4},{6,7},{7,6},{8,9},{9,8},{10,11... | collective-permute-start | bytes 98312 | tf_op jit(solution)/shard_map/ppermute | solution.py:91
  3.6 22.9 %collective-permute-start.2 = (bf16[5120,640]{1,0:T(8,128)(2,1)}, bf16[5120,640]{1,0:T(8,128)(2,1)}, u32[]{:S(2)}, u32[]{:S(2)}) collective-permute-start(bf16[5120,640]{1,0:T(8,128)(2,1)} %own_s.3), channel_id=1, source_target_pairs={{0,1},{1,0},{2,3},{3,2},{4,5},{5,4},{6,7},{7,6},{8,9},{9,8},{10,11... | collective-permute-start | bytes 19660808 | tf_op jit(solution)/shard_map/ppermute | solution.py:91
  3.7 33.9 %collective-permute-start.10 = (bf16[4096,640]{1,0:T(8,128)(2,1)}, bf16[4096,640]{1,0:T(8,128)(2,1)}, u32[]{:S(2)}, u32[]{:S(2)}) collective-permute-start(bf16[4096,640]{1,0:T(8,128)(2,1)} %own_t.1), channel_id=1, source_target_pairs={{0,1},{1,0},{2,3},{3,2},{4,5},{5,4},{6,7},{7,6},{8,9},{9,8},{10,11... | collective-permute-start | bytes 15728648 | tf_op jit(solution)/shard_map/ppermute | solution.py:91
  4.1 0.7 copy-start.4
  26.5 19.1 %copy-start.5 = (bf16[8,304,128]{2,1,0:T(8,128)(2,1)}, bf16[8,304,128]{2,1,0:T(8,128)(2,1)S(1)}, u32[]{:S(2)}) copy-start(bf16[8,304,128]{2,1,0:T(8,128)(2,1)S(1)} %all_to_all.15.refs_0_) | copy-start | bytes 1867780
  26.5 9.1 %collective-permute-start.5 = (bf16[8,304,128]{2,1,0:T(8,128)(2,1)S(1)}, bf16[8,304,128]{2,1,0:T(8,128)(2,1)S(1)}, u32[]{:S(2)}, u32[]{:S(2)}) collective-permute-start(bf16[8,304,128]{2,1,0:T(8,128)(2,1)S(1)} %all_to_all.15.refs_0_), channel_id=1, source_target_pairs={{0,48},{1,17},{16,32},{17,1},{32,16},{33,49},{48,0},{49,33},{2,50}... | collective-permute-start | bytes 1867784 | tf_op jit(solution)/shard_map/ppermute | solution.py:103
  26.5 9.2 %collective-permute-start.4 = (bf16[8,304,128]{2,1,0:T(8,128)(2,1)S(1)}, bf16[8,304,128]{2,1,0:T(8,128)(2,1)S(1)}, u32[]{:S(2)}, u32[]{:S(2)}) collective-permute-start(bf16[8,304,128]{2,1,0:T(8,128)(2,1)S(1)} %all_to_all.15.refs_0_), channel_id=1, source_target_pairs={{0,6},{1,3},{16,22},{17,19},{32,38},{33,35},{48,54},{49,51},{2,4},... | collective-permute-start | bytes 1867784 | tf_op jit(solution)/shard_map/ppermute | solution.py:103
  26.6 9.5 %collective-permute-start.3 = (bf16[8,304,128]{2,1,0:T(8,128)(2,1)S(1)}, bf16[8,304,128]{2,1,0:T(8,128)(2,1)S(1)}, u32[]{:S(2)}, u32[]{:S(2)}) collective-permute-start(bf16[8,304,128]{2,1,0:T(8,128)(2,1)S(1)} %all_to_all.15.refs_0_), channel_id=1, source_target_pairs={{0,72},{1,65},{16,88},{17,81},{32,104},{33,97},{48,120},{49,113},{... | collective-permute-start | bytes 1867784 | tf_op jit(solution)/shard_map/ppermute | solution.py:103
  26.7 18.9 %collective-permute-start.9 = (bf16[8,304,128]{2,1,0:T(8,128)(2,1)S(1)}, bf16[8,304,128]{2,1,0:T(8,128)(2,1)S(1)}, u32[]{:S(2)}, u32[]{:S(2)}) collective-permute-start(bf16[8,304,128]{2,1,0:T(8,128)(2,1)S(1)} %all_to_all.15.refs_0_), channel_id=1, source_target_pairs={{0,126},{1,83},{16,110},{17,67},{32,94},{33,115},{48,78},{49,99},{... | collective-permute-start | bytes 1867784 | tf_op jit(solution)/shard_map/ppermute | solution.py:103
  35.6 10.0 %copy-start = (bf16[8,304,128]{2,1,0:T(8,128)(2,1)}, bf16[8,304,128]{2,1,0:T(8,128)(2,1)S(1)}, u32[]{:S(2)}) copy-start(bf16[8,304,128]{2,1,0:T(8,128)(2,1)S(1)} %collective-permute-done.5.third.refs_3_) | copy-start | bytes 1867780
  35.6 14.7 %collective-permute-start.6 = (bf16[8,304,128]{2,1,0:T(8,128)(2,1)S(1)}, bf16[8,304,128]{2,1,0:T(8,128)(2,1)}, u32[]{:S(2)}, u32[]{:S(2)}) collective-permute-start(bf16[8,304,128]{2,1,0:T(8,128)(2,1)S(1)} %collective-permute-done.5.third.refs_3_), channel_id=1, source_target_pairs={{0,6},{1,3},{16,22},{17,19},{32,38},{33,35},{48,54},{49,51},{2,4},... | collective-permute-start | bytes 1867784 | tf_op jit(solution)/shard_map/ppermute | solution.py:103
  35.7 9.9 %copy-start.1 = (bf16[8,304,128]{2,1,0:T(8,128)(2,1)}, bf16[8,304,128]{2,1,0:T(8,128)(2,1)S(1)}, u32[]{:S(2)}) copy-start(bf16[8,304,128]{2,1,0:T(8,128)(2,1)S(1)} %collective-permute-done.4.second.refs_2_) | copy-start | bytes 1867780
  35.7 14.6 %collective-permute-start.8 = (bf16[8,304,128]{2,1,0:T(8,128)(2,1)S(1)}, bf16[8,304,128]{2,1,0:T(8,128)(2,1)}, u32[]{:S(2)}, u32[]{:S(2)}) collective-permute-start(bf16[8,304,128]{2,1,0:T(8,128)(2,1)S(1)} %collective-permute-done.4.second.refs_2_), channel_id=1, source_target_pairs={{0,72},{1,65},{16,88},{17,81},{32,104},{33,97},{48,120},{49,113},{... | collective-permute-start | bytes 1867784 | tf_op jit(solution)/shard_map/ppermute | solution.py:103
  36.1 9.5 %copy-start.2 = (bf16[8,304,128]{2,1,0:T(8,128)(2,1)}, bf16[8,304,128]{2,1,0:T(8,128)(2,1)S(1)}, u32[]{:S(2)}) copy-start(bf16[8,304,128]{2,1,0:T(8,128)(2,1)S(1)} %collective-permute-done.3.first.refs_1_) | copy-start | bytes 1867780
  36.1 15.4 %collective-permute-start.7 = (bf16[8,304,128]{2,1,0:T(8,128)(2,1)S(1)}, bf16[8,304,128]{2,1,0:T(8,128)(2,1)}, u32[]{:S(2)}, u32[]{:S(2)}) collective-permute-start(bf16[8,304,128]{2,1,0:T(8,128)(2,1)S(1)} %collective-permute-done.3.first.refs_1_), channel_id=1, source_target_pairs={{0,48},{1,17},{16,32},{17,1},{32,16},{33,49},{48,0},{49,33},{2,50}... | collective-permute-start | bytes 1867784 | tf_op jit(solution)/shard_map/ppermute | solution.py:103
  37.6 13.8 %copy-start.3 = (s32[4]{0:T(128)}, s32[4]{0:T(128)S(1)}, u32[]{:S(2)}) copy-start(s32[4]{0:T(128)S(1)} %pad_add_fusion.place_ref) | copy-start | bytes 52
  45.6 5.8 %copy-start.7 = (bf16[8,304,128]{2,1,0:T(8,128)(2,1)}, bf16[8,304,128]{2,1,0:T(8,128)(2,1)S(1)}, u32[]{:S(2)}) copy-start(bf16[8,304,128]{2,1,0:T(8,128)(2,1)S(1)} %collective-permute-done.9.refs_7_) | copy-start | bytes 1867780
  63.0 13.9 %all-to-all-start.1 = ((f32[64,8,128]{2,1,0:T(8,128)}), f32[64,8,128]{2,1,0:T(8,128)S(1)}, u32[]{:S(2)}, u32[]{:S(2)}) async-start(f32[64,8,128]{2,1,0:T(8,128)} %get-tuple-element.29), calls=%async_computation.1 | async-start | bytes 524288 | tf_op jit(solution)/shard_map/all_to_all | solution.py:517
  67.7 29.6 %collective-permute-start.11 = (bf16[256,5120]{1,0:T(8,128)(2,1)}, bf16[256,5120]{1,0:T(8,128)(2,1)}, u32[]{:S(2)}, u32[]{:S(2)}) collective-permute-start(bf16[256,5120]{1,0:T(8,128)(2,1)} %get-tuple-element.33.own_ref), channel_id=1, source_target_pairs={{0,1},{1,0},{2,3},{3,2},{4,5},{5,4},{6,7},{7,6},{8,9},{9,8},{10,11... | collective-permute-start | bytes 7864328 | tf_op jit(solution)/shard_map/ppermute | solution.py:91
  86.4 5.2 %copy-start.6 = (bf16[256,1280]{1,0:T(8,128)(2,1)S(1)}, bf16[256,1280]{1,0:T(8,128)(2,1)}, u32[]{:S(2)}) copy-start(bf16[256,1280]{1,0:T(8,128)(2,1)} %get-tuple-element.34.mine_ref) | copy-start | bytes 1966084
  86.4 37.3 %all-to-all-start.2 = ((bf16[64,32,640]{2,1,0:T(8,128)(2,1)}), bf16[64,32,640]{2,1,0:T(8,128)(2,1)S(1)}, u32[]{:S(2)}, u32[]{:S(2)}) async-start(bf16[64,32,640]{2,1,0:T(8,128)(2,1)} %bitcast.11), calls=%async_computation.2 | async-start | bytes 5242880 | tf_op jit(solution)/shard_map/all_to_all | solution.py:523
  91.7 5.6 %collective-permute-start.12 = (bf16[256,640]{1,0:T(8,128)(2,1)S(1)}, bf16[256,640]{1,0:T(8,128)(2,1)S(1)}, u32[]{:S(2)}, u32[]{:S(2)}) collective-permute-start(bf16[256,640]{1,0:T(8,128)(2,1)S(1)} %slice.15), channel_id=1, source_target_pairs={{0,1},{1,0},{2,3},{3,2},{4,5},{5,4},{6,7},{7,6},{8,9},{9,8},{10,11... | collective-permute-start | bytes 983048 | tf_op jit(solution)/shard_map/ppermute | solution.py:91
  95.3 1.1 collective-permute-start.14
  97.2 0.7 copy-start.8
  124.2 4.3 %collective-permute-start.13 = (bf16[32,320]{1,0:T(8,128)(2,1)S(1)}, bf16[32,320]{1,0:T(8,128)(2,1)S(1)}, u32[]{:S(2)}, u32[]{:S(2)}) collective-permute-start(bf16[32,320]{1,0:T(8,128)(2,1)S(1)} %broadcast_select_fusion.2), channel_id=1, source_target_pairs={{0,1},{1,0},{2,3},{3,2},{4,5},{5,4},{6,7},{7,6},{8,9},{9,8},{10,11... | collective-permute-start | bytes 61448 | tf_op jit(solution)/shard_map/ppermute | solution.py:91

commit v5 on v4

--- a/solution.py
+++ b/solution.py
@@ -52,6 +52,7 @@
 
 
 FIRST = cubes(0, 1, low) + cubes(1, 3, high)
+SECOND = cubes(0, 3, high) + cubes(1, 1, parity)
 SAME_CORE = [[2 * chip + core for chip in range(64)] for core in (0, 1)]
 SWAP = [(i, i ^ 1) for i in range(128)]
 
@@ -299,9 +300,9 @@
         at_t, at_s, weight = (work[at, j : j + 1] for j in range(3))
         grad = weight * (jnp.exp(student[at, :] - at_s) - jnp.exp(teacher[at, :] - at_t))
         grads[at, :] = grad.astype(BF16)
-    leaving = [pltpu.make_async_copy(grads, grads_out, out_sems.at[4])]
+    leaving = [pltpu.make_async_copy(grads, grads_out, out_sems.at[64])]
     leaving[0].start()
-    width = part.shape[3]
+    width = part.shape[2]
     chunks = size // width
     for i in range(4):
         stream.wait(2 * i)
@@ -311,12 +312,13 @@
         ).astype(BF16)
         for group in range(8):
             for j in range(chunks):
-                part[group, chunks * i + j] = product[
-                    group * HALF : (group + 1) * HALF, j * width : (j + 1) * width
-                ]
-        at = pl.ds(chunks * i, chunks)
-        leaving.append(pltpu.make_async_copy(part.at[:, at], part_out.at[:, at], out_sems.at[i]))
-        leaving[-1].start()
+                chunk = chunks * i + j
+                to = position(place_ref[3], group, chunk)
+                part[to] = product[group * HALF : (group + 1) * HALF, j * width : (j + 1) * width]
+                leaving.append(
+                    pltpu.make_async_copy(part.at[to], part_out.at[to], out_sems.at[group * 8 + chunk])
+                )
+                leaving[-1].start()
     for copy in leaving:
         copy.wait()
 
@@ -403,17 +405,17 @@
         in_specs=[SMEM] * 2 + [VMEM] * 3 + [HBM] * 2,
         out_specs=[HBM, HBM, VMEM],
         out_shape=[
-            pltpu.HBM((8, 8, HALF, wide // 8), BF16),
+            pltpu.HBM((64, HALF, wide // 8), BF16),
             pltpu.HBM((tokens, columns), BF16),
             jax.ShapeDtypeStruct((8, tokens), F32),
         ],
         scratch_shapes=[
             pltpu.VMEM((wide, columns), BF16),
-            pltpu.VMEM((8, 8, HALF, wide // 8), BF16),
+            pltpu.VMEM((64, HALF, wide // 8), BF16),
             pltpu.VMEM((tokens, columns), BF16),
             pltpu.VMEM((tokens, LANES), F32),
             pltpu.SemaphoreType.DMA((8,)),
-            pltpu.SemaphoreType.DMA((5,)),
+            pltpu.SemaphoreType.DMA((65,)),
         ],
         compiler_params=params(LIMIT),
         cost_estimate=cost(2 * tokens * wide * columns, 2 * wide * columns),
@@ -513,16 +515,22 @@
     place = [number_of * columns, (number_of + 1 - 2 * core) * columns, corner, core]
     place = jnp.stack(place).astype(jnp.int32)
     teacher_logits, student_logits, stats, own_rows = logits_of(place, units, heads_t, heads_s)
-    other_rows = swap(own_rows)
     all_stats = lax.all_to_all(stats, BOTH, 0, 0, axis_index_groups=SAME_CORE)
 
     part, grads, kl = gradient_of(
         place, lengths, all_stats, teacher_logits, student_logits, student_head, other_student_head
     )
+    grads, late_rows = lax.optimization_barrier((grads, own_rows))
+    other_rows = swap(late_rows)
     got_grad = swap(grads[:, columns:])
-    parts = lax.all_to_all(part.reshape(64, HALF, part_s), BOTH, 0, 0, axis_index_groups=SAME_CORE)
+
+    def spread(value, groups):
+        return lax.all_to_all(value, BOTH, 0, 0, axis_index_groups=groups)
+
+    parts = spread(part.reshape(8, 8, HALF, part_s), SECOND)
     head_grad = head_gradient_of(own_rows, other_rows, grads, got_grad)
     parts, head_grad = lax.optimization_barrier((parts, head_grad))
+    parts = spread(jnp.sum(parts.astype(F32), axis=0).astype(BF16), FIRST)
     hidden = jnp.sum(parts.astype(F32), axis=0).astype(BF16)
     one, two = hidden[:, : part_s // 2], hidden[:, part_s // 2 :]
     kept = jnp.where(is_first, one, two)

time: 130 us -> 129 us (level)
  blocking collectives: 20.8 us -> 34.8 us
  waiting for transfers between devices: 37.4 us -> 25.1 us
  starting transfers between devices: 25.5 us -> 20.4 us
    all_to_all x0 -> x1, blocking collectives: none -> 14 us  [per_device(): all_stats = lax.all_to_all(stats, BOTH, 0, 0, axis_index_groups=SAME_CORE)]
    all_to_all x2, waiting for transfers between devices: 23.1 us -> 9.3 us  [spread(): return lax.all_to_all(value, BOTH, 0, 0, axis_index_groups=groups)]
    all_to_all x2, starting transfers between devices: 9.76 us -> 7.06 us  [spread(): return lax.all_to_all(value, BOTH, 0, 0, axis_index_groups=groups)]
    ppermute x8, starting transfers between devices: 10.4 us -> 8.06 us  [swap(): return lax.ppermute(value, BOTH, SWAP)]
    ppermute x8, waiting for transfers between devices: 2.79 us -> 4.28 us  [swap(): return lax.ppermute(value, BOTH, SWAP)]
  transfers between devices with their start and end apart: 17 -> 17, of which waited for: 10 -> 11; matrix products, arithmetic and copies ran while one was open for 2% -> 2% of each run, Pallas kernels for 22% -> 15%
where the time goes in v5:
time: 129 us; the launch traced here: 128 us
  Pallas kernels  40.5 us (31%)
  blocking collectives  34.8 us (27%)
  waiting for transfers between devices  25.1 us (19%)
  starting transfers between devices  20.4 us (16%)
  local copies, waits for them, and re-layouts  3.48 us (3%)
  other arithmetic  2.85 us (2%)
    all_to_all x1, blocking collectives, per_device(): near = lax.all_to_all(blocks, BOTH, 0, 0, axis_index_groups=FIRST)  20.8 us
    all_to_all x1, blocking collectives, per_device(): all_stats = lax.all_to_all(stats, BOTH, 0, 0, axis_index_groups=SAME_CORE)  14 us
    pallas_call x1, Pallas kernels, logits_of(): pl.pallas_call(logits_kernel, name='logits', in_specs=[SMEM] + [HBM] * 8...  11.7 us
    ppermute x7, waiting for transfers between devices, along(): return lax.ppermute(value, BOTH, links(axes))  11.5 us
    pallas_call x1, Pallas kernels, head_gradient_of(): pl.pallas_call(head_kernel, name='head_gradient', grid=(8,), in_specs=[st...  10 us
    pallas_call x1, Pallas kernels, gradient_of(): pl.pallas_call(gradient_kernel, name='hidden_gradient', in_specs=[SMEM] *...  9.91 us
    all_to_all x2, waiting for transfers between devices, spread(): return lax.all_to_all(value, BOTH, 0, 0, axis_index_groups=groups)  9.3 us
    ppermute x8, starting transfers between devices, swap(): return lax.ppermute(value, BOTH, SWAP)  8.06 us
  transfers between devices with their start and end apart: 17, of which 11 were waited for; matrix products, arithmetic and copies ran while one was open for 2% of the time, Pallas kernels for 15%

profile of v5, /device:TPU:1, one launch (start us, length us, event | category | flops | bytes accessed | tf_op | source)
XLA Modules:
  0.0 128.0 jit_solution(3933240627139118626)
XLA Ops:
  0.6 1.5 %collective-permute-start.1 = (bf16[64,320]{1,0:T(8,128)(2,1)}, bf16[64,320]{1,0:T(8,128)(2,1)S(1)}, u32[]{:S(2)}, u32[]{:S(2)}) collective-permute-start(bf16[64,320]{1,0:T(8,128)(2,1)} %own_s_in.1), channel_id=1, source_target_pairs={{0,1},{1,0},{2,3},{3,2},{4,5},{5,4},{6,7},{7,6},{8,9},{9,8},{10,11... | collective-permute-start | bytes 122888 | tf_op jit(solution)/shard_map/ppermute | solution.py:92
  2.2 1.3 %collective-permute-done.got_t = bf16[64,256]{1,0:T(8,128)(2,1)S(1)} collective-permute-done((bf16[64,256]{1,0:T(8,128)(2,1)}, bf16[64,256]{1,0:T(8,128)(2,1)S(1)}, u32[]{:S(2)}, u32[]{:S(2)}) %collective-permute-start) | collective-permute-done | bytes 32800 | tf_op jit(solution)/shard_map/ppermute | solution.py:92
  4.1 0.7 copy-done.4
  4.7 0.9 pack.1
  5.7 20.8 %all_to_all.20.refs_0_ = bf16[8,304,128]{2,1,0:T(8,128)(2,1)S(1)} all-to-all(bf16[8,304,128]{2,1,0:T(8,128)(2,1)S(1)} %pack.1), channel_id=1, replica_groups={{0,16,2,18,64,80,66,82},{32,48,34,50,96,112,98,114},{4,20,6,22,68,84,70..., dimensions={0} | all-to-all | bytes 1245184 | tf_op jit(solution)/shard_map/all_to_all | solution.py:504
  26.7 3.6 %collective-permute-start.9 = (bf16[8,304,128]{2,1,0:T(8,128)(2,1)S(1)}, bf16[8,304,128]{2,1,0:T(8,128)(2,1)S(1)}, u32[]{:S(2)}, u32[]{:S(2)}) collective-permute-start(bf16[8,304,128]{2,1,0:T(8,128)(2,1)S(1)} %all_to_all.20.refs_0_), channel_id=1, source_target_pairs={{0,126},{1,83},{16,110},{17,67},{32,94},{33,115},{48,78},{49,99},{... | collective-permute-start | bytes 1867784 | tf_op jit(solution)/shard_map/ppermute | solution.py:104
  30.3 5.3 %collective-permute-done.5.third.refs_3_ = bf16[8,304,128]{2,1,0:T(8,128)(2,1)S(1)} collective-permute-done((bf16[8,304,128]{2,1,0:T(8,128)(2,1)S(1)}, bf16[8,304,128]{2,1,0:T(8,128)(2,1)S(1)}, u32[]{:S(2)}, u32[]{:S(2)}) %collective-permute-start.5) | collective-permute-done | bytes 622624 | tf_op jit(solution)/shard_map/ppermute | solution.py:104
  35.7 0.4 collective-permute-done.3.first.refs_1_
  36.1 1.5 %collective-permute-start.7 = (bf16[8,304,128]{2,1,0:T(8,128)(2,1)S(1)}, bf16[8,304,128]{2,1,0:T(8,128)(2,1)}, u32[]{:S(2)}, u32[]{:S(2)}) collective-permute-start(bf16[8,304,128]{2,1,0:T(8,128)(2,1)S(1)} %collective-permute-done.3.first.refs_1_), channel_id=1, source_target_pairs={{0,48},{1,17},{16,32},{17,1},{32,16},{33,49},{48,0},{49,33},{2,50}... | collective-permute-start | bytes 1867784 | tf_op jit(solution)/shard_map/ppermute | solution.py:104
  37.6 7.9 %prefetch_heads.1 = (bf16[4096,1280]{1,0:T(8,128)(2,1)S(1)}, bf16[5120,1280]{1,0:T(8,128)(2,1)S(1)}) custom-call(bf16[4096,640]{1,0:T(8,128)(2,1)} %own_t.1, bf16[4096,640]{1,0:T(8,128)(2,1)} %collective-permute-done.10.other_t, bf16[5120,640]{1,0:T(8,128)(2,1)} %own_s.3, bf16[5120,640]{1,0:T(8,128)(2,1)} %collective-permute-done.2.other_s, ...), custom_call_target="tpu_custom_call" | custom-call | bytes 47185920 | tf_op jit(solution)/shard_map/prefetch_heads/pallas_call | solution.py:357
  45.6 4.7 %collective-permute-done.6.refs_4_ = bf16[8,304,128]{2,1,0:T(8,128)(2,1)} collective-permute-done((bf16[8,304,128]{2,1,0:T(8,128)(2,1)S(1)}, bf16[8,304,128]{2,1,0:T(8,128)(2,1)}, u32[]{:S(2)}, u32[]{:S(2)}) %collective-permute-start.6) | collective-permute-done | bytes 622624 | tf_op jit(solution)/shard_map/ppermute | solution.py:104
  50.3 1.1 collective-permute-done.7.refs_5_
  51.4 11.7 %logits.1 = (f32[256,1280]{1,0:T(8,128)S(1)}, f32[256,1280]{1,0:T(8,128)S(1)}, f32[64,8,128]{2,1,0:T(8,128)}, bf16[256,5120]{1,0:T(8,128)(2,1)}) custom-call(s32[4]{0:T(128)S(1)} %pad_add_fusion.place_ref, bf16[8,304,128]{2,1,0:T(8,128)(2,1)} %copy-done.5, bf16[8,304,128]{2,1,0:T(8,128)(2,1)} %copy-done.2, bf16[8,304,128]{2,1,0:T(8,128)(2,1)} %copy-done.1, ...), custom_call_target="tpu_custom_call" | custom-call | flops 6039797760 | bytes 8388608 | tf_op jit(solution)/shard_map/logits/pallas_call | solution.py:373
  63.2 14.0 %all_to_all.21.stats_ref = f32[64,8,128]{2,1,0:T(8,128)S(1)} all-to-all(f32[64,8,128]{2,1,0:T(8,128)} %get-tuple-element.31), channel_id=1, replica_groups={{0,2,4,6,8,10,12,14,16,18,20,22,24,26,28,30,32,34,36,38,40,42,44,46,48,..., dimensions={0} | all-to-all | bytes 524288 | tf_op jit(solution)/shard_map/all_to_all | solution.py:518
  77.1 9.9 %hidden_gradient.1 = (bf16[64,32,640]{2,1,0:T(8,128)(2,1)}, bf16[256,1280]{1,0:T(8,128)(2,1)}, f32[8,256]{1,0:T(8,128)}) custom-call(s32[4]{0:T(128)} %copy-done.3, s32[8]{0:T(128)} %lengths_ref.1, f32[64,8,128]{2,1,0:T(8,128)S(1)} %all_to_all.21.stats_ref, f32[256,1280]{1,0:T(8,128)S(1)} %get-tuple-element.32.teacher, ...), custom_call_target="tpu_custom_call" | custom-call | flops 3355443200 | bytes 13107200 | tf_op jit(solution)/shard_map/hidden_gradient/pallas_call | solution.py:402
  87.1 2.8 %collective-permute-start.11 = (bf16[256,5120]{1,0:T(8,128)(2,1)}, bf16[256,5120]{1,0:T(8,128)(2,1)}, u32[]{:S(2)}, u32[]{:S(2)}) collective-permute-start(bf16[256,5120]{1,0:T(8,128)(2,1)} %get-tuple-element.37.own_ref), channel_id=1, source_target_pairs={{0,1},{1,0},{2,3},{3,2},{4,5},{5,4},{6,7},{7,6},{8,9},{9,8},{10,11... | collective-permute-start | bytes 7864328 | tf_op jit(solution)/shard_map/ppermute | solution.py:92
  89.9 3.6 %all-to-all-start.2 = ((bf16[8,8,32,640]{3,2,1,0:T(8,128)(2,1)}), bf16[8,8,32,640]{3,2,1,0:T(8,128)(2,1)S(1)}, u32[]{:S(2)}, u32[]{:S(2)}) async-start(bf16[8,8,32,640]{3,2,1,0:T(8,128)(2,1)} %bitcast.11), calls=%async_computation.2 | async-start | bytes 5242880 | tf_op jit(solution)/shard_map/all_to_all | solution.py:528
  93.5 0.8 slice.15
  94.4 1.7 %collective-permute-done.12.got_ref = bf16[256,640]{1,0:T(8,128)(2,1)S(1)} collective-permute-done((bf16[256,640]{1,0:T(8,128)(2,1)}, bf16[256,640]{1,0:T(8,128)(2,1)S(1)}, u32[]{:S(2)}, u32[]{:S(2)}) %collective-permute-start.12) | collective-permute-done | bytes 327712 | tf_op jit(solution)/shard_map/ppermute | solution.py:92
  96.1 0.8 copy-done.8
  96.9 10.0 %head_gradient.1 = bf16[5120,640]{1,0:T(8,128)(2,1)} custom-call(bf16[256,5120]{1,0:T(8,128)(2,1)} %get-tuple-element.37.own_ref, bf16[256,5120]{1,0:T(8,128)(2,1)} %collective-permute-done.11.other_ref, bf16[256,1280]{1,0:T(8,128)(2,1)} %get-tuple-element.38.mine_ref, bf16[256,640]{1,0:T(8,128)(2,1)} %copy-done.8), custom_call_target="tpu_custom_call" | custom-call | flops 3355443200 | bytes 16777216 | tf_op jit(solution)/shard_map/head_gradient/pallas_call | solution.py:430
  106.9 5.1 %all-to-all-done.2 = bf16[8,8,32,640]{3,2,1,0:T(8,128)(2,1)S(1)} async-done(((bf16[8,8,32,640]{3,2,1,0:T(8,128)(2,1)}), bf16[8,8,32,640]{3,2,1,0:T(8,128)(2,1)S(1)}, u32[]{:S(2)}, u32[]{:S(2)}) %all-to-all-start.2) | async-done | bytes 2621472 | tf_op jit(solution)/shard_map/all_to_all | solution.py:528
  112.0 1.2 reduce_sum.24
  113.2 3.4 %all-to-all-start.3 = ((bf16[8,32,640]{2,1,0:T(8,128)(2,1)}), bf16[8,32,640]{2,1,0:T(8,128)(2,1)S(1)}, u32[]{:S(2)}, u32[]{:S(2)}) async-start(bf16[8,32,640]{2,1,0:T(8,128)(2,1)} %reduce_sum.24), calls=%async_computation.3 | async-start | bytes 655360 | tf_op jit(solution)/shard_map/all_to_all | solution.py:528
  116.6 0.8 constant_dynamic-slice_fusion
  117.4 2.7 %collective-permute-start.14 = (f32[2,4]{1,0:T(2,128)S(1)}, f32[2,4]{1,0:T(2,128)S(1)}, u32[]{:S(2)}, u32[]{:S(2)}) collective-permute-start(f32[2,4]{1,0:T(2,128)S(1)} %constant_dynamic-slice_fusion), channel_id=1, source_target_pairs={{0,1},{1,0},{2,3},{3,2},{4,5},{5,4},{6,7},{7,6},{8,9},{9,8},{10,11... | collective-permute-start | bytes 104 | tf_op jit(solution)/shard_map/ppermute | solution.py:92
  120.1 0.8 collective-permute-done.14
  120.9 0.8 dynamic-slice_select_fusion
  121.7 4.2 %all-to-all-done.3 = bf16[8,32,640]{2,1,0:T(8,128)(2,1)S(1)} async-done(((bf16[8,32,640]{2,1,0:T(8,128)(2,1)}), bf16[8,32,640]{2,1,0:T(8,128)(2,1)S(1)}, u32[]{:S(2)}, u32[]{:S(2)}) %all-to-all-start.3) | async-done | bytes 327712 | tf_op jit(solution)/shard_map/all_to_all | solution.py:528
  126.3 0.5 slice_bitcast_fusion
  126.8 0.4 collective-permute-done.13
  127.4 0.6 pad_maximum_fusion
  (37 shorter events, 1.7 us)
Async XLA Ops:
  0.6 2.9 %collective-permute-start.1 = (bf16[64,320]{1,0:T(8,128)(2,1)}, bf16[64,320]{1,0:T(8,128)(2,1)S(1)}, u32[]{:S(2)}, u32[]{:S(2)}) collective-permute-start(bf16[64,320]{1,0:T(8,128)(2,1)} %own_s_in.1), channel_id=1, source_target_pairs={{0,1},{1,0},{2,3},{3,2},{4,5},{5,4},{6,7},{7,6},{8,9},{9,8},{10,11... | collective-permute-start | bytes 122888 | tf_op jit(solution)/shard_map/ppermute | solution.py:92
  2.1 1.4 %collective-permute-start = (bf16[64,256]{1,0:T(8,128)(2,1)}, bf16[64,256]{1,0:T(8,128)(2,1)S(1)}, u32[]{:S(2)}, u32[]{:S(2)}) collective-permute-start(bf16[64,256]{1,0:T(8,128)(2,1)} %own_t_in.1), channel_id=1, source_target_pairs={{0,1},{1,0},{2,3},{3,2},{4,5},{5,4},{6,7},{7,6},{8,9},{9,8},{10,11... | collective-permute-start | bytes 98312 | tf_op jit(solution)/shard_map/ppermute | solution.py:92
  3.6 22.9 %collective-permute-start.2 = (bf16[5120,640]{1,0:T(8,128)(2,1)}, bf16[5120,640]{1,0:T(8,128)(2,1)}, u32[]{:S(2)}, u32[]{:S(2)}) collective-permute-start(bf16[5120,640]{1,0:T(8,128)(2,1)} %own_s.3), channel_id=1, source_target_pairs={{0,1},{1,0},{2,3},{3,2},{4,5},{5,4},{6,7},{7,6},{8,9},{9,8},{10,11... | collective-permute-start | bytes 19660808 | tf_op jit(solution)/shard_map/ppermute | solution.py:92
  3.7 33.9 %collective-permute-start.10 = (bf16[4096,640]{1,0:T(8,128)(2,1)}, bf16[4096,640]{1,0:T(8,128)(2,1)}, u32[]{:S(2)}, u32[]{:S(2)}) collective-permute-start(bf16[4096,640]{1,0:T(8,128)(2,1)} %own_t.1), channel_id=1, source_target_pairs={{0,1},{1,0},{2,3},{3,2},{4,5},{5,4},{6,7},{7,6},{8,9},{9,8},{10,11... | collective-permute-start | bytes 15728648 | tf_op jit(solution)/shard_map/ppermute | solution.py:92
  4.1 0.7 copy-start.4
  26.5 19.1 %copy-start.5 = (bf16[8,304,128]{2,1,0:T(8,128)(2,1)}, bf16[8,304,128]{2,1,0:T(8,128)(2,1)S(1)}, u32[]{:S(2)}) copy-start(bf16[8,304,128]{2,1,0:T(8,128)(2,1)S(1)} %all_to_all.20.refs_0_) | copy-start | bytes 1867780
  26.5 9.1 %collective-permute-start.5 = (bf16[8,304,128]{2,1,0:T(8,128)(2,1)S(1)}, bf16[8,304,128]{2,1,0:T(8,128)(2,1)S(1)}, u32[]{:S(2)}, u32[]{:S(2)}) collective-permute-start(bf16[8,304,128]{2,1,0:T(8,128)(2,1)S(1)} %all_to_all.20.refs_0_), channel_id=1, source_target_pairs={{0,48},{1,17},{16,32},{17,1},{32,16},{33,49},{48,0},{49,33},{2,50}... | collective-permute-start | bytes 1867784 | tf_op jit(solution)/shard_map/ppermute | solution.py:104
  26.5 9.2 %collective-permute-start.4 = (bf16[8,304,128]{2,1,0:T(8,128)(2,1)S(1)}, bf16[8,304,128]{2,1,0:T(8,128)(2,1)S(1)}, u32[]{:S(2)}, u32[]{:S(2)}) collective-permute-start(bf16[8,304,128]{2,1,0:T(8,128)(2,1)S(1)} %all_to_all.20.refs_0_), channel_id=1, source_target_pairs={{0,6},{1,3},{16,22},{17,19},{32,38},{33,35},{48,54},{49,51},{2,4},... | collective-permute-start | bytes 1867784 | tf_op jit(solution)/shard_map/ppermute | solution.py:104
  26.6 9.5 %collective-permute-start.3 = (bf16[8,304,128]{2,1,0:T(8,128)(2,1)S(1)}, bf16[8,304,128]{2,1,0:T(8,128)(2,1)S(1)}, u32[]{:S(2)}, u32[]{:S(2)}) collective-permute-start(bf16[8,304,128]{2,1,0:T(8,128)(2,1)S(1)} %all_to_all.20.refs_0_), channel_id=1, source_target_pairs={{0,72},{1,65},{16,88},{17,81},{32,104},{33,97},{48,120},{49,113},{... | collective-permute-start | bytes 1867784 | tf_op jit(solution)/shard_map/ppermute | solution.py:104
  26.7 18.9 %collective-permute-start.9 = (bf16[8,304,128]{2,1,0:T(8,128)(2,1)S(1)}, bf16[8,304,128]{2,1,0:T(8,128)(2,1)S(1)}, u32[]{:S(2)}, u32[]{:S(2)}) collective-permute-start(bf16[8,304,128]{2,1,0:T(8,128)(2,1)S(1)} %all_to_all.20.refs_0_), channel_id=1, source_target_pairs={{0,126},{1,83},{16,110},{17,67},{32,94},{33,115},{48,78},{49,99},{... | collective-permute-start | bytes 1867784 | tf_op jit(solution)/shard_map/ppermute | solution.py:104
  35.6 10.0 %copy-start = (bf16[8,304,128]{2,1,0:T(8,128)(2,1)}, bf16[8,304,128]{2,1,0:T(8,128)(2,1)S(1)}, u32[]{:S(2)}) copy-start(bf16[8,304,128]{2,1,0:T(8,128)(2,1)S(1)} %collective-permute-done.5.third.refs_3_) | copy-start | bytes 1867780
  35.6 14.7 %collective-permute-start.6 = (bf16[8,304,128]{2,1,0:T(8,128)(2,1)S(1)}, bf16[8,304,128]{2,1,0:T(8,128)(2,1)}, u32[]{:S(2)}, u32[]{:S(2)}) collective-permute-start(bf16[8,304,128]{2,1,0:T(8,128)(2,1)S(1)} %collective-permute-done.5.third.refs_3_), channel_id=1, source_target_pairs={{0,6},{1,3},{16,22},{17,19},{32,38},{33,35},{48,54},{49,51},{2,4},... | collective-permute-start | bytes 1867784 | tf_op jit(solution)/shard_map/ppermute | solution.py:104
  35.7 9.9 %copy-start.1 = (bf16[8,304,128]{2,1,0:T(8,128)(2,1)}, bf16[8,304,128]{2,1,0:T(8,128)(2,1)S(1)}, u32[]{:S(2)}) copy-start(bf16[8,304,128]{2,1,0:T(8,128)(2,1)S(1)} %collective-permute-done.4.second.refs_2_) | copy-start | bytes 1867780
  35.7 14.6 %collective-permute-start.8 = (bf16[8,304,128]{2,1,0:T(8,128)(2,1)S(1)}, bf16[8,304,128]{2,1,0:T(8,128)(2,1)}, u32[]{:S(2)}, u32[]{:S(2)}) collective-permute-start(bf16[8,304,128]{2,1,0:T(8,128)(2,1)S(1)} %collective-permute-done.4.second.refs_2_), channel_id=1, source_target_pairs={{0,72},{1,65},{16,88},{17,81},{32,104},{33,97},{48,120},{49,113},{... | collective-permute-start | bytes 1867784 | tf_op jit(solution)/shard_map/ppermute | solution.py:104
  36.1 9.5 %copy-start.2 = (bf16[8,304,128]{2,1,0:T(8,128)(2,1)}, bf16[8,304,128]{2,1,0:T(8,128)(2,1)S(1)}, u32[]{:S(2)}) copy-start(bf16[8,304,128]{2,1,0:T(8,128)(2,1)S(1)} %collective-permute-done.3.first.refs_1_) | copy-start | bytes 1867780
  36.1 15.4 %collective-permute-start.7 = (bf16[8,304,128]{2,1,0:T(8,128)(2,1)S(1)}, bf16[8,304,128]{2,1,0:T(8,128)(2,1)}, u32[]{:S(2)}, u32[]{:S(2)}) collective-permute-start(bf16[8,304,128]{2,1,0:T(8,128)(2,1)S(1)} %collective-permute-done.3.first.refs_1_), channel_id=1, source_target_pairs={{0,48},{1,17},{16,32},{17,1},{32,16},{33,49},{48,0},{49,33},{2,50}... | collective-permute-start | bytes 1867784 | tf_op jit(solution)/shard_map/ppermute | solution.py:104
  37.6 13.8 %copy-start.3 = (s32[4]{0:T(128)}, s32[4]{0:T(128)S(1)}, u32[]{:S(2)}) copy-start(s32[4]{0:T(128)S(1)} %pad_add_fusion.place_ref) | copy-start | bytes 52
  45.6 5.8 %copy-start.7 = (bf16[8,304,128]{2,1,0:T(8,128)(2,1)}, bf16[8,304,128]{2,1,0:T(8,128)(2,1)S(1)}, u32[]{:S(2)}) copy-start(bf16[8,304,128]{2,1,0:T(8,128)(2,1)S(1)} %collective-permute-done.9.refs_7_) | copy-start | bytes 1867780
  87.1 6.4 %copy-start.6 = (bf16[256,1280]{1,0:T(8,128)(2,1)S(1)}, bf16[256,1280]{1,0:T(8,128)(2,1)}, u32[]{:S(2)}) copy-start(bf16[256,1280]{1,0:T(8,128)(2,1)} %get-tuple-element.38.mine_ref) | copy-start | bytes 1966084
  87.1 9.0 %collective-permute-start.11 = (bf16[256,5120]{1,0:T(8,128)(2,1)}, bf16[256,5120]{1,0:T(8,128)(2,1)}, u32[]{:S(2)}, u32[]{:S(2)}) collective-permute-start(bf16[256,5120]{1,0:T(8,128)(2,1)} %get-tuple-element.37.own_ref), channel_id=1, source_target_pairs={{0,1},{1,0},{2,3},{3,2},{4,5},{5,4},{6,7},{7,6},{8,9},{9,8},{10,11... | collective-permute-start | bytes 7864328 | tf_op jit(solution)/shard_map/ppermute | solution.py:92
  89.9 22.1 %all-to-all-start.2 = ((bf16[8,8,32,640]{3,2,1,0:T(8,128)(2,1)}), bf16[8,8,32,640]{3,2,1,0:T(8,128)(2,1)S(1)}, u32[]{:S(2)}, u32[]{:S(2)}) async-start(bf16[8,8,32,640]{3,2,1,0:T(8,128)(2,1)} %bitcast.11), calls=%async_computation.2 | async-start | bytes 5242880 | tf_op jit(solution)/shard_map/all_to_all | solution.py:528
  94.3 1.8 %collective-permute-start.12 = (bf16[256,640]{1,0:T(8,128)(2,1)}, bf16[256,640]{1,0:T(8,128)(2,1)S(1)}, u32[]{:S(2)}, u32[]{:S(2)}) collective-permute-start(bf16[256,640]{1,0:T(8,128)(2,1)} %slice.15), channel_id=1, source_target_pairs={{0,1},{1,0},{2,3},{3,2},{4,5},{5,4},{6,7},{7,6},{8,9},{9,8},{10,11... | collective-permute-start | bytes 983048 | tf_op jit(solution)/shard_map/ppermute | solution.py:92
  96.1 0.8 copy-start.8
  113.2 12.7 %all-to-all-start.3 = ((bf16[8,32,640]{2,1,0:T(8,128)(2,1)}), bf16[8,32,640]{2,1,0:T(8,128)(2,1)S(1)}, u32[]{:S(2)}, u32[]{:S(2)}) async-start(bf16[8,32,640]{2,1,0:T(8,128)(2,1)} %reduce_sum.24), calls=%async_computation.3 | async-start | bytes 655360 | tf_op jit(solution)/shard_map/all_to_all | solution.py:528
  117.4 3.5 %collective-permute-start.14 = (f32[2,4]{1,0:T(2,128)S(1)}, f32[2,4]{1,0:T(2,128)S(1)}, u32[]{:S(2)}, u32[]{:S(2)}) collective-permute-start(f32[2,4]{1,0:T(2,128)S(1)} %constant_dynamic-slice_fusion), channel_id=1, source_target_pairs={{0,1},{1,0},{2,3},{3,2},{4,5},{5,4},{6,7},{7,6},{8,9},{9,8},{10,11... | collective-permute-start | bytes 104 | tf_op jit(solution)/shard_map/ppermute | solution.py:92
  126.0 1.2 collective-permute-start.13

commit v6 on v4

--- a/solution.py
+++ b/solution.py
@@ -52,6 +52,7 @@
 
 
 FIRST = cubes(0, 1, low) + cubes(1, 3, high)
+SECOND = cubes(0, 3, high) + cubes(1, 1, parity)
 SAME_CORE = [[2 * chip + core for chip in range(64)] for core in (0, 1)]
 SWAP = [(i, i ^ 1) for i in range(128)]
 
@@ -303,6 +304,16 @@
     leaving[0].start()
     width = part.shape[3]
     chunks = size // width
+    core = place_ref[3]
+
+    def piece(i, who):
+        at = (pl.ds(2 * i, 2),) if who == 0 else (slice(None), pl.ds(2 * i, 2))
+        return pltpu.make_async_copy(part.at[at], part_out.at[at], out_sems.at[i])
+
+    def by_core(act):
+        for who in (0, 1):
+            pl.when(core == who)(lambda who=who: act(who))
+
     for i in range(4):
         stream.wait(2 * i)
         stream.wait(2 * i + 1)
@@ -311,12 +322,10 @@
         ).astype(BF16)
         for group in range(8):
             for j in range(chunks):
-                part[group, chunks * i + j] = product[
-                    group * HALF : (group + 1) * HALF, j * width : (j + 1) * width
-                ]
-        at = pl.ds(chunks * i, chunks)
-        leaving.append(pltpu.make_async_copy(part.at[:, at], part_out.at[:, at], out_sems.at[i]))
-        leaving[-1].start()
+                to = position(core, group, chunks * i + j)
+                part[to // 8, to % 8] = product[group * HALF : (group + 1) * HALF, j * width : (j + 1) * width]
+        by_core(lambda who, i=i: piece(i, who).start())
+    by_core(lambda who: [piece(i, who).wait() for i in range(4)] and None)
     for copy in leaving:
         copy.wait()
 
@@ -513,16 +522,22 @@
     place = [number_of * columns, (number_of + 1 - 2 * core) * columns, corner, core]
     place = jnp.stack(place).astype(jnp.int32)
     teacher_logits, student_logits, stats, own_rows = logits_of(place, units, heads_t, heads_s)
-    other_rows = swap(own_rows)
     all_stats = lax.all_to_all(stats, BOTH, 0, 0, axis_index_groups=SAME_CORE)
 
     part, grads, kl = gradient_of(
         place, lengths, all_stats, teacher_logits, student_logits, student_head, other_student_head
     )
+    grads, late_rows = lax.optimization_barrier((grads, own_rows))
+    other_rows = swap(late_rows)
     got_grad = swap(grads[:, columns:])
-    parts = lax.all_to_all(part.reshape(64, HALF, part_s), BOTH, 0, 0, axis_index_groups=SAME_CORE)
+
+    def spread(value, groups):
+        return lax.all_to_all(value, BOTH, 0, 0, axis_index_groups=groups)
+
+    parts = spread(part, SECOND)
     head_grad = head_gradient_of(own_rows, other_rows, grads, got_grad)
     parts, head_grad = lax.optimization_barrier((parts, head_grad))
+    parts = spread(jnp.sum(parts.astype(F32), axis=0).astype(BF16), FIRST)
     hidden = jnp.sum(parts.astype(F32), axis=0).astype(BF16)
     one, two = hidden[:, : part_s // 2], hidden[:, part_s // 2 :]
     kept = jnp.where(is_first, one, two)

time: 130 us -> 128 us (0.985)
  blocking collectives: 20.8 us -> 34.8 us
  waiting for transfers between devices: 37.4 us -> 25.1 us
  starting transfers between devices: 25.5 us -> 20.4 us
    all_to_all x0 -> x1, blocking collectives: none -> 14 us  [per_device(): all_stats = lax.all_to_all(stats, BOTH, 0, 0, axis_index_groups=SAME_CORE)]
    all_to_all x2, waiting for transfers between devices: 23.1 us -> 9.3 us  [spread(): return lax.all_to_all(value, BOTH, 0, 0, axis_index_groups=groups)]
    all_to_all x2, starting transfers between devices: 9.76 us -> 7.06 us  [spread(): return lax.all_to_all(value, BOTH, 0, 0, axis_index_groups=groups)]
    ppermute x8, starting transfers between devices: 10.4 us -> 8.04 us  [swap(): return lax.ppermute(value, BOTH, SWAP)]
    ppermute x8, waiting for transfers between devices: 2.79 us -> 4.28 us  [swap(): return lax.ppermute(value, BOTH, SWAP)]
  transfers between devices with their start and end apart: 17 -> 17, of which waited for: 10 -> 11; matrix products, arithmetic and copies ran while one was open for 2% -> 2% of each run, Pallas kernels for 22% -> 15%
where the time goes in v6:
time: 128 us
  Pallas kernels  40.1 us (31%)
  blocking collectives  34.8 us (27%)
  waiting for transfers between devices  25.1 us (20%)
  starting transfers between devices  20.4 us (16%)
  local copies, waits for them, and re-layouts  3.48 us (3%)
  other arithmetic  2.85 us (2%)
    all_to_all x1, blocking collectives, per_device(): near = lax.all_to_all(blocks, BOTH, 0, 0, axis_index_groups=FIRST)  20.8 us
    all_to_all x1, blocking collectives, per_device(): all_stats = lax.all_to_all(stats, BOTH, 0, 0, axis_index_groups=SAME_CORE)  14 us
    pallas_call x1, Pallas kernels, logits_of(): pl.pallas_call(logits_kernel, name='logits', in_specs=[SMEM] + [HBM] * 8...  11.7 us
    ppermute x7, waiting for transfers between devices, along(): return lax.ppermute(value, BOTH, links(axes))  11.5 us
    pallas_call x1, Pallas kernels, head_gradient_of(): pl.pallas_call(head_kernel, name='head_gradient', grid=(8,), in_specs=[st...  10 us
    pallas_call x1, Pallas kernels, gradient_of(): pl.pallas_call(gradient_kernel, name='hidden_gradient', in_specs=[SMEM] *...  9.48 us
    all_to_all x2, waiting for transfers between devices, spread(): return lax.all_to_all(value, BOTH, 0, 0, axis_index_groups=groups)  9.3 us
    ppermute x8, starting transfers between devices, swap(): return lax.ppermute(value, BOTH, SWAP)  8.04 us
  transfers between devices with their start and end apart: 17, of which 11 were waited for; matrix products, arithmetic and copies ran while one was open for 2% of the time, Pallas kernels for 15%

profile of v6, /device:TPU:1, one launch (start us, length us, event | category | flops | bytes accessed | tf_op | source)
XLA Modules:
  0.0 127.5 jit_solution(4445099393830396178)
XLA Ops:
  0.6 1.5 %collective-permute-start.1 = (bf16[64,320]{1,0:T(8,128)(2,1)}, bf16[64,320]{1,0:T(8,128)(2,1)S(1)}, u32[]{:S(2)}, u32[]{:S(2)}) collective-permute-start(bf16[64,320]{1,0:T(8,128)(2,1)} %own_s_in.1), channel_id=1, source_target_pairs={{0,1},{1,0},{2,3},{3,2},{4,5},{5,4},{6,7},{7,6},{8,9},{9,8},{10,11... | collective-permute-start | bytes 122888 | tf_op jit(solution)/shard_map/ppermute | solution.py:92
  2.2 1.3 %collective-permute-done.got_t = bf16[64,256]{1,0:T(8,128)(2,1)S(1)} collective-permute-done((bf16[64,256]{1,0:T(8,128)(2,1)}, bf16[64,256]{1,0:T(8,128)(2,1)S(1)}, u32[]{:S(2)}, u32[]{:S(2)}) %collective-permute-start) | collective-permute-done | bytes 32800 | tf_op jit(solution)/shard_map/ppermute | solution.py:92
  4.1 0.7 copy-done.4
  4.7 0.9 pack.1
  5.7 20.8 %all_to_all.20.refs_0_ = bf16[8,304,128]{2,1,0:T(8,128)(2,1)S(1)} all-to-all(bf16[8,304,128]{2,1,0:T(8,128)(2,1)S(1)} %pack.1), channel_id=1, replica_groups={{0,16,2,18,64,80,66,82},{32,48,34,50,96,112,98,114},{4,20,6,22,68,84,70..., dimensions={0} | all-to-all | bytes 1245184 | tf_op jit(solution)/shard_map/all_to_all | solution.py:511
  26.7 3.6 %collective-permute-start.9 = (bf16[8,304,128]{2,1,0:T(8,128)(2,1)S(1)}, bf16[8,304,128]{2,1,0:T(8,128)(2,1)S(1)}, u32[]{:S(2)}, u32[]{:S(2)}) collective-permute-start(bf16[8,304,128]{2,1,0:T(8,128)(2,1)S(1)} %all_to_all.20.refs_0_), channel_id=1, source_target_pairs={{0,126},{1,83},{16,110},{17,67},{32,94},{33,115},{48,78},{49,99},{... | collective-permute-start | bytes 1867784 | tf_op jit(solution)/shard_map/ppermute | solution.py:104
  30.3 5.3 %collective-permute-done.5.third.refs_3_ = bf16[8,304,128]{2,1,0:T(8,128)(2,1)S(1)} collective-permute-done((bf16[8,304,128]{2,1,0:T(8,128)(2,1)S(1)}, bf16[8,304,128]{2,1,0:T(8,128)(2,1)S(1)}, u32[]{:S(2)}, u32[]{:S(2)}) %collective-permute-start.5) | collective-permute-done | bytes 622624 | tf_op jit(solution)/shard_map/ppermute | solution.py:104
  35.7 0.4 collective-permute-done.3.first.refs_1_
  36.1 1.5 %collective-permute-start.7 = (bf16[8,304,128]{2,1,0:T(8,128)(2,1)S(1)}, bf16[8,304,128]{2,1,0:T(8,128)(2,1)}, u32[]{:S(2)}, u32[]{:S(2)}) collective-permute-start(bf16[8,304,128]{2,1,0:T(8,128)(2,1)S(1)} %collective-permute-done.3.first.refs_1_), channel_id=1, source_target_pairs={{0,48},{1,17},{16,32},{17,1},{32,16},{33,49},{48,0},{49,33},{2,50}... | collective-permute-start | bytes 1867784 | tf_op jit(solution)/shard_map/ppermute | solution.py:104
  37.6 7.9 %prefetch_heads.1 = (bf16[4096,1280]{1,0:T(8,128)(2,1)S(1)}, bf16[5120,1280]{1,0:T(8,128)(2,1)S(1)}) custom-call(bf16[4096,640]{1,0:T(8,128)(2,1)} %own_t.1, bf16[4096,640]{1,0:T(8,128)(2,1)} %collective-permute-done.10.other_t, bf16[5120,640]{1,0:T(8,128)(2,1)} %own_s.3, bf16[5120,640]{1,0:T(8,128)(2,1)} %collective-permute-done.2.other_s, ...), custom_call_target="tpu_custom_call" | custom-call | bytes 47185920 | tf_op jit(solution)/shard_map/prefetch_heads/pallas_call | solution.py:364
  45.6 4.7 %collective-permute-done.6.refs_4_ = bf16[8,304,128]{2,1,0:T(8,128)(2,1)} collective-permute-done((bf16[8,304,128]{2,1,0:T(8,128)(2,1)S(1)}, bf16[8,304,128]{2,1,0:T(8,128)(2,1)}, u32[]{:S(2)}, u32[]{:S(2)}) %collective-permute-start.6) | collective-permute-done | bytes 622624 | tf_op jit(solution)/shard_map/ppermute | solution.py:104
  50.3 1.1 collective-permute-done.7.refs_5_
  51.4 11.7 %logits.1 = (f32[256,1280]{1,0:T(8,128)S(1)}, f32[256,1280]{1,0:T(8,128)S(1)}, f32[64,8,128]{2,1,0:T(8,128)}, bf16[256,5120]{1,0:T(8,128)(2,1)}) custom-call(s32[4]{0:T(128)S(1)} %pad_add_fusion.place_ref, bf16[8,304,128]{2,1,0:T(8,128)(2,1)} %copy-done.5, bf16[8,304,128]{2,1,0:T(8,128)(2,1)} %copy-done.2, bf16[8,304,128]{2,1,0:T(8,128)(2,1)} %copy-done.1, ...), custom_call_target="tpu_custom_call" | custom-call | flops 6039797760 | bytes 8388608 | tf_op jit(solution)/shard_map/logits/pallas_call | solution.py:380
  63.2 14.0 %all_to_all.21.stats_ref = f32[64,8,128]{2,1,0:T(8,128)S(1)} all-to-all(f32[64,8,128]{2,1,0:T(8,128)} %get-tuple-element.31), channel_id=1, replica_groups={{0,2,4,6,8,10,12,14,16,18,20,22,24,26,28,30,32,34,36,38,40,42,44,46,48,..., dimensions={0} | all-to-all | bytes 524288 | tf_op jit(solution)/shard_map/all_to_all | solution.py:525
  77.1 9.5 %hidden_gradient.1 = (bf16[8,8,32,640]{3,2,1,0:T(8,128)(2,1)}, bf16[256,1280]{1,0:T(8,128)(2,1)}, f32[8,256]{1,0:T(8,128)}) custom-call(s32[4]{0:T(128)} %copy-done.3, s32[8]{0:T(128)} %lengths_ref.1, f32[64,8,128]{2,1,0:T(8,128)S(1)} %all_to_all.21.stats_ref, f32[256,1280]{1,0:T(8,128)S(1)} %get-tuple-element.32.teacher, ...), custom_call_target="tpu_custom_call" | custom-call | flops 3355443200 | bytes 13107200 | tf_op jit(solution)/shard_map/hidden_gradient/pallas_call | solution.py:409
  86.6 2.8 %collective-permute-start.11 = (bf16[256,5120]{1,0:T(8,128)(2,1)}, bf16[256,5120]{1,0:T(8,128)(2,1)}, u32[]{:S(2)}, u32[]{:S(2)}) collective-permute-start(bf16[256,5120]{1,0:T(8,128)(2,1)} %get-tuple-element.37.own_ref), channel_id=1, source_target_pairs={{0,1},{1,0},{2,3},{3,2},{4,5},{5,4},{6,7},{7,6},{8,9},{9,8},{10,11... | collective-permute-start | bytes 7864328 | tf_op jit(solution)/shard_map/ppermute | solution.py:92
  89.4 3.6 %all-to-all-start.2 = ((bf16[8,8,32,640]{3,2,1,0:T(8,128)(2,1)}), bf16[8,8,32,640]{3,2,1,0:T(8,128)(2,1)S(1)}, u32[]{:S(2)}, u32[]{:S(2)}) async-start(bf16[8,8,32,640]{3,2,1,0:T(8,128)(2,1)} %get-tuple-element.34), calls=%async_computation.2 | async-start | bytes 5242880 | tf_op jit(solution)/shard_map/all_to_all | solution.py:535
  93.1 0.8 slice.15
  94.0 1.7 %collective-permute-done.12.got_ref = bf16[256,640]{1,0:T(8,128)(2,1)S(1)} collective-permute-done((bf16[256,640]{1,0:T(8,128)(2,1)}, bf16[256,640]{1,0:T(8,128)(2,1)S(1)}, u32[]{:S(2)}, u32[]{:S(2)}) %collective-permute-start.12) | collective-permute-done | bytes 327712 | tf_op jit(solution)/shard_map/ppermute | solution.py:92
  95.7 0.8 copy-done.8
  96.4 10.0 %head_gradient.1 = bf16[5120,640]{1,0:T(8,128)(2,1)} custom-call(bf16[256,5120]{1,0:T(8,128)(2,1)} %get-tuple-element.37.own_ref, bf16[256,5120]{1,0:T(8,128)(2,1)} %collective-permute-done.11.other_ref, bf16[256,1280]{1,0:T(8,128)(2,1)} %get-tuple-element.38.mine_ref, bf16[256,640]{1,0:T(8,128)(2,1)} %copy-done.8), custom_call_target="tpu_custom_call" | custom-call | flops 3355443200 | bytes 16777216 | tf_op jit(solution)/shard_map/head_gradient/pallas_call | solution.py:437
  106.5 5.1 %all-to-all-done.2 = bf16[8,8,32,640]{3,2,1,0:T(8,128)(2,1)S(1)} async-done(((bf16[8,8,32,640]{3,2,1,0:T(8,128)(2,1)}), bf16[8,8,32,640]{3,2,1,0:T(8,128)(2,1)S(1)}, u32[]{:S(2)}, u32[]{:S(2)}) %all-to-all-start.2) | async-done | bytes 2621472 | tf_op jit(solution)/shard_map/all_to_all | solution.py:535
  111.5 1.2 reduce_sum.24
  112.7 3.4 %all-to-all-start.3 = ((bf16[8,32,640]{2,1,0:T(8,128)(2,1)}), bf16[8,32,640]{2,1,0:T(8,128)(2,1)S(1)}, u32[]{:S(2)}, u32[]{:S(2)}) async-start(bf16[8,32,640]{2,1,0:T(8,128)(2,1)} %reduce_sum.24), calls=%async_computation.3 | async-start | bytes 655360 | tf_op jit(solution)/shard_map/all_to_all | solution.py:535
  116.1 0.8 constant_dynamic-slice_fusion
  116.9 2.7 %collective-permute-start.14 = (f32[2,4]{1,0:T(2,128)S(1)}, f32[2,4]{1,0:T(2,128)S(1)}, u32[]{:S(2)}, u32[]{:S(2)}) collective-permute-start(f32[2,4]{1,0:T(2,128)S(1)} %constant_dynamic-slice_fusion), channel_id=1, source_target_pairs={{0,1},{1,0},{2,3},{3,2},{4,5},{5,4},{6,7},{7,6},{8,9},{9,8},{10,11... | collective-permute-start | bytes 104 | tf_op jit(solution)/shard_map/ppermute | solution.py:92
  119.6 0.8 collective-permute-done.14
  120.5 0.8 dynamic-slice_select_fusion
  121.2 4.2 %all-to-all-done.3 = bf16[8,32,640]{2,1,0:T(8,128)(2,1)S(1)} async-done(((bf16[8,32,640]{2,1,0:T(8,128)(2,1)}), bf16[8,32,640]{2,1,0:T(8,128)(2,1)S(1)}, u32[]{:S(2)}, u32[]{:S(2)}) %all-to-all-start.3) | async-done | bytes 327712 | tf_op jit(solution)/shard_map/all_to_all | solution.py:535
  125.9 0.5 slice_bitcast_fusion
  126.4 0.4 collective-permute-done.13
  126.9 0.6 pad_maximum_fusion
  (37 shorter events, 1.7 us)
Async XLA Ops:
  0.6 2.9 %collective-permute-start.1 = (bf16[64,320]{1,0:T(8,128)(2,1)}, bf16[64,320]{1,0:T(8,128)(2,1)S(1)}, u32[]{:S(2)}, u32[]{:S(2)}) collective-permute-start(bf16[64,320]{1,0:T(8,128)(2,1)} %own_s_in.1), channel_id=1, source_target_pairs={{0,1},{1,0},{2,3},{3,2},{4,5},{5,4},{6,7},{7,6},{8,9},{9,8},{10,11... | collective-permute-start | bytes 122888 | tf_op jit(solution)/shard_map/ppermute | solution.py:92
  2.1 1.4 %collective-permute-start = (bf16[64,256]{1,0:T(8,128)(2,1)}, bf16[64,256]{1,0:T(8,128)(2,1)S(1)}, u32[]{:S(2)}, u32[]{:S(2)}) collective-permute-start(bf16[64,256]{1,0:T(8,128)(2,1)} %own_t_in.1), channel_id=1, source_target_pairs={{0,1},{1,0},{2,3},{3,2},{4,5},{5,4},{6,7},{7,6},{8,9},{9,8},{10,11... | collective-permute-start | bytes 98312 | tf_op jit(solution)/shard_map/ppermute | solution.py:92
  3.6 22.9 %collective-permute-start.2 = (bf16[5120,640]{1,0:T(8,128)(2,1)}, bf16[5120,640]{1,0:T(8,128)(2,1)}, u32[]{:S(2)}, u32[]{:S(2)}) collective-permute-start(bf16[5120,640]{1,0:T(8,128)(2,1)} %own_s.3), channel_id=1, source_target_pairs={{0,1},{1,0},{2,3},{3,2},{4,5},{5,4},{6,7},{7,6},{8,9},{9,8},{10,11... | collective-permute-start | bytes 19660808 | tf_op jit(solution)/shard_map/ppermute | solution.py:92
  3.7 33.9 %collective-permute-start.10 = (bf16[4096,640]{1,0:T(8,128)(2,1)}, bf16[4096,640]{1,0:T(8,128)(2,1)}, u32[]{:S(2)}, u32[]{:S(2)}) collective-permute-start(bf16[4096,640]{1,0:T(8,128)(2,1)} %own_t.1), channel_id=1, source_target_pairs={{0,1},{1,0},{2,3},{3,2},{4,5},{5,4},{6,7},{7,6},{8,9},{9,8},{10,11... | collective-permute-start | bytes 15728648 | tf_op jit(solution)/shard_map/ppermute | solution.py:92
  4.1 0.7 copy-start.4
  26.5 19.1 %copy-start.5 = (bf16[8,304,128]{2,1,0:T(8,128)(2,1)}, bf16[8,304,128]{2,1,0:T(8,128)(2,1)S(1)}, u32[]{:S(2)}) copy-start(bf16[8,304,128]{2,1,0:T(8,128)(2,1)S(1)} %all_to_all.20.refs_0_) | copy-start | bytes 1867780
  26.5 9.1 %collective-permute-start.5 = (bf16[8,304,128]{2,1,0:T(8,128)(2,1)S(1)}, bf16[8,304,128]{2,1,0:T(8,128)(2,1)S(1)}, u32[]{:S(2)}, u32[]{:S(2)}) collective-permute-start(bf16[8,304,128]{2,1,0:T(8,128)(2,1)S(1)} %all_to_all.20.refs_0_), channel_id=1, source_target_pairs={{0,48},{1,17},{16,32},{17,1},{32,16},{33,49},{48,0},{49,33},{2,50}... | collective-permute-start | bytes 1867784 | tf_op jit(solution)/shard_map/ppermute | solution.py:104
  26.5 9.2 %collective-permute-start.4 = (bf16[8,304,128]{2,1,0:T(8,128)(2,1)S(1)}, bf16[8,304,128]{2,1,0:T(8,128)(2,1)S(1)}, u32[]{:S(2)}, u32[]{:S(2)}) collective-permute-start(bf16[8,304,128]{2,1,0:T(8,128)(2,1)S(1)} %all_to_all.20.refs_0_), channel_id=1, source_target_pairs={{0,6},{1,3},{16,22},{17,19},{32,38},{33,35},{48,54},{49,51},{2,4},... | collective-permute-start | bytes 1867784 | tf_op jit(solution)/shard_map/ppermute | solution.py:104
  26.6 9.5 %collective-permute-start.3 = (bf16[8,304,128]{2,1,0:T(8,128)(2,1)S(1)}, bf16[8,304,128]{2,1,0:T(8,128)(2,1)S(1)}, u32[]{:S(2)}, u32[]{:S(2)}) collective-permute-start(bf16[8,304,128]{2,1,0:T(8,128)(2,1)S(1)} %all_to_all.20.refs_0_), channel_id=1, source_target_pairs={{0,72},{1,65},{16,88},{17,81},{32,104},{33,97},{48,120},{49,113},{... | collective-permute-start | bytes 1867784 | tf_op jit(solution)/shard_map/ppermute | solution.py:104
  26.7 18.9 %collective-permute-start.9 = (bf16[8,304,128]{2,1,0:T(8,128)(2,1)S(1)}, bf16[8,304,128]{2,1,0:T(8,128)(2,1)S(1)}, u32[]{:S(2)}, u32[]{:S(2)}) collective-permute-start(bf16[8,304,128]{2,1,0:T(8,128)(2,1)S(1)} %all_to_all.20.refs_0_), channel_id=1, source_target_pairs={{0,126},{1,83},{16,110},{17,67},{32,94},{33,115},{48,78},{49,99},{... | collective-permute-start | bytes 1867784 | tf_op jit(solution)/shard_map/ppermute | solution.py:104
  35.6 10.0 %copy-start = (bf16[8,304,128]{2,1,0:T(8,128)(2,1)}, bf16[8,304,128]{2,1,0:T(8,128)(2,1)S(1)}, u32[]{:S(2)}) copy-start(bf16[8,304,128]{2,1,0:T(8,128)(2,1)S(1)} %collective-permute-done.5.third.refs_3_) | copy-start | bytes 1867780
  35.6 14.7 %collective-permute-start.6 = (bf16[8,304,128]{2,1,0:T(8,128)(2,1)S(1)}, bf16[8,304,128]{2,1,0:T(8,128)(2,1)}, u32[]{:S(2)}, u32[]{:S(2)}) collective-permute-start(bf16[8,304,128]{2,1,0:T(8,128)(2,1)S(1)} %collective-permute-done.5.third.refs_3_), channel_id=1, source_target_pairs={{0,6},{1,3},{16,22},{17,19},{32,38},{33,35},{48,54},{49,51},{2,4},... | collective-permute-start | bytes 1867784 | tf_op jit(solution)/shard_map/ppermute | solution.py:104
  35.7 9.9 %copy-start.1 = (bf16[8,304,128]{2,1,0:T(8,128)(2,1)}, bf16[8,304,128]{2,1,0:T(8,128)(2,1)S(1)}, u32[]{:S(2)}) copy-start(bf16[8,304,128]{2,1,0:T(8,128)(2,1)S(1)} %collective-permute-done.4.second.refs_2_) | copy-start | bytes 1867780
  35.7 14.6 %collective-permute-start.8 = (bf16[8,304,128]{2,1,0:T(8,128)(2,1)S(1)}, bf16[8,304,128]{2,1,0:T(8,128)(2,1)}, u32[]{:S(2)}, u32[]{:S(2)}) collective-permute-start(bf16[8,304,128]{2,1,0:T(8,128)(2,1)S(1)} %collective-permute-done.4.second.refs_2_), channel_id=1, source_target_pairs={{0,72},{1,65},{16,88},{17,81},{32,104},{33,97},{48,120},{49,113},{... | collective-permute-start | bytes 1867784 | tf_op jit(solution)/shard_map/ppermute | solution.py:104
  36.1 9.5 %copy-start.2 = (bf16[8,304,128]{2,1,0:T(8,128)(2,1)}, bf16[8,304,128]{2,1,0:T(8,128)(2,1)S(1)}, u32[]{:S(2)}) copy-start(bf16[8,304,128]{2,1,0:T(8,128)(2,1)S(1)} %collective-permute-done.3.first.refs_1_) | copy-start | bytes 1867780
  36.1 15.4 %collective-permute-start.7 = (bf16[8,304,128]{2,1,0:T(8,128)(2,1)S(1)}, bf16[8,304,128]{2,1,0:T(8,128)(2,1)}, u32[]{:S(2)}, u32[]{:S(2)}) collective-permute-start(bf16[8,304,128]{2,1,0:T(8,128)(2,1)S(1)} %collective-permute-done.3.first.refs_1_), channel_id=1, source_target_pairs={{0,48},{1,17},{16,32},{17,1},{32,16},{33,49},{48,0},{49,33},{2,50}... | collective-permute-start | bytes 1867784 | tf_op jit(solution)/shard_map/ppermute | solution.py:104
  37.6 13.8 %copy-start.3 = (s32[4]{0:T(128)}, s32[4]{0:T(128)S(1)}, u32[]{:S(2)}) copy-start(s32[4]{0:T(128)S(1)} %pad_add_fusion.place_ref) | copy-start | bytes 52
  45.6 5.8 %copy-start.7 = (bf16[8,304,128]{2,1,0:T(8,128)(2,1)}, bf16[8,304,128]{2,1,0:T(8,128)(2,1)S(1)}, u32[]{:S(2)}) copy-start(bf16[8,304,128]{2,1,0:T(8,128)(2,1)S(1)} %collective-permute-done.9.refs_7_) | copy-start | bytes 1867780
  86.6 6.4 %copy-start.6 = (bf16[256,1280]{1,0:T(8,128)(2,1)S(1)}, bf16[256,1280]{1,0:T(8,128)(2,1)}, u32[]{:S(2)}) copy-start(bf16[256,1280]{1,0:T(8,128)(2,1)} %get-tuple-element.38.mine_ref) | copy-start | bytes 1966084
  86.6 9.0 %collective-permute-start.11 = (bf16[256,5120]{1,0:T(8,128)(2,1)}, bf16[256,5120]{1,0:T(8,128)(2,1)}, u32[]{:S(2)}, u32[]{:S(2)}) collective-permute-start(bf16[256,5120]{1,0:T(8,128)(2,1)} %get-tuple-element.37.own_ref), channel_id=1, source_target_pairs={{0,1},{1,0},{2,3},{3,2},{4,5},{5,4},{6,7},{7,6},{8,9},{9,8},{10,11... | collective-permute-start | bytes 7864328 | tf_op jit(solution)/shard_map/ppermute | solution.py:92
  89.4 22.1 %all-to-all-start.2 = ((bf16[8,8,32,640]{3,2,1,0:T(8,128)(2,1)}), bf16[8,8,32,640]{3,2,1,0:T(8,128)(2,1)S(1)}, u32[]{:S(2)}, u32[]{:S(2)}) async-start(bf16[8,8,32,640]{3,2,1,0:T(8,128)(2,1)} %get-tuple-element.34), calls=%async_computation.2 | async-start | bytes 5242880 | tf_op jit(solution)/shard_map/all_to_all | solution.py:535
  93.8 1.8 %collective-permute-start.12 = (bf16[256,640]{1,0:T(8,128)(2,1)}, bf16[256,640]{1,0:T(8,128)(2,1)S(1)}, u32[]{:S(2)}, u32[]{:S(2)}) collective-permute-start(bf16[256,640]{1,0:T(8,128)(2,1)} %slice.15), channel_id=1, source_target_pairs={{0,1},{1,0},{2,3},{3,2},{4,5},{5,4},{6,7},{7,6},{8,9},{9,8},{10,11... | collective-permute-start | bytes 983048 | tf_op jit(solution)/shard_map/ppermute | solution.py:92
  95.7 0.8 copy-start.8
  112.7 12.7 %all-to-all-start.3 = ((bf16[8,32,640]{2,1,0:T(8,128)(2,1)}), bf16[8,32,640]{2,1,0:T(8,128)(2,1)S(1)}, u32[]{:S(2)}, u32[]{:S(2)}) async-start(bf16[8,32,640]{2,1,0:T(8,128)(2,1)} %reduce_sum.24), calls=%async_computation.3 | async-start | bytes 655360 | tf_op jit(solution)/shard_map/all_to_all | solution.py:535
  116.9 3.5 %collective-permute-start.14 = (f32[2,4]{1,0:T(2,128)S(1)}, f32[2,4]{1,0:T(2,128)S(1)}, u32[]{:S(2)}, u32[]{:S(2)}) collective-permute-start(f32[2,4]{1,0:T(2,128)S(1)} %constant_dynamic-slice_fusion), channel_id=1, source_target_pairs={{0,1},{1,0},{2,3},{3,2},{4,5},{5,4},{6,7},{7,6},{8,9},{9,8},{10,11... | collective-permute-start | bytes 104 | tf_op jit(solution)/shard_map/ppermute | solution.py:92
  125.6 1.2 collective-permute-start.13
